TPU v7x, 256 devices: a whole 4x4x8 slice. The times are simulated.
256 devices in a mesh: group: 8 (over x, core), shard: 32 (over y, z).
Axes of the slice: x: 4, y: 4, z: 8, core: 2. Of those that a mesh axis runs over, the one named last changes fastest.
Arguments:
- caption_embed: bfloat16 [1024, 256], P(('group', 'shard')), may hold values from -12 to 12
- gallery_embed: bfloat16 [131072, 256], P('shard'), may hold values from -6 to 6
- probe_blocks: int32 [8, 128], P('group'), may hold values from 0 to 511, all different within a row
- query_states: bfloat16 [1024, 32, 768], P(('group', 'shard')), may hold values from -136 to 136
- patches: bfloat16 [32, 257, 1408], P('shard'), may hold values from -6 to 6
- candidates: int32 [1024, 16, 1], P(('group', 'shard')), may hold values from 0 to 31; in each aligned block of 64 rows (0 to 63, 64 to 127, ..., all dimensions but the last counted through in order) at most 3 rows name the same one
- query_weight: bfloat16 [768, 768], replicated, may hold values from -0.21875 to 0.21875
- keyvalue_weight: bfloat16 [1408, 1536], P(None, 'group'), may hold values from -0.15625 to 0.15625
- output_weight: bfloat16 [768, 768], replicated, may hold values from -0.21875 to 0.21875
- norm_gain: float32 [768], replicated, may hold values from 0.5 to 1.5
- norm_bias: float32 [768], replicated, may hold values from -3 to 3
Outputs:
- layer_out: bfloat16 [1024, 16, 32, 768], P(('group', 'shard'))
- normalizer: float32 [1024], P(('group', 'shard'))
Inputs may be any that keep to these rules, and one draw needn't show every extreme that they name: `candidates`: within the 64 candidate entries of the captions of one device, no image id occurs more than 3 times; a caption may name an image twice. `probe_blocks`: the 128 ids of one group are distinct.
All inputs are finite; a program needn't handle non-finite values.
Results may differ from a plain program's by a relative error of at most 0.0025.
The roundings to bfloat16 on the way count: a program that leaves them out, or rounds other values in their place, can miss the bound.
Values may be sent and summed in bfloat16 or wider, within the bound.
No kernel may reach another device: no remote copies, remote signals or barrier semaphores. Data moves between devices by JAX's collectives and lax.ppermute only.
A program may use at most 128 MiB of HBM per device.

v0:
```python
import math

import jax
import jax.numpy as jnp
from jax import lax
from jax.sharding import PartitionSpec as P

HEADS = 12
BLK = 256


def combined_all(value, axis, combine):
    everything = jax.tree.map(lambda part: lax.all_gather(part, axis), value)
    initial = jax.tree.map(lambda part: part[0], everything)

    def step(k, so_far):
        return combine(so_far, jax.tree.map(lambda part: part[k], everything))

    return lax.fori_loop(1, lax.axis_size(axis), step, initial)


def layer_norm(hidden, gain_row, bias_row):
    average = jnp.mean(hidden, axis=-1, keepdims=True)
    centered = hidden - average
    variance = jnp.mean(centered * centered, axis=-1, keepdims=True)
    return centered * lax.rsqrt(variance + 1e-06) * gain_row + bias_row


def combine_partial(earlier_part, later_part):
    highest = jnp.maximum(earlier_part[0], later_part[0])
    summed = earlier_part[1] * jnp.exp(earlier_part[0] - highest) + later_part[1] * jnp.exp(
        later_part[0] - highest
    )
    return (highest, summed)


def bucket_select(image_ids, slot_count, bucket_count):
    pair_count = image_ids.shape[0]
    same_id = image_ids[:, None] == image_ids[None, :]
    indices = jnp.arange(pair_count, dtype=jnp.int32)
    earlier = indices[None, :] < indices[:, None]
    slot_rank = jnp.sum(jnp.logical_and(same_id, earlier), axis=1)
    position = image_ids * slot_count + slot_rank
    return position[None, :] == jnp.arange(bucket_count, dtype=jnp.int32)[:, None]


def attend_slots(received, keyvalue, head_count):
    sources, images, item_count, row_width = received.shape
    model_width = keyvalue.shape[-1] // 2
    tokens = row_width // model_width
    head_size = model_width // head_count
    per_block = math.gcd(sources, max(1, 256 // (item_count * tokens)))
    blocked = received.reshape(
        sources // per_block, per_block, images, item_count, tokens, head_count, head_size
    )
    key_rows = keyvalue[:, :, :model_width].reshape(images, -1, head_count, head_size)
    value_rows = keyvalue[:, :, model_width:].reshape(images, -1, head_count, head_size)
    inverse_root = 1.0 / math.sqrt(head_size)

    def one_block(query_block):
        scores = (
            jnp.einsum(
                "sjiqhd,jphd->sjihqp", query_block, key_rows, preferred_element_type=jnp.float32
            )
            * inverse_root
        )
        softmax_rows = jax.nn.softmax(scores, axis=-1).astype(jnp.bfloat16)
        context = jnp.einsum(
            "sjihqp,jphd->sjiqhd", softmax_rows, value_rows, preferred_element_type=jnp.float32
        )
        return context.astype(jnp.bfloat16).reshape(
            query_block.shape[0], images, item_count, row_width
        )

    return lax.map(one_block, blocked).reshape(sources, images, item_count, row_width)


def on_device(
    caption_embed,
    gallery_embed,
    probe_blocks,
    query_states,
    patches,
    candidates,
    query_weight,
    keyvalue_weight,
    output_weight,
    norm_gain,
    norm_bias,
):
    shards = lax.axis_size("shard")
    shard_index = lax.axis_index("shard")
    cap_dev, tokens, model_width = query_states.shape
    images, patch_rows, vision = patches.shape
    cand_count = candidates.shape[1]
    sim_scale = 1.0 / (0.07 * math.sqrt(caption_embed.shape[1]))
    group_rows = lax.all_gather(caption_embed, "shard", axis=0, tiled=True)
    local_blocks = gallery_embed.shape[0] // BLK
    block_ids = shard_index * local_blocks + jnp.arange(local_blocks, dtype=jnp.int32)
    probed = jnp.any(probe_blocks[0][:, None] == block_ids[None, :], axis=0)
    scores = (
        jnp.einsum("ce,re->cr", group_rows, gallery_embed, preferred_element_type=jnp.float32)
        * sim_scale
    )
    scores = scores.reshape(group_rows.shape[0], local_blocks, BLK)
    is_live = probed[None, :, None]
    masked = jnp.where(is_live, scores, -1e30)
    highest = jnp.max(masked, axis=(1, 2))
    summed = jnp.sum(jnp.where(is_live, jnp.exp(masked - highest[:, None, None]), 0.0), axis=(1, 2))
    highest, summed = combined_all((highest, summed), "shard", combine_partial)
    own_highest = lax.dynamic_slice_in_dim(highest, shard_index * cap_dev, cap_dev)
    own_summed = lax.dynamic_slice_in_dim(summed, shard_index * cap_dev, cap_dev)
    normalizer = own_highest + jnp.log(own_summed)
    queries = jnp.dot(
        query_states.reshape(-1, model_width), query_weight, preferred_element_type=jnp.float32
    ).astype(jnp.bfloat16)
    flat_patches = patches.reshape(-1, vision)
    keyvalue = jnp.dot(
        flat_patches,
        lax.all_gather(keyvalue_weight, "group", axis=1, tiled=True),
        preferred_element_type=jnp.float32,
    ).astype(jnp.bfloat16)
    keyvalue = keyvalue.reshape(images, patch_rows, 2 * model_width)
    all_images = images * shards
    slot_count = max(2, (3 * cap_dev * cand_count + 2 * all_images - 1) // (2 * all_images))
    bucket_count = all_images * slot_count
    row_width = tokens * model_width
    query_rows = queries.reshape(cap_dev, row_width)
    picked = bucket_select(candidates.reshape(-1), slot_count, bucket_count)
    per_caption = jnp.any(picked.reshape(bucket_count, cap_dev, cand_count), axis=2).astype(
        jnp.bfloat16
    )
    outgoing = jnp.dot(per_caption, query_rows, preferred_element_type=jnp.float32).astype(
        jnp.bfloat16
    )
    outgoing = outgoing.reshape(shards, images, slot_count, row_width)
    context = attend_slots(
        lax.all_to_all(outgoing, "shard", split_axis=0, concat_axis=0, tiled=True), keyvalue, HEADS
    )
    returned = lax.all_to_all(context, "shard", split_axis=0, concat_axis=0, tiled=True).reshape(
        bucket_count, row_width
    )
    gathered = jnp.einsum(
        "rp,rx->px", picked.astype(jnp.bfloat16), returned, preferred_element_type=jnp.float32
    ).astype(jnp.bfloat16)
    mixed_rows = jnp.dot(
        gathered.reshape(-1, model_width), output_weight, preferred_element_type=jnp.float32
    )
    mixed_rows = (
        mixed_rows.reshape(cap_dev, cand_count, tokens, model_width)
        + query_states.astype(jnp.float32)[:, None]
    )
    layer_out = layer_norm(mixed_rows, norm_gain, norm_bias).astype(jnp.bfloat16)
    return (layer_out, normalizer)


def solution(mesh):
    placed = (
        P(("group", "shard"), None),
        P("shard", None),
        P("group", None),
        P(("group", "shard"), None, None),
        P("shard", None, None),
        P(("group", "shard"), None, None),
        P(),
        P(None, "group"),
        P(),
        P(),
        P(),
    )
    return jax.shard_map(
        on_device,
        mesh=mesh,
        in_specs=placed,
        out_specs=(P(("group", "shard"), None, None, None), P(("group", "shard"))),
        check_vma=False,
    )
```

profile of v0, /device:TPU:2, one launch (start us, length us, event | category | flops | bytes accessed | tf_op | source)
XLA Modules:
  0.0 618.7 jit_solution(5236341984136496107)
XLA Ops:
  11.5 3.7 convolution_convert_fusion
  15.1 6.6 %reshape.123 = bf16[32,1,3,24576]{3,2,0,1:T(4,128)(2,1)} reshape(bf16[96,24576]{1,0:T(8,128)(2,1)} %convolution_convert_fusion) | data formatting | bytes 9437184 | tf_op jit(solution)/shard_map/reshape | solution.py:136
  21.7 11.7 %all-to-all-start = ((bf16[32,1,3,24576]{3,2,1,0:T(4,128)(2,1)}), bf16[32,1,3,24576]{3,2,1,0:T(4,128)(2,1)}, u32[]{:S(2)}, u32[]{:S(2)}) async-start(bf16[32,1,3,24576]{3,2,1,0:T(4,128)(2,1)} %bitcast.133), calls=%async_computation | async-start | bytes 12582912 | tf_op jit(solution)/shard_map/all_to_all | solution.py:138
  34.2 37.3 %all-gather.7.cloned.1.call-done = bf16[1408,1536]{0,1:T(8,128)(2,1)} async-done(((bf16[1408,192]{0,1:T(8,128)(2,1)}), bf16[1408,1536]{0,1:T(8,128)(2,1)}) %all-gather.7.cloned.1.call-update) | async-done | bytes 4325392 | tf_op jit(solution)/shard_map/all_gather | solution.py:120
  71.6 3.7 fusion.23
  77.4 95.8 %all-to-all-done = bf16[32,1,3,24576]{3,2,1,0:T(4,128)(2,1)} async-done(((bf16[32,1,3,24576]{3,2,1,0:T(4,128)(2,1)}), bf16[32,1,3,24576]{3,2,1,0:T(4,128)(2,1)}, u32[]{:S(2)}, u32[]{:S(2)}) %all-to-all-start) | async-done | bytes 4718624 | tf_op jit(solution)/shard_map/all_to_all | solution.py:138
  173.2 16.6 %reshape.150 = bf16[16,2,1,3,32,12,64]{6,5,4,3,1,0,2:T(8,128)(2,1)} reshape(bf16[32,1,3,24576]{3,2,1,0:T(4,128)(2,1)} %all-to-all-done) | data formatting | bytes 9437184 | tf_op jit(solution)/shard_map/reshape | solution.py:53
  189.8 10.6 %copy.40 = bf16[16,2,1,3,32,12,64]{6,4,3,1,5,2,0:T(8,128)(2,1)} copy(bf16[16,2,1,3,32,12,64]{6,5,4,3,1,0,2:T(8,128)(2,1)} %reshape.150) | data formatting | bytes 9437184 | tf_op jit(solution)/shard_map/while | solution.py:75
  200.4 113.6 %while.27 = (s32[]{:T(128)}, bf16[16,2,1,3,24576]{4,1,3,2,0:T(2,128)(2,1)}, bf16[16,2,1,3,32,12,64]{6,4,3,1,5,2,0:T(8,128)(2,1)}, bf16[1,257,12,64]{1,3,2,0:T(8,...) while((s32[]{:T(128)}, bf16[16,2,1,3,24576]{4,1,3,2,0:T(2,128)(2,1)}, ...), condition=%wide.region_5.6_spmd, body=%wide.region_2.5_spmd.sunk | while | flops 157056768 | bytes 10791493 | solution.py:75
  203.4 2.3 fusion.48
  210.5 2.3 fusion.48
  217.7 2.3 fusion.48
  224.7 2.3 fusion.48
  231.8 2.3 fusion.48
  238.9 2.3 fusion.48
  246.0 2.3 fusion.48
  253.1 2.3 fusion.48
  260.2 2.3 fusion.48
  267.3 2.3 fusion.48
  281.5 2.3 fusion.48
  295.7 2.3 fusion.48
  302.8 2.3 fusion.48
  309.9 2.3 fusion.48
  314.0 9.1 %copy.48 = bf16[16,2,1,3,24576]{4,3,1,0,2:T(4,128)(2,1)} copy(bf16[16,2,1,3,24576]{4,1,3,2,0:T(2,128)(2,1)} %get-tuple-element.162) | data formatting | bytes 9437184 | tf_op jit(solution)/shard_map/reshape | solution.py:75
  323.1 10.6 %all-to-all-start.1 = ((bf16[32,1,3,24576]{3,2,1,0:T(4,128)(2,1)}), bf16[32,1,3,24576]{3,2,1,0:T(4,128)(2,1)}, u32[]{:S(2)}, u32[]{:S(2)}) async-start(bf16[32,1,3,24576]{3,2,1,0:T(4,128)(2,1)} %bitcast.132), calls=%async_computation.1 | async-start | bytes 12582912 | tf_op jit(solution)/shard_map/all_to_all | solution.py:140
  334.1 181.5 %all-gather.2 = bf16[32,4,256]{2,1,0:T(4,128)(2,1)S(1)} all-gather(bf16[1,4,256]{2,1,0:T(4,128)(2,1)S(1)} %bitcast.141), channel_id=1, replica_groups=mesh['group'=8,'shard'=32] {'shard'}, dimensions={0}, use_global_device_ids=true | all-gather | bytes 67584 | tf_op jit(solution)/shard_map/all_gather | solution.py:97
  517.1 36.1 %all-gather.4 = f32[32,1,128]{2,1,0:T(1,128)S(1)} all-gather(f32[1,1,128]{2,1,0:T(1,128)S(1)} %bitcast.142), channel_id=3, replica_groups=mesh['group'=8,'shard'=32] {'shard'}, dimensions={0}, use_global_device_ids=true | all-gather | bytes 16896 | tf_op jit(solution)/shard_map/all_gather | solution.py:13
  553.2 38.1 %all-gather.3 = f32[32,1,128]{2,1,0:T(1,128)S(1)} all-gather(f32[1,1,128]{2,1,0:T(1,128)S(1)} %bitcast.140), channel_id=2, replica_groups=mesh['group'=8,'shard'=32] {'shard'}, dimensions={0}, use_global_device_ids=true | all-gather | bytes 16896 | tf_op jit(solution)/shard_map/all_gather | solution.py:13
  593.3 7.4 %reshape.130 = bf16[96,24576]{1,0:T(8,128)(2,1)} reshape(bf16[32,1,3,24576]{3,2,1,0:T(4,128)(2,1)} %all-to-all-done.1) | data formatting | bytes 9437184 | tf_op jit(solution)/shard_map/reshape | solution.py:140
  600.7 3.4 convolution_convert_fusion.1
  605.3 2.9 add_reduce_fusion
  609.3 2.5 add_convert_fusion
  (162 shorter events, 95.7 us)
Async XLA Ops:
  7.2 508.4 %copy-start = (bf16[4096,256]{1,0:T(8,128)(2,1)S(1)}, bf16[4096,256]{1,0:T(8,128)(2,1)}, u32[]{:S(2)}) copy-start(bf16[4096,256]{1,0:T(8,128)(2,1)} %param.16) | copy-start | bytes 6291460
  21.7 49.8 %copy-start.6 = (bf16[1,257,1408]{2,1,0:T(8,128)(2,1)S(1)}, bf16[1,257,1408]{2,1,0:T(8,128)(2,1)}, u32[]{:S(2)}) copy-start(bf16[1,257,1408]{2,1,0:T(8,128)(2,1)} %param.19) | copy-start | bytes 2171140
  21.7 151.4 %all-to-all-start = ((bf16[32,1,3,24576]{3,2,1,0:T(4,128)(2,1)}), bf16[32,1,3,24576]{3,2,1,0:T(4,128)(2,1)}, u32[]{:S(2)}, u32[]{:S(2)}) async-start(bf16[32,1,3,24576]{3,2,1,0:T(4,128)(2,1)} %bitcast.133), calls=%async_computation | async-start | bytes 12582912 | tf_op jit(solution)/shard_map/all_to_all | solution.py:138
  33.5 38.1 %all-gather.7.cloned.1.call-start = ((), (), s32[]{:S(2)}) async-start(), calls=%async_computation.2 | async-start | bytes 4866048 | tf_op jit(solution)/shard_map/all_gather | solution.py:120
  323.1 10.6 %copy-start.1 = (bf16[4,32,768]{2,1,0:T(8,128)(2,1)S(1)}, bf16[4,32,768]{2,1,0:T(8,128)(2,1)}, u32[]{:S(2)}) copy-start(bf16[4,32,768]{2,1,0:T(8,128)(2,1)} %param.18) | copy-start | bytes 589828
  323.1 10.7 %copy-start.7 = (s32[1,128]{1,0:T(1,128)S(1)}, s32[1,128]{1,0:T(1,128)}, u32[]{:S(2)}) copy-start(s32[1,128]{1,0:T(1,128)} %param.17) | copy-start | bytes 1540
  323.1 11.0 %copy-start.4 = (bf16[4,256]{1,0:T(4,128)(2,1)S(1)}, bf16[4,256]{1,0:T(4,128)(2,1)}, u32[]{:S(2)}) copy-start(bf16[4,256]{1,0:T(4,128)(2,1)} %param.15) | copy-start | bytes 6148
  323.1 270.2 %all-to-all-start.1 = ((bf16[32,1,3,24576]{3,2,1,0:T(4,128)(2,1)}), bf16[32,1,3,24576]{3,2,1,0:T(4,128)(2,1)}, u32[]{:S(2)}, u32[]{:S(2)}) async-start(bf16[32,1,3,24576]{3,2,1,0:T(4,128)(2,1)} %bitcast.132), calls=%async_computation.1 | async-start | bytes 12582912 | tf_op jit(solution)/shard_map/all_to_all | solution.py:140
  604.1 1.3 copy-start.5
  608.2 1.1 copy-start.2
  608.2 1.1 copy-start.3
Sparse Core Ops, SparseCore 0:
  36.1 35.3 all-gather.6
where the time goes:
time: 621 us; the launch traced here: 619 us
  blocking collectives  256 us (41%)
  waiting for transfers between devices  134 us (22%)
  local copies, waits for them, and re-layouts  83.3 us (13%)
  matrix products  83.2 us (13%)
  other arithmetic  25 us (4%)
  starting transfers between devices  22.4 us (4%)
  between operations  14.2 us (2%)
    all_gather x1, blocking collectives, on_device(): group_rows = lax.all_gather(caption_embed, 'shard', axis=0, tiled=True)  182 us
    all_to_all x1, waiting for transfers between devices, on_device(): lax.all_to_all(outgoing, 'shard', split_axis=0, concat_axis=0, tiled=True)  95.8 us
    all_gather x2, blocking collectives, combined_all(): everything = jax.tree.map(lambda part: lax.all_gather(part, axis), value)  74.2 us
    all_gather x1, waiting for transfers between devices, on_device(): lax.all_gather(keyvalue_weight, 'group', axis=1, tiled=True)  37.3 us
    dot_general x16, matrix products, one_block(): jnp.einsum('sjihqp,jphd->sjiqhd', softmax_rows, value_rows, preferred_ele...  36.2 us
    dot_general x16, matrix products, one_block(): jnp.einsum('sjiqhd,jphd->sjihqp', query_block, key_rows, preferred_elemen...  30.9 us
    reduce_sum x16, other arithmetic, one_block(): softmax_rows = jax.nn.softmax(scores, axis=-1).astype(jnp.bfloat16)  17.5 us
    reshape x1, local copies, waits for them, and re-layouts, attend_slots(): received.reshape(sources // per_block, per_block, images, item_count, tok...  16.6 us
  transfers between devices with their start and end apart: 3, of which 2 were waited for; matrix products, arithmetic and copies ran while one was open for 1% of the time, Pallas kernels for 0%

commit v1 on v0

v1 whole, which is shorter than its diff:
```python
import functools
import math

import jax
import jax.numpy as jnp
from jax import lax
from jax.experimental import pallas as pl
from jax.experimental.pallas import tpu as pltpu
from jax.sharding import PartitionSpec as P

HEADS = 12
BLK = 256
HD = 64
NQ = 32
SLOTS = 12
HROWS = 144
BROWS = 3 * HROWS
EXP_SCALE = math.log2(math.e) / math.sqrt(HD)
F32 = jnp.float32
BF16 = jnp.bfloat16


def project_kernel(group_ref, patches_ref, weight_ref, out_ref):
    kv = jnp.dot(patches_ref[0], weight_ref[...], preferred_element_type=F32)
    last = kv[256:257].astype(BF16)
    body = kv[:256]
    out_ref[...] = jnp.zeros_like(out_ref)
    for h in range(3):
        out_ref[h * HROWS + 128 : h * HROWS + 129, 0:HD] = last[:, h * HD : (h + 1) * HD]

    @pl.when(group_ref[0] < 4)
    def _():
        for h in range(3):
            out_ref[h * HROWS : h * HROWS + 128, 0:HD] = body[:128, h * HD : (h + 1) * HD].astype(BF16)
            out_ref[h * HROWS : h * HROWS + 128, HD:128] = body[128:, h * HD : (h + 1) * HD].astype(BF16)

    @pl.when(group_ref[0] >= 4)
    def _():
        turned = body.T
        for h in range(3):
            rows = turned[h * HD : (h + 1) * HD].astype(BF16)
            out_ref[h * HROWS : h * HROWS + HD] = rows[:, :128]
            out_ref[h * HROWS + HD : h * HROWS + 128] = rows[:, 128:]


def attend_kernel(
    core_ref,
    image_ref,
    count_ref,
    table_ref,
    q0,
    q1,
    q2,
    q3,
    *refs,
):
    own_refs, other_refs = refs[0:4], refs[4:8]
    out_refs = refs[8:12]
    query, held, result, sems = refs[12:16]
    step = pl.program_id(0)

    @pl.when(step == 0)
    def _():
        left = lax.broadcasted_iota(jnp.int32, (128, 128), 1) < HD
        for d, q_ref in enumerate((q0, q1, q2, q3)):
            rows = q_ref[0:128, :].astype(F32)
            first, second = rows[:, 0:128], rows[:, 128:256]
            turned = pltpu.roll(first, HD, 1)
            parts = (
                (jnp.where(left, first, 0.0), jnp.where(left, 0.0, turned)),
                (jnp.where(left, turned, 0.0), jnp.where(left, 0.0, first)),
                (second, pltpu.roll(second, HD, 1)),
            )
            for h in range(3):
                for side in range(2):
                    for c in range(4):
                        query[h, side, d * 4 + c] = parts[h][side][c * 32 : (c + 1) * 32].astype(BF16)

    first_core = core_ref[0] == 0
    for r in range(4):

        @pl.when(step // 8 == r)
        def _():
            mine, theirs = own_refs[r][0], other_refs[r][0]
            held[0] = jnp.where(first_core, mine, theirs)
            held[1] = jnp.where(first_core, theirs, mine)

    image = image_ref[step]
    count = count_ref[image]
    columns = []
    for h in range(3):
        block = held[1, h * HROWS + 128 : (h + 1) * HROWS, :].astype(F32)
        columns.append(block.T[0:HD, 0:1])

    def tile(t, carry):
        pairs = [table_ref[image * SLOTS + jnp.minimum(t * 4 + j, count - 1)] for j in range(4)]
        caps = [lax.shift_right_logical(p, 4) for p in pairs]
        contexts = []
        for h in range(3):
            q = jnp.concatenate(
                [query[h, 0, c] for c in caps] + [query[h, 1, c] for c in caps], axis=0
            )
            s = lax.dot_general(
                held[0, h * HROWS : (h + 1) * HROWS, :],
                q,
                (((1,), (1,)), ((), ())),
                preferred_element_type=F32,
            )
            top, bottom, cls = s[:128, :128], s[:128, 128:], s[128:129, :128]
            highest = jnp.maximum(jnp.max(jnp.maximum(top, bottom), axis=0, keepdims=True), cls)
            e_top = jnp.exp2((top - highest) * EXP_SCALE)
            e_bottom = jnp.exp2((bottom - highest) * EXP_SCALE)
            e_cls = jnp.exp2((cls - highest) * EXP_SCALE)
            inverse = 1.0 / (jnp.sum(e_top + e_bottom, axis=0, keepdims=True) + e_cls)
            a = jnp.concatenate([e_top * inverse, e_bottom * inverse], axis=1).astype(BF16)
            a_cls = (e_cls * inverse).astype(BF16).astype(F32)
            c = jnp.dot(
                held[1, h * HROWS : h * HROWS + 128, :], a, preferred_element_type=F32
            )
            contexts.append(c[:HD, :128] + c[HD:, 128:] + columns[h] * a_cls)
        pair01 = jnp.concatenate(contexts[0:2], axis=0).T.astype(BF16)
        pair2 = jnp.concatenate([contexts[2], pltpu.roll(contexts[2], 128 - 16, 1)], axis=0).T.astype(BF16)
        for j in range(4):
            result[pairs[j], 0:32, :] = pair01[j * 32 : (j + 1) * 32]
            result[pairs[j], 32:48, :] = pair2[j * 32 : j * 32 + 16]
        return carry

    lax.fori_loop(0, (count + 3) // 4, tile, 0)

    @pl.when(step == 31)
    def _():
        copies = [
            pltpu.make_async_copy(result.at[pl.ds(64 * d, 64)], out_refs[d], sems.at[d])
            for d in range(4)
        ]
        for copy in copies:
            copy.start()
        for copy in copies:
            copy.wait()


def attend(core, image_of, count, table, queries, own, other):
    def at(r):
        return lambda s, *_: (jnp.clip(s - 8 * r, 0, 7), 0, 0)

    whole = pl.BlockSpec((144, 256), lambda s, *_: (0, 0))
    return pl.pallas_call(
        attend_kernel,
        out_shape=[jax.ShapeDtypeStruct((64, 48, 128), BF16)] * 4,
        grid_spec=pltpu.PrefetchScalarGridSpec(
            num_scalar_prefetch=4,
            grid=(32,),
            in_specs=[whole] * 4
            + [pl.BlockSpec((1, BROWS, 128), at(r)) for r in range(4)] * 2,
            out_specs=[pl.BlockSpec(memory_space=pl.ANY)] * 4,
            scratch_shapes=[
                pltpu.VMEM((3, 2, 16, 32, 128), BF16),
                pltpu.VMEM((2, BROWS, 128), BF16),
                pltpu.VMEM((256, 48, 128), BF16),
                pltpu.SemaphoreType.DMA((4,)),
            ],
        ),
        compiler_params=pltpu.CompilerParams(vmem_limit_bytes=40 * 1024 * 1024),
        name="attend",
    )(core, image_of, count, table, *queries, *own, *other)


def finish_kernel(x_ref, c0, c1, c2, c3, weight_ref, states_ref, gain_ref, bias_ref, out_ref, main, low, high):
    @pl.when(pl.program_id(0) == 0)
    def _():
        low[...] = jnp.zeros_like(low)
        high[...] = jnp.zeros_like(high)
        for d in range(4):
            source = lax.rem(x_ref[0] + d, 4)
            main[d * 128 : (d + 1) * 128] = weight_ref[source, 0:128]
            low[d * 128 : d * 128 + 64] = weight_ref[source, 128:192]
            high[d * 128 + 64 : d * 128 + 128] = weight_ref[source, 128:192]

    parts = (c0, c1, c2, c3)
    count = c0.shape[0]
    first = jnp.concatenate([part[:, 0:32, :].reshape(count * 32, 128) for part in parts], axis=1)
    second = jnp.concatenate([part[:, 32:48, :].reshape(count * 16, 128) for part in parts], axis=1)
    mixed = jnp.dot(first, main[...], preferred_element_type=F32).reshape(count, 2, 16, 768)
    early = jnp.dot(second, low[...], preferred_element_type=F32).reshape(count, 16, 768)
    late = jnp.dot(second, high[...], preferred_element_type=F32).reshape(count, 16, 768)
    states = states_ref[0].astype(F32)
    gain = gain_ref[...]
    bias = bias_ref[...]
    for half, extra in ((0, early), (1, late)):
        hidden = mixed[:, half] + extra + states[half * 16 : (half + 1) * 16][None]
        average = jnp.mean(hidden, axis=-1, keepdims=True)
        centered = hidden - average
        variance = jnp.mean(centered * centered, axis=-1, keepdims=True)
        out_ref[0, :, half * 16 : (half + 1) * 16, :] = (
            centered * lax.rsqrt(variance + 1e-06) * gain + bias
        ).astype(BF16)


def finish(x, contexts, output_weight, query_states, gain, bias):
    per_step = 16
    steps = 64 // per_step
    return pl.pallas_call(
        finish_kernel,
        out_shape=jax.ShapeDtypeStruct((4, 16, NQ, 768), BF16),
        grid_spec=pltpu.PrefetchScalarGridSpec(
            num_scalar_prefetch=1,
            grid=(steps,),
            in_specs=[pl.BlockSpec((per_step, 48, 128), lambda s, *_: (s, 0, 0))] * 4
            + [
                pl.BlockSpec((4, 192, 768), lambda s, *_: (0, 0, 0)),
                pl.BlockSpec((1, NQ, 768), lambda s, *_: (s, 0, 0)),
                pl.BlockSpec((1, 768), lambda s, *_: (0, 0)),
                pl.BlockSpec((1, 768), lambda s, *_: (0, 0)),
            ],
            out_specs=pl.BlockSpec((1, 16, NQ, 768), lambda s, *_: (s, 0, 0, 0)),
            scratch_shapes=[pltpu.VMEM((512, 768), BF16)] * 3,
        ),
        compiler_params=pltpu.CompilerParams(vmem_limit_bytes=40 * 1024 * 1024),
        name="finish",
    )(x, *contexts, output_weight.reshape(4, 192, 768), query_states, gain.reshape(1, 768), bias.reshape(1, 768))


def grid_moves(dy, dz):
    return [
        (y * 8 + z, ((y + dy) % 4) * 8 + (z + dz) % 8) for y in range(4) for z in range(8)
    ]


def group_moves(dx, flip=0):
    return [(2 * x + c, 2 * ((x + dx) % 4) + (c ^ flip)) for x in range(4) for c in range(2)]


def on_device(
    caption_embed,
    gallery_embed,
    probe_blocks,
    query_states,
    patches,
    candidates,
    query_weight,
    keyvalue_weight,
    output_weight,
    norm_gain,
    norm_bias,
):
    group_index = lax.axis_index("group")
    shard_index = lax.axis_index("shard")
    x, core = group_index // 2, group_index % 2
    my_y, my_z = shard_index // 8, shard_index % 8
    cap_dev, tokens, model_width = query_states.shape

    def along_shard(value, dy, dz):
        return lax.ppermute(value, "shard", grid_moves(dy, dz))

    def along_group(value, dx, flip=0):
        return lax.ppermute(value, "group", group_moves(dx, flip))

    block = pl.pallas_call(
        project_kernel,
        out_shape=jax.ShapeDtypeStruct((BROWS, 128), BF16),
        in_specs=[
            pl.BlockSpec(memory_space=pltpu.SMEM),
            pl.BlockSpec(memory_space=pltpu.VMEM),
            pl.BlockSpec(memory_space=pltpu.VMEM),
        ],
        out_specs=pl.BlockSpec(memory_space=pltpu.VMEM),
        compiler_params=pltpu.CompilerParams(vmem_limit_bytes=40 * 1024 * 1024),
        name="project",
    )(group_index.reshape(1), patches, keyvalue_weight)
    block = lax.ppermute(
        block, "group", [(k, 2 * k) for k in range(4)] + [(4 + k, 2 * k + 1) for k in range(4)]
    )
    block = lax.dynamic_update_slice(block, caption_embed.reshape(8, 128), (136, 0))

    queries = jnp.dot(
        query_states.reshape(-1, model_width), query_weight, preferred_element_type=F32
    ).astype(BF16)
    ids = candidates.reshape(1, 64).astype(BF16)
    ids = jnp.pad(ids, ((0, 15), (0, 256 - 64)))
    by_chip = jnp.pad(queries.reshape(128, 4, 192), ((0, 0), (0, 0), (0, 64)))

    def message(d):
        rows = lax.dynamic_slice_in_dim(by_chip, (x + d) % 4, 1, axis=1)[:, 0]
        return jnp.concatenate([rows, ids], axis=0)

    received = [message(0)] + [along_group(message(4 - d), 4 - d) for d in (1, 2, 3)]
    pair_images = jnp.concatenate([part[128, :64] for part in received]).astype(jnp.int32)
    numbers = jnp.arange(256, dtype=jnp.int32)
    same = pair_images[:, None] == pair_images[None, :]
    rank = jnp.sum(jnp.logical_and(same, numbers[None, :] < numbers[:, None]), axis=1)
    position = pair_images * SLOTS + rank
    places = jnp.arange(32 * SLOTS, dtype=jnp.int32)
    table = jnp.sum(
        jnp.where(position[None, :] == places[:, None], numbers[None, :], 0), axis=1
    ).astype(jnp.int32)
    count = jnp.sum(
        pair_images[None, :] == jnp.arange(32, dtype=jnp.int32)[:, None], axis=1
    ).astype(jnp.int32)

    half = BROWS // 2
    r1, l1 = along_shard(block, 0, 1), along_shard(block, 0, -1)
    r2, l2 = along_shard(r1, 0, 1), along_shard(l1, 0, -1)
    r3, l3 = along_shard(r2, 0, 1), along_shard(l2, 0, -1)
    r4, l4 = along_shard(r3[:half], 0, 1), along_shard(l3[half:], 0, -1)
    row = jnp.stack([block, r1, l1, r2, l2, r3, l3, jnp.concatenate([r4, l4])])
    rows = [row] + [along_shard(row, d, 0) for d in (1, 2, 3)]
    others = [along_group(part, 0, 1) for part in rows]

    z_shift = jnp.array([0, -1, 1, -2, 2, -3, 3, -4], dtype=jnp.int32)
    y_shift = jnp.array([0, -1, -2, -3], dtype=jnp.int32)
    image_of = (
        ((my_y + y_shift) % 4)[:, None] * 8 + ((my_z + z_shift) % 8)[None, :]
    ).reshape(32)

    sim_scale = 1.0 / (0.07 * math.sqrt(caption_embed.shape[1]))
    group_rows = jnp.concatenate([part[:, 136:144, :] for part in rows]).reshape(128, 256)
    local_blocks = gallery_embed.shape[0] // BLK
    block_ids = shard_index * local_blocks + jnp.arange(local_blocks, dtype=jnp.int32)
    probed = jnp.any(probe_blocks[0][:, None] == block_ids[None, :], axis=0)
    scores = jnp.einsum("ce,re->cr", group_rows, gallery_embed, preferred_element_type=F32) * sim_scale
    scores = scores.reshape(128, local_blocks, BLK)
    is_live = probed[None, :, None]
    masked = jnp.where(is_live, scores, -1e30)
    highest = jnp.max(masked, axis=(1, 2))
    summed = jnp.sum(jnp.where(is_live, jnp.exp(masked - highest[:, None, None]), 0.0), axis=(1, 2))
    partial = jnp.stack([highest.reshape(32, 4), summed.reshape(32, 4)], axis=1)
    order = jnp.arange(32, dtype=jnp.int32)
    pick = image_of[None, :] == order[:, None]
    partial = jnp.sum(jnp.where(pick[:, :, None, None], partial[None], 0.0), axis=1)
    partial = lax.all_to_all(partial, "shard", split_axis=0, concat_axis=0, tiled=True)
    top = jnp.max(partial[:, 0], axis=0)
    normalizer = top + jnp.log(jnp.sum(partial[:, 1] * jnp.exp(partial[:, 0] - top[None]), axis=0))

    contexts = attend(core.reshape(1), image_of, count, table, received, rows, others)
    returned = [contexts[0]] + [along_group(contexts[4 - d], 4 - d) for d in (1, 2, 3)]
    layer_out = finish(x.reshape(1), returned, output_weight, query_states, norm_gain, norm_bias)
    return (layer_out, normalizer)


def solution(mesh):
    placed = (
        P(("group", "shard"), None),
        P("shard", None),
        P("group", None),
        P(("group", "shard"), None, None),
        P("shard", None, None),
        P(("group", "shard"), None, None),
        P(),
        P(None, "group"),
        P(),
        P(),
        P(),
    )
    return jax.shard_map(
        on_device,
        mesh=mesh,
        in_specs=placed,
        out_specs=(P(("group", "shard"), None, None, None), P(("group", "shard"))),
        check_vma=False,
    )
```

time: 621 us -> 215 us (0.35)
  the two profiles are of different devices: /device:TPU:2 before, /device:TPU:1 now
where the time goes in v1:
time: 215 us; the launch traced here: 214 us
  Pallas kernels  73.4 us (34%)
  starting transfers between devices  58.6 us (27%)
  waiting for transfers between devices  49.8 us (23%)
  local copies, waits for them, and re-layouts  19.5 us (9%)
  other arithmetic  7.1 us (3%)
  matrix products  4.58 us (2%)
    pallas_call x1, Pallas kernels, attend(): pl.pallas_call(attend_kernel, out_shape=[jax.ShapeDtypeStruct((64, 48, 12...  65.3 us
    ppermute x10, starting transfers between devices, along_group(): return lax.ppermute(value, 'group', group_moves(dx, flip))  25.5 us
    ppermute x11, waiting for transfers between devices, along_shard(): return lax.ppermute(value, 'shard', grid_moves(dy, dz))  25.4 us
    ppermute x11, starting transfers between devices, along_shard(): return lax.ppermute(value, 'shard', grid_moves(dy, dz))  20 us
    ppermute x10, waiting for transfers between devices, along_group(): return lax.ppermute(value, 'group', group_moves(dx, flip))  17 us
    unnamed x50, local copies, waits for them, and re-layouts  10.8 us
    all_to_all x1, starting transfers between devices, on_device(): lax.all_to_all(partial, 'shard', split_axis=0, concat_axis=0, tiled=True)  8.4 us
    pallas_call x1, Pallas kernels, finish(): pl.pallas_call(finish_kernel, out_shape=jax.ShapeDtypeStruct((4, 16, NQ,...  7.55 us
  transfers between devices with their start and end apart: 23, of which 11 were waited for; matrix products, arithmetic and copies ran while one was open for 10% of the time, Pallas kernels for 0%

profile of v1, /device:TPU:1, one launch (start us, length us, event | category | flops | bytes accessed | tf_op | source)
XLA Modules:
  0.0 214.1 jit_solution(15339158993914031371)
XLA Ops:
  0.7 1.5 copy.41.weight_ref
  2.2 1.1 copy-done.7
  3.9 4.6 %collective-permute-start.3 = (bf16[432,128]{1,0:T(8,128)(2,1)S(1)}, bf16[432,128]{1,0:T(8,128)(2,1)}, u32[]{:S(2)}, u32[]{:S(2)}) collective-permute-start(bf16[432,128]{1,0:T(8,128)(2,1)S(1)} %project.1), channel_id=1, source_target_pairs={{0,0},{32,64},{64,128},{96,192},{128,32},{160,96},{192,160},{224,2... | collective-permute-start | bytes 331784 | tf_op jit(solution)/shard_map/ppermute | solution.py:270
  8.6 1.6 convolution_convert_fusion
  11.7 1.8 collective-permute-start.2
  13.6 2.4 %collective-permute-start = (bf16[144,256]{1,0:T(8,128)(2,1)}, bf16[144,256]{1,0:T(8,128)(2,1)S(1)}, u32[]{:S(2)}, u32[]{:S(2)}) collective-permute-start(bf16[144,256]{1,0:T(8,128)(2,1)} %get-tuple-element.18), channel_id=1, source_target_pairs={{0,192},{32,224},{64,0},{96,32},{128,64},{160,96},{192,128},{224,1... | collective-permute-start | bytes 221192 | tf_op jit(solution)/shard_map/ppermute | solution.py:256
  19.0 1.6 collective-permute-start.4
  20.6 0.9 bitcast_dynamic-update-slice_fusion.6
  21.6 3.9 %collective-permute-start.5 = (bf16[432,128]{1,0:T(8,128)(2,1)}, bf16[432,128]{1,0:T(8,128)(2,1)S(1)}, u32[]{:S(2)}, u32[]{:S(2)}) collective-permute-start(bf16[432,128]{1,0:T(8,128)(2,1)} %constant_dynamic-update-slice_fusion), channel_id=1, source_target_pairs={{0,7},{1,0},{2,1},{3,2},{4,3},{5,4},{6,5},{7,6},{8,15},{9,8},{10,9... | collective-permute-start | bytes 331784 | tf_op jit(solution)/shard_map/ppermute | solution.py:253
  25.5 2.4 %collective-permute-done.4 = bf16[432,128]{1,0:T(8,128)(2,1)S(1)} collective-permute-done((bf16[432,128]{1,0:T(8,128)(2,1)}, bf16[432,128]{1,0:T(8,128)(2,1)S(1)}, u32[]{:S(2)}, u32[]{:S(2)}) %collective-permute-start.4) | collective-permute-done | bytes 110624 | tf_op jit(solution)/shard_map/ppermute | solution.py:253
  28.0 3.3 %collective-permute-start.7 = (bf16[432,128]{1,0:T(8,128)(2,1)S(1)}, bf16[432,128]{1,0:T(8,128)(2,1)S(1)}, u32[]{:S(2)}, u32[]{:S(2)}) collective-permute-start(bf16[432,128]{1,0:T(8,128)(2,1)S(1)} %collective-permute-done.5), channel_id=1, source_target_pairs={{0,7},{1,0},{2,1},{3,2},{4,3},{5,4},{6,5},{7,6},{8,15},{9,8},{10,9... | collective-permute-start | bytes 331784 | tf_op jit(solution)/shard_map/ppermute | solution.py:253
  31.3 1.5 collective-permute-done.6
  33.0 3.1 %collective-permute-start.9 = (bf16[432,128]{1,0:T(8,128)(2,1)S(1)}, bf16[432,128]{1,0:T(8,128)(2,1)S(1)}, u32[]{:S(2)}, u32[]{:S(2)}) collective-permute-start(bf16[432,128]{1,0:T(8,128)(2,1)S(1)} %collective-permute-done.7), channel_id=1, source_target_pairs={{0,7},{1,0},{2,1},{3,2},{4,3},{5,4},{6,5},{7,6},{8,15},{9,8},{10,9... | collective-permute-start | bytes 331784 | tf_op jit(solution)/shard_map/ppermute | solution.py:253
  36.1 1.5 collective-permute-done.8
  37.8 3.1 %collective-permute-start.11 = (bf16[216,128]{1,0:T(8,128)(2,1)S(1)}, bf16[216,128]{1,0:T(8,128)(2,1)S(1)}, u32[]{:S(2)}, u32[]{:S(2)}) collective-permute-start(bf16[216,128]{1,0:T(8,128)(2,1)S(1)} %slice.50), channel_id=1, source_target_pairs={{0,7},{1,0},{2,1},{3,2},{4,3},{5,4},{6,5},{7,6},{8,15},{9,8},{10,9... | collective-permute-start | bytes 165896 | tf_op jit(solution)/shard_map/ppermute | solution.py:253
  42.1 1.4 collective-permute-start.12
  43.5 2.6 %collective-permute-start.13 = (bf16[8,432,128]{2,1,0:T(8,128)(2,1)S(1)}, bf16[8,432,128]{2,1,0:T(8,128)(2,1)}, u32[]{:S(2)}, u32[]{:S(2)}) collective-permute-start(bf16[8,432,128]{2,1,0:T(8,128)(2,1)S(1)} %fusion.3.refs_0_), channel_id=1, source_target_pairs={{0,16},{1,17},{2,18},{3,19},{4,20},{5,21},{6,22},{7,23},{8,24},{9,... | collective-permute-start | bytes 2654216 | tf_op jit(solution)/shard_map/ppermute | solution.py:253
  46.1 1.1 collective-permute-start.14
  48.2 5.2 %collective-permute-start.15 = (bf16[8,432,128]{2,1,0:T(8,128)(2,1)S(1)}, bf16[8,432,128]{2,1,0:T(8,128)(2,1)}, u32[]{:S(2)}, u32[]{:S(2)}) collective-permute-start(bf16[8,432,128]{2,1,0:T(8,128)(2,1)S(1)} %fusion.3.refs_0_), channel_id=1, source_target_pairs={{0,32},{32,0},{64,96},{96,64},{128,160},{160,128},{192,224},{224,1... | collective-permute-start | bytes 2654216 | tf_op jit(solution)/shard_map/ppermute | solution.py:256
  53.4 7.1 %collective-permute-done.12.refs_1_ = bf16[8,432,128]{2,1,0:T(8,128)(2,1)} collective-permute-done((bf16[8,432,128]{2,1,0:T(8,128)(2,1)S(1)}, bf16[8,432,128]{2,1,0:T(8,128)(2,1)}, u32[]{:S(2)}, u32[]{:S(2)}) %collective-permute-start.12) | collective-permute-done | bytes 884768 | tf_op jit(solution)/shard_map/ppermute | solution.py:253
  60.5 8.8 %collective-permute-start.16 = (bf16[8,432,128]{2,1,0:T(8,128)(2,1)}, bf16[8,432,128]{2,1,0:T(8,128)(2,1)}, u32[]{:S(2)}, u32[]{:S(2)}) collective-permute-start(bf16[8,432,128]{2,1,0:T(8,128)(2,1)} %collective-permute-done.12.refs_1_), channel_id=1, source_target_pairs={{0,32},{32,0},{64,96},{96,64},{128,160},{160,128},{192,224},{224,1... | collective-permute-start | bytes 2654216 | tf_op jit(solution)/shard_map/ppermute | solution.py:256
  69.3 11.3 %collective-permute-done.13.refs_2_ = bf16[8,432,128]{2,1,0:T(8,128)(2,1)} collective-permute-done((bf16[8,432,128]{2,1,0:T(8,128)(2,1)S(1)}, bf16[8,432,128]{2,1,0:T(8,128)(2,1)}, u32[]{:S(2)}, u32[]{:S(2)}) %collective-permute-start.13) | collective-permute-done | bytes 884768 | tf_op jit(solution)/shard_map/ppermute | solution.py:253
  80.6 5.2 %collective-permute-start.17 = (bf16[8,432,128]{2,1,0:T(8,128)(2,1)}, bf16[8,432,128]{2,1,0:T(8,128)(2,1)}, u32[]{:S(2)}, u32[]{:S(2)}) collective-permute-start(bf16[8,432,128]{2,1,0:T(8,128)(2,1)} %collective-permute-done.13.refs_2_), channel_id=1, source_target_pairs={{0,32},{32,0},{64,96},{96,64},{128,160},{160,128},{192,224},{224,1... | collective-permute-start | bytes 2654216 | tf_op jit(solution)/shard_map/ppermute | solution.py:256
  89.5 3.0 %fusion.15 = (f32[128]{0:T(128)S(1)}, f32[128,4096]{1,0:T(8,128)}) fusion(bf16[128,256]{1,0:T(8,128)(2,1)} %reshape.198, bf16[4096,256]{1,0:T(8,128)(2,1)S(1)} %copy-done, pred[4096]{0:T(1024)(128)(4,1)S(1)} %broadcast_in_dim.76), kind=kOutput, calls=%fused_computation.60 | convolution fusion | flops 270008192 | bytes 4264448 | tf_op jit(solution)/shard_map/ce,re->cr/dot_general | solution.py:320
  93.2 2.1 select_reduce_fusion
  96.0 1.2 copy-done.3
  100.5 65.3 %attend.1 = (bf16[64,48,128]{2,1,0:T(8,128)(2,1)S(1)}, bf16[64,48,128]{2,1,0:T(8,128)(2,1)}, bf16[64,48,128]{2,1,0:T(8,128)(2,1)}, bf16[64,48,128]{2,1,0:T(8,128)(2,1)}) custom-call(s32[1]{0:T(128)} %bitcast.1.core_ref, s32[32]{0:T(128)S(1)} %add.122.image_ref, s32[32]{0:T(128)S(1)} %copy-done.14, s32[384]{0:T(512)S(1)} %select_reduce_fusion.1.table_ref, ...), custom_call_target="tpu_custom_call" | custom-call | tf_op jit(solution)/shard_map/attend/pallas_call | solution.py:147
  170.4 8.4 %all-to-all-start = ((f32[32,2,4]{2,1,0:T(2,128)}), f32[32,2,4]{2,1,0:T(2,128)S(1)}, u32[]{:S(2)}, u32[]{:S(2)}) async-start(f32[32,2,4]{2,1,0:T(2,128)} %copy.43), calls=%async_computation | async-start | bytes 65536 | tf_op jit(solution)/shard_map/all_to_all | solution.py:330
  180.2 7.4 %all-to-all-done = f32[32,2,4]{2,1,0:T(2,128)S(1)} async-done(((f32[32,2,4]{2,1,0:T(2,128)}), f32[32,2,4]{2,1,0:T(2,128)S(1)}, u32[]{:S(2)}, u32[]{:S(2)}) %all-to-all-start) | async-done | bytes 1056 | tf_op jit(solution)/shard_map/all_to_all | solution.py:330
  188.5 17.0 %collective-permute-done.21.c3 = bf16[64,48,128]{2,1,0:T(8,128)(2,1)} collective-permute-done((bf16[64,48,128]{2,1,0:T(8,128)(2,1)}, bf16[64,48,128]{2,1,0:T(8,128)(2,1)}, u32[]{:S(2)}, u32[]{:S(2)}) %collective-permute-start.21) | collective-permute-done | bytes 786464 | tf_op jit(solution)/shard_map/ppermute | solution.py:256
  205.5 1.1 copy-done.5
  206.6 7.5 %finish.1 = bf16[4,16,32,768]{3,2,1,0:T(8,128)(2,1)} custom-call(s32[1]{0:T(128)} %bitcast.x_ref, bf16[64,48,128]{2,1,0:T(8,128)(2,1)S(1)} %copy-done.5, bf16[64,48,128]{2,1,0:T(8,128)(2,1)} %collective-permute-done.19.c1, bf16[64,48,128]{2,1,0:T(8,128)(2,1)} %collective-permute-done.20.c2, bf16[64,48,128]{2,1,0:T(8,128)(2,1)} %collective-permute-done.21.c3, ...), custom_call_target="tpu_custom_call" | custom-call | tf_op jit(solution)/shard_map/finish/pallas_call | solution.py:202
  (121 shorter events, 22.9 us)
Async XLA Ops:
  0.6 88.8 %copy-start = (bf16[4096,256]{1,0:T(8,128)(2,1)S(1)}, bf16[4096,256]{1,0:T(8,128)(2,1)}, u32[]{:S(2)}) copy-start(bf16[4096,256]{1,0:T(8,128)(2,1)} %param.14) | copy-start | bytes 6291460
  3.9 12.8 %copy-start.20 = (s32[8]{0:T(128)S(1)}, s32[8]{0:T(128)}, u32[]{:S(2)}) copy-start(s32[8]{0:T(128)} %constant.116.clone) | copy-start | bytes 100
  3.9 13.6 %copy-start.19 = (s32[1,128]{1,0:T(1,128)S(1)}, s32[1,128]{1,0:T(1,128)}, u32[]{:S(2)}) copy-start(s32[1,128]{1,0:T(1,128)} %param.15) | copy-start | bytes 1540
  3.9 14.5 %collective-permute-start.3 = (bf16[432,128]{1,0:T(8,128)(2,1)S(1)}, bf16[432,128]{1,0:T(8,128)(2,1)}, u32[]{:S(2)}, u32[]{:S(2)}) collective-permute-start(bf16[432,128]{1,0:T(8,128)(2,1)S(1)} %project.1), channel_id=1, source_target_pairs={{0,0},{32,64},{64,128},{96,192},{128,32},{160,96},{192,160},{224,2... | collective-permute-start | bytes 331784 | tf_op jit(solution)/shard_map/ppermute | solution.py:270
  11.7 6.0 %collective-permute-start.2 = (bf16[144,256]{1,0:T(8,128)(2,1)S(1)}, bf16[144,256]{1,0:T(8,128)(2,1)S(1)}, u32[]{:S(2)}, u32[]{:S(2)}) collective-permute-start(bf16[144,256]{1,0:T(8,128)(2,1)S(1)} %get-tuple-element.20), channel_id=1, source_target_pairs={{0,64},{32,96},{64,128},{96,160},{128,192},{160,224},{192,0},{224,... | collective-permute-start | bytes 221192 | tf_op jit(solution)/shard_map/ppermute | solution.py:256
  13.6 33.6 %collective-permute-start.1 = (bf16[144,256]{1,0:T(8,128)(2,1)}, bf16[144,256]{1,0:T(8,128)(2,1)S(1)}, u32[]{:S(2)}, u32[]{:S(2)}) collective-permute-start(bf16[144,256]{1,0:T(8,128)(2,1)} %get-tuple-element.19), channel_id=1, source_target_pairs={{0,128},{32,160},{64,192},{96,224},{128,0},{160,32},{192,64},{224,... | collective-permute-start | bytes 221192 | tf_op jit(solution)/shard_map/ppermute | solution.py:256
  13.6 33.7 %collective-permute-start = (bf16[144,256]{1,0:T(8,128)(2,1)}, bf16[144,256]{1,0:T(8,128)(2,1)S(1)}, u32[]{:S(2)}, u32[]{:S(2)}) collective-permute-start(bf16[144,256]{1,0:T(8,128)(2,1)} %get-tuple-element.18), channel_id=1, source_target_pairs={{0,192},{32,224},{64,0},{96,32},{128,64},{160,96},{192,128},{224,1... | collective-permute-start | bytes 221192 | tf_op jit(solution)/shard_map/ppermute | solution.py:256
  19.0 9.0 %collective-permute-start.4 = (bf16[432,128]{1,0:T(8,128)(2,1)}, bf16[432,128]{1,0:T(8,128)(2,1)S(1)}, u32[]{:S(2)}, u32[]{:S(2)}) collective-permute-start(bf16[432,128]{1,0:T(8,128)(2,1)} %constant_dynamic-update-slice_fusion), channel_id=1, source_target_pairs={{0,1},{1,2},{2,3},{3,4},{4,5},{5,6},{6,7},{7,0},{8,9},{9,10},{10,1... | collective-permute-start | bytes 331784 | tf_op jit(solution)/shard_map/ppermute | solution.py:253
  21.6 6.4 %collective-permute-start.5 = (bf16[432,128]{1,0:T(8,128)(2,1)}, bf16[432,128]{1,0:T(8,128)(2,1)S(1)}, u32[]{:S(2)}, u32[]{:S(2)}) collective-permute-start(bf16[432,128]{1,0:T(8,128)(2,1)} %constant_dynamic-update-slice_fusion), channel_id=1, source_target_pairs={{0,7},{1,0},{2,1},{3,2},{4,3},{5,4},{6,5},{7,6},{8,15},{9,8},{10,9... | collective-permute-start | bytes 331784 | tf_op jit(solution)/shard_map/ppermute | solution.py:253
  27.9 4.8 %collective-permute-start.6 = (bf16[432,128]{1,0:T(8,128)(2,1)S(1)}, bf16[432,128]{1,0:T(8,128)(2,1)S(1)}, u32[]{:S(2)}, u32[]{:S(2)}) collective-permute-start(bf16[432,128]{1,0:T(8,128)(2,1)S(1)} %collective-permute-done.4), channel_id=1, source_target_pairs={{0,1},{1,2},{2,3},{3,4},{4,5},{5,6},{6,7},{7,0},{8,9},{9,10},{10,1... | collective-permute-start | bytes 331784 | tf_op jit(solution)/shard_map/ppermute | solution.py:253
  28.0 5.0 %collective-permute-start.7 = (bf16[432,128]{1,0:T(8,128)(2,1)S(1)}, bf16[432,128]{1,0:T(8,128)(2,1)S(1)}, u32[]{:S(2)}, u32[]{:S(2)}) collective-permute-start(bf16[432,128]{1,0:T(8,128)(2,1)S(1)} %collective-permute-done.5), channel_id=1, source_target_pairs={{0,7},{1,0},{2,1},{3,2},{4,3},{5,4},{6,5},{7,6},{8,15},{9,8},{10,9... | collective-permute-start | bytes 331784 | tf_op jit(solution)/shard_map/ppermute | solution.py:253
  32.8 4.8 %collective-permute-start.8 = (bf16[432,128]{1,0:T(8,128)(2,1)S(1)}, bf16[432,128]{1,0:T(8,128)(2,1)S(1)}, u32[]{:S(2)}, u32[]{:S(2)}) collective-permute-start(bf16[432,128]{1,0:T(8,128)(2,1)S(1)} %collective-permute-done.6), channel_id=1, source_target_pairs={{0,1},{1,2},{2,3},{3,4},{4,5},{5,6},{6,7},{7,0},{8,9},{9,10},{10,1... | collective-permute-start | bytes 331784 | tf_op jit(solution)/shard_map/ppermute | solution.py:253
  33.0 4.8 %collective-permute-start.9 = (bf16[432,128]{1,0:T(8,128)(2,1)S(1)}, bf16[432,128]{1,0:T(8,128)(2,1)S(1)}, u32[]{:S(2)}, u32[]{:S(2)}) collective-permute-start(bf16[432,128]{1,0:T(8,128)(2,1)S(1)} %collective-permute-done.7), channel_id=1, source_target_pairs={{0,7},{1,0},{2,1},{3,2},{4,3},{5,4},{6,5},{7,6},{8,15},{9,8},{10,9... | collective-permute-start | bytes 331784 | tf_op jit(solution)/shard_map/ppermute | solution.py:253
  37.6 4.2 %collective-permute-start.10 = (bf16[216,128]{1,0:T(8,128)(2,1)S(1)}, bf16[216,128]{1,0:T(8,128)(2,1)S(1)}, u32[]{:S(2)}, u32[]{:S(2)}) collective-permute-start(bf16[216,128]{1,0:T(8,128)(2,1)S(1)} %slice.49), channel_id=1, source_target_pairs={{0,1},{1,2},{2,3},{3,4},{4,5},{5,6},{6,7},{7,0},{8,9},{9,10},{10,1... | collective-permute-start | bytes 165896 | tf_op jit(solution)/shard_map/ppermute | solution.py:253
  37.8 4.3 %collective-permute-start.11 = (bf16[216,128]{1,0:T(8,128)(2,1)S(1)}, bf16[216,128]{1,0:T(8,128)(2,1)S(1)}, u32[]{:S(2)}, u32[]{:S(2)}) collective-permute-start(bf16[216,128]{1,0:T(8,128)(2,1)S(1)} %slice.50), channel_id=1, source_target_pairs={{0,7},{1,0},{2,1},{3,2},{4,3},{5,4},{6,5},{7,6},{8,15},{9,8},{10,9... | collective-permute-start | bytes 165896 | tf_op jit(solution)/shard_map/ppermute | solution.py:253
  42.1 50.3 %copy-start.2 = (bf16[8,432,128]{2,1,0:T(8,128)(2,1)}, bf16[8,432,128]{2,1,0:T(8,128)(2,1)S(1)}, u32[]{:S(2)}) copy-start(bf16[8,432,128]{2,1,0:T(8,128)(2,1)S(1)} %fusion.3.refs_0_) | copy-start | bytes 2654212
  42.1 18.3 %collective-permute-start.12 = (bf16[8,432,128]{2,1,0:T(8,128)(2,1)S(1)}, bf16[8,432,128]{2,1,0:T(8,128)(2,1)}, u32[]{:S(2)}, u32[]{:S(2)}) collective-permute-start(bf16[8,432,128]{2,1,0:T(8,128)(2,1)S(1)} %fusion.3.refs_0_), channel_id=1, source_target_pairs={{0,8},{1,9},{2,10},{3,11},{4,12},{5,13},{6,14},{7,15},{8,16},{9,17... | collective-permute-start | bytes 2654216 | tf_op jit(solution)/shard_map/ppermute | solution.py:253
  43.5 37.0 %collective-permute-start.13 = (bf16[8,432,128]{2,1,0:T(8,128)(2,1)S(1)}, bf16[8,432,128]{2,1,0:T(8,128)(2,1)}, u32[]{:S(2)}, u32[]{:S(2)}) collective-permute-start(bf16[8,432,128]{2,1,0:T(8,128)(2,1)S(1)} %fusion.3.refs_0_), channel_id=1, source_target_pairs={{0,16},{1,17},{2,18},{3,19},{4,20},{5,21},{6,22},{7,23},{8,24},{9,... | collective-permute-start | bytes 2654216 | tf_op jit(solution)/shard_map/ppermute | solution.py:253
  46.1 39.7 %collective-permute-start.14 = (bf16[8,432,128]{2,1,0:T(8,128)(2,1)S(1)}, bf16[8,432,128]{2,1,0:T(8,128)(2,1)}, u32[]{:S(2)}, u32[]{:S(2)}) collective-permute-start(bf16[8,432,128]{2,1,0:T(8,128)(2,1)S(1)} %fusion.3.refs_0_), channel_id=1, source_target_pairs={{0,24},{1,25},{2,26},{3,27},{4,28},{5,29},{6,30},{7,31},{8,0},{9,1... | collective-permute-start | bytes 2654216 | tf_op jit(solution)/shard_map/ppermute | solution.py:253
  47.2 45.3 %copy-start.10 = (bf16[144,256]{1,0:T(8,128)(2,1)}, bf16[144,256]{1,0:T(8,128)(2,1)S(1)}, u32[]{:S(2)}) copy-start(bf16[144,256]{1,0:T(8,128)(2,1)S(1)} %collective-permute-done.1.q2) | copy-start | bytes 221188
  47.2 45.3 %copy-start.12 = (bf16[144,256]{1,0:T(8,128)(2,1)}, bf16[144,256]{1,0:T(8,128)(2,1)S(1)}, u32[]{:S(2)}) copy-start(bf16[144,256]{1,0:T(8,128)(2,1)S(1)} %collective-permute-done.q1) | copy-start | bytes 221188
  48.2 47.8 %collective-permute-start.15 = (bf16[8,432,128]{2,1,0:T(8,128)(2,1)S(1)}, bf16[8,432,128]{2,1,0:T(8,128)(2,1)}, u32[]{:S(2)}, u32[]{:S(2)}) collective-permute-start(bf16[8,432,128]{2,1,0:T(8,128)(2,1)S(1)} %fusion.3.refs_0_), channel_id=1, source_target_pairs={{0,32},{32,0},{64,96},{96,64},{128,160},{160,128},{192,224},{224,1... | collective-permute-start | bytes 2654216 | tf_op jit(solution)/shard_map/ppermute | solution.py:256
  60.5 35.5 %collective-permute-start.16 = (bf16[8,432,128]{2,1,0:T(8,128)(2,1)}, bf16[8,432,128]{2,1,0:T(8,128)(2,1)}, u32[]{:S(2)}, u32[]{:S(2)}) collective-permute-start(bf16[8,432,128]{2,1,0:T(8,128)(2,1)} %collective-permute-done.12.refs_1_), channel_id=1, source_target_pairs={{0,32},{32,0},{64,96},{96,64},{128,160},{160,128},{192,224},{224,1... | collective-permute-start | bytes 2654216 | tf_op jit(solution)/shard_map/ppermute | solution.py:256
  80.6 15.5 %collective-permute-start.17 = (bf16[8,432,128]{2,1,0:T(8,128)(2,1)}, bf16[8,432,128]{2,1,0:T(8,128)(2,1)}, u32[]{:S(2)}, u32[]{:S(2)}) collective-permute-start(bf16[8,432,128]{2,1,0:T(8,128)(2,1)} %collective-permute-done.13.refs_2_), channel_id=1, source_target_pairs={{0,32},{32,0},{64,96},{96,64},{128,160},{160,128},{192,224},{224,1... | collective-permute-start | bytes 2654216 | tf_op jit(solution)/shard_map/ppermute | solution.py:256
  85.8 10.2 %collective-permute-start.18 = (bf16[8,432,128]{2,1,0:T(8,128)(2,1)}, bf16[8,432,128]{2,1,0:T(8,128)(2,1)}, u32[]{:S(2)}, u32[]{:S(2)}) collective-permute-start(bf16[8,432,128]{2,1,0:T(8,128)(2,1)} %collective-permute-done.14.refs_3_), channel_id=1, source_target_pairs={{0,32},{32,0},{64,96},{96,64},{128,160},{160,128},{192,224},{224,1... | collective-permute-start | bytes 2654216 | tf_op jit(solution)/shard_map/ppermute | solution.py:256
  100.5 68.2 %copy-start.15 = (f32[32,1,4]{2,0,1:T(8,128)S(1)}, f32[32,1,4]{2,0,1:T(8,128)}, u32[]{:S(2)}) copy-start(f32[32,1,4]{2,0,1:T(8,128)} %stack_reshape.6) | copy-start | bytes 1540
  100.5 68.2 %copy-start.16 = (f32[32,1,4]{2,0,1:T(8,128)S(1)}, f32[32,1,4]{2,0,1:T(8,128)}, u32[]{:S(2)}) copy-start(f32[32,1,4]{2,0,1:T(8,128)} %stack_reshape.7) | copy-start | bytes 1540
  100.5 104.9 %copy-start.1 = (bf16[768,768]{1,0:T(8,128)(2,1)S(1)}, bf16[768,768]{1,0:T(8,128)(2,1)}, u32[]{:S(2)}) copy-start(bf16[768,768]{1,0:T(8,128)(2,1)} %param.21) | copy-start | bytes 3538948
  166.8 21.7 %collective-permute-start.19 = (bf16[64,48,128]{2,1,0:T(8,128)(2,1)}, bf16[64,48,128]{2,1,0:T(8,128)(2,1)}, u32[]{:S(2)}, u32[]{:S(2)}) collective-permute-start(bf16[64,48,128]{2,1,0:T(8,128)(2,1)} %get-tuple-element.7), channel_id=1, source_target_pairs={{0,192},{32,224},{64,0},{96,32},{128,64},{160,96},{192,128},{224,1... | collective-permute-start | bytes 2359304 | tf_op jit(solution)/shard_map/ppermute | solution.py:256
  167.3 21.2 %collective-permute-start.20 = (bf16[64,48,128]{2,1,0:T(8,128)(2,1)}, bf16[64,48,128]{2,1,0:T(8,128)(2,1)}, u32[]{:S(2)}, u32[]{:S(2)}) collective-permute-start(bf16[64,48,128]{2,1,0:T(8,128)(2,1)} %get-tuple-element.8), channel_id=1, source_target_pairs={{0,128},{32,160},{64,192},{96,224},{128,0},{160,32},{192,64},{224,... | collective-permute-start | bytes 2359304 | tf_op jit(solution)/shard_map/ppermute | solution.py:256
  167.9 37.6 %collective-permute-start.21 = (bf16[64,48,128]{2,1,0:T(8,128)(2,1)}, bf16[64,48,128]{2,1,0:T(8,128)(2,1)}, u32[]{:S(2)}, u32[]{:S(2)}) collective-permute-start(bf16[64,48,128]{2,1,0:T(8,128)(2,1)} %get-tuple-element.9), channel_id=1, source_target_pairs={{0,64},{32,96},{64,128},{96,160},{128,192},{160,224},{192,0},{224,... | collective-permute-start | bytes 2359304 | tf_op jit(solution)/shard_map/ppermute | solution.py:256
  170.4 17.2 %all-to-all-start = ((f32[32,2,4]{2,1,0:T(2,128)}), f32[32,2,4]{2,1,0:T(2,128)S(1)}, u32[]{:S(2)}, u32[]{:S(2)}) async-start(f32[32,2,4]{2,1,0:T(2,128)} %copy.43), calls=%async_computation | async-start | bytes 65536 | tf_op jit(solution)/shard_map/all_to_all | solution.py:330
  (12 other events, 36.7 us)

commit v2 on v1

v2 whole, which is shorter than its diff:
```python
import functools
import math

import jax
import jax.numpy as jnp
from jax import lax
from jax.experimental import pallas as pl
from jax.experimental.pallas import tpu as pltpu
from jax.sharding import PartitionSpec as P

HEADS = 12
BLK = 256
HD = 64
NQ = 32
SLOTS = 12
TAIL = 3 * 128
BROWS = TAIL + 16
EXP_SCALE = math.log2(math.e) / math.sqrt(HD)
PARTS = ((0, 64), (64, 64), (128, 64), (192, 64))
F32 = jnp.float32
BF16 = jnp.bfloat16


def in_hbm(value):
    return pltpu.with_memory_space_constraint(value, pltpu.HBM)


def fetched(sources, targets, sems):
    copies = [
        pltpu.make_async_copy(source, target, sems.at[k])
        for k, (source, target) in enumerate(zip(sources, targets))
    ]
    for copy in copies:
        copy.start()
    for copy in copies:
        copy.wait()


def open_kernel(group_ref, *refs):
    candidate_ref, block_ref, messages = refs[6], refs[7], refs[8:12]
    patches_ref, weight_ref, caption_ref, probe_ref, states_ref, ask_ref, sems = refs[12:]
    fetched(refs[:6], refs[12:18], sems)
    across = (((1,), (1,)), ((), ()))
    patches = patches_ref[0]
    weight = weight_ref[...]
    last = lax.dot_general(patches[256:257], weight, across, preferred_element_type=F32)
    pad = jnp.zeros((1, HD), F32)
    captions = caption_ref[...].astype(F32)
    tail = [jnp.concatenate([last[:, h * HD : (h + 1) * HD], pad], axis=1) for h in range(3)]
    tail += [
        lax.shift_right_logical(probe_ref[...], 4).astype(F32),
        (probe_ref[...] & 15).astype(F32),
        jnp.zeros((3, 128), F32),
        captions[:, 0:128],
        captions[:, 128:256],
    ]
    block_ref[TAIL:BROWS, :] = jnp.concatenate(tail).astype(BF16)

    @pl.when(group_ref[0] < 4)
    def _():
        keys = lax.dot_general(patches[:256], weight, across, preferred_element_type=F32)
        for h in range(3):
            block_ref[h * 128 : (h + 1) * 128, 0:HD] = keys[:128, h * HD : (h + 1) * HD].astype(BF16)
            block_ref[h * 128 : (h + 1) * 128, HD:128] = keys[128:, h * HD : (h + 1) * HD].astype(BF16)

    @pl.when(group_ref[0] >= 4)
    def _():
        values = lax.dot_general(weight, patches[:256], across, preferred_element_type=F32)
        for h in range(3):
            rows = values[h * HD : (h + 1) * HD].astype(BF16)
            block_ref[h * 128 : h * 128 + HD] = rows[:, :128]
            block_ref[h * 128 + HD : (h + 1) * 128] = rows[:, 128:]

    queries = jnp.dot(states_ref[...].reshape(128, 768), ask_ref[...], preferred_element_type=F32)
    ids = jnp.concatenate([candidate_ref[c] for c in range(4)], axis=1).astype(F32)
    tail = jnp.concatenate([ids, jnp.zeros((16, 252), F32)], axis=1).astype(BF16)
    pad = jnp.zeros((128, HD), F32)
    x = lax.shift_right_logical(group_ref[0], 1)
    for k in range(4):
        rows = jnp.concatenate([queries[:, k * 192 : (k + 1) * 192], pad], axis=1).astype(BF16)
        for d in range(4):

            @pl.when(((k - x) & 3) == d)
            def _():
                messages[d][0:128, :] = rows

    for d in range(4):
        messages[d][128:144, :] = tail


def opening(group, sources, candidates):
    vmem, hbm = pl.BlockSpec(memory_space=pltpu.VMEM), pl.BlockSpec(memory_space=pltpu.HBM)
    outs = pl.pallas_call(
        open_kernel,
        out_shape=[jax.ShapeDtypeStruct((BROWS, 128), BF16)]
        + [jax.ShapeDtypeStruct((144, 256), BF16)] * 4,
        in_specs=[pl.BlockSpec(memory_space=pltpu.SMEM)] + [hbm] * 6 + [vmem],
        out_specs=[vmem] * 5,
        scratch_shapes=[pltpu.VMEM(source.shape, source.dtype) for source in sources]
        + [pltpu.SemaphoreType.DMA((6,))],
        compiler_params=pltpu.CompilerParams(vmem_limit_bytes=12 * 1024 * 1024),
        name="opening",
    )(group, *[in_hbm(source) for source in sources], candidates)
    return outs[0], outs[1:]


def hold_kernel(*refs):
    pass


def hold(values, after):
    hbm = pl.BlockSpec(memory_space=pltpu.HBM)
    return pl.pallas_call(
        hold_kernel,
        out_shape=[jax.ShapeDtypeStruct(value.shape, value.dtype) for value in values],
        in_specs=[hbm] * (len(values) + len(after)),
        out_specs=[hbm] * len(values),
        input_output_aliases={k: k for k in range(len(values))},
        compiler_params=pltpu.CompilerParams(vmem_limit_bytes=1024 * 1024),
        name="hold",
    )(*[in_hbm(value) for value in values], *after)


def spread_kernel(q0, q1, q2, q3, query):
    left = lax.broadcasted_iota(jnp.int32, (128, 128), 1) < HD
    for d, q_ref in enumerate((q0, q1, q2, q3)):
        rows = q_ref[0:128, :].astype(F32)
        first, second = rows[:, 0:128], rows[:, 128:256]
        turned = pltpu.roll(first, HD, 1)
        parts = (
            (jnp.where(left, first, 0.0), jnp.where(left, 0.0, turned)),
            (jnp.where(left, turned, 0.0), jnp.where(left, 0.0, first)),
            (second, pltpu.roll(second, HD, 1)),
        )
        for h in range(3):
            for side in range(2):
                for c in range(4):
                    query[h, side, d * 4 + c] = parts[h][side][c * 32 : (c + 1) * 32].astype(BF16)


def spread(messages):
    vmem = pl.BlockSpec(memory_space=pltpu.VMEM)
    return pl.pallas_call(
        spread_kernel,
        out_shape=jax.ShapeDtypeStruct((3, 2, 16, NQ, 128), BF16),
        in_specs=[vmem] * 4,
        out_specs=vmem,
        compiler_params=pltpu.CompilerParams(vmem_limit_bytes=8 * 1024 * 1024),
        name="spread",
    )(*messages)


def attend_kernel(sizes, unroll, fresh, final, core_ref, image_ref, count_ref, table_ref, query, *refs):
    parts = len(sizes)
    own_refs, other_refs = refs[:parts], refs[parts : 2 * parts]
    refs = refs[2 * parts + (0 if fresh else 1) :]
    context, token = refs[0:2]
    outs = refs[2:6] if final else ()
    held, column, tiles = refs[2 + len(outs) : 5 + len(outs)]
    images = sum(sizes)
    first_core = core_ref[0] == 0
    total = jnp.int32(0)
    for i in range(images):
        for t in range(3):
            tiles[total + t] = 4 * i + t
        total = total + lax.shift_right_logical(count_ref[image_ref[i]] + 3, 2)
    start = 0
    for part, size in enumerate(sizes):
        for k in range(size):
            mine, theirs = own_refs[part][k], other_refs[part][k]
            held[0, start + k] = jnp.where(first_core, mine, theirs)
            held[1, start + k] = jnp.where(first_core, theirs, mine)
        start += size
    for i in range(images):
        turned = held[1, i, TAIL:BROWS, :].astype(F32).T
        for h in range(3):
            column[i, h] = jnp.broadcast_to(turned[0:HD, h : h + 1], (HD, 128))

    def scores(code):
        i = lax.shift_right_logical(code, 2)
        image = image_ref[i]
        last = count_ref[image] - 1
        first = (code & 3) * 4
        pairs = [table_ref[image * SLOTS + jnp.minimum(first + j, last)] for j in range(4)]
        caps = [lax.shift_right_logical(p, 4) for p in pairs]
        found = []
        for h in range(3):
            q = jnp.concatenate(
                [query[h, 0, c] for c in caps] + [query[h, 1, c] for c in caps], axis=0
            )
            keys = jnp.concatenate([held[0, i, h * 128 : (h + 1) * 128, :], held[0, i, TAIL:BROWS, :]])
            found.append(
                lax.dot_general(
                    keys,
                    q,
                    (((1,), (1,)), ((), ())),
                    preferred_element_type=F32,
                )
            )
        return i, pairs, found

    def mix(i, pairs, found):
        contexts = []
        for h in range(3):
            s = found[h]
            top, bottom, cls = s[:128, :128], s[:128, 128:], s[128 + h : 129 + h, :128]
            highest = jnp.maximum(jnp.max(jnp.maximum(top, bottom), axis=0, keepdims=True), cls)
            e_top = jnp.exp2((top - highest) * EXP_SCALE)
            e_bottom = jnp.exp2((bottom - highest) * EXP_SCALE)
            e_cls = jnp.exp2((cls - highest) * EXP_SCALE)
            inverse = 1.0 / (jnp.sum(e_top + e_bottom, axis=0, keepdims=True) + e_cls)
            a_cls = (e_cls * inverse).astype(BF16).astype(F32)
            a = jnp.concatenate(
                [(e_top * inverse).astype(BF16), (e_bottom * inverse).astype(BF16)], axis=0
            )
            at = h * 128
            v = jnp.concatenate([held[1, i, at : at + HD, :], held[1, i, at + HD : at + 128, :]], axis=1)
            contexts.append(jnp.dot(v, a, preferred_element_type=F32) + column[i, h] * a_cls)
        both = jnp.concatenate(contexts[0:2], axis=0).astype(BF16).T
        third = jnp.concatenate([contexts[2], pltpu.roll(contexts[2], 128 - 16, 1)], axis=0)
        third = third.astype(BF16).T
        for j in range(4):
            context[pairs[j], 0:32, :] = both[j * 32 : (j + 1) * 32]
            context[pairs[j], 32:48, :] = third[j * 32 : j * 32 + 16]

    def group(g, carry):
        codes = [tiles[jnp.minimum(g * unroll + u, total - 1)] for u in range(unroll)]
        for item in [scores(code) for code in codes]:
            mix(*item)
        return carry

    lax.fori_loop(0, lax.div(total + unroll - 1, unroll), group, 0)
    token[...] = jnp.zeros_like(token)
    if final:
        fetched([context.at[pl.ds(at, size)] for at, size in PARTS], outs, refs[-1])


def attend(core, image_of, count, table, query, own, other, context, final):
    sizes = tuple(part.shape[0] for part in own)
    images = sum(sizes)
    fresh = context is None
    smem, vmem = pl.BlockSpec(memory_space=pltpu.SMEM), pl.BlockSpec(memory_space=pltpu.VMEM)
    operands = [core, image_of, count, table, query, *own, *other] + ([] if fresh else [context])
    parts = PARTS if final else ()
    outs = pl.pallas_call(
        functools.partial(attend_kernel, sizes, 5, fresh, final),
        out_shape=[jax.ShapeDtypeStruct((256, 48, 128), BF16), jax.ShapeDtypeStruct((8, 128), F32)]
        + [jax.ShapeDtypeStruct((size, 48, 128), BF16) for _, size in parts],
        in_specs=[smem] * 4 + [vmem] * (len(operands) - 4),
        out_specs=[vmem, vmem] + [pl.BlockSpec(memory_space=pltpu.HBM)] * len(parts),
        input_output_aliases={} if fresh else {len(operands) - 1: 0},
        scratch_shapes=[
            pltpu.VMEM((2, images, BROWS, 128), BF16),
            pltpu.VMEM((images, 3, HD, 128), F32),
            pltpu.SMEM((images * 3 + 4,), jnp.int32),
        ]
        + ([pltpu.SemaphoreType.DMA((4,))] if final else []),
        cost_estimate=pl.CostEstimate(
            flops=images * 600_000_000, bytes_accessed=images * 800_000, transcendentals=images * 800_000
        ),
        compiler_params=pltpu.CompilerParams(vmem_limit_bytes=14 * 1024 * 1024),
        name="attend",
    )(*operands)
    return outs[0], outs[1], outs[2:]


def score_kernel(shard_ref, *refs):
    count = len(refs) - 6
    pieces, gallery, out_ref = refs[:count], refs[count], refs[count + 1]
    tails, rows, scores, sems = refs[count + 2 :]
    copies = [pltpu.make_async_copy(gallery, rows, sems.at[count])]
    start = 0
    for k, piece in enumerate(pieces):
        images = piece.shape[0]
        copies.append(
            pltpu.make_async_copy(
                piece.at[:, pl.ds(TAIL, 16), :], tails.at[pl.ds(start, images)], sems.at[k]
            )
        )
        start += images
    for copy in copies:
        copy.start()
    for copy in copies:
        copy.wait()
    scale = 1.0 / (0.07 * math.sqrt(256))
    first, second = [], []
    for i in range(32):
        tail = tails[i].astype(F32)
        first.append(tail[8:12])
        second.append(tail[12:16])
    captions = jnp.concatenate([jnp.concatenate(first), jnp.concatenate(second)], axis=1).astype(BF16)
    tail = tails[0].astype(F32)
    near = tail[3:4] == shard_ref[0].astype(F32)
    highest = jnp.full((8, 128), -1e30, F32)
    alive = []
    for b in range(16):
        hit = jnp.where(jnp.logical_and(near, tail[4:5] == float(b)), 1.0, 0.0)
        alive.append(jnp.broadcast_to(jnp.max(hit, axis=1, keepdims=True), (8, 128)) > 0.5)
        s = lax.dot_general(
            rows[b * BLK : (b + 1) * BLK], captions, (((1,), (1,)), ((), ())), preferred_element_type=F32
        )
        s = s * scale
        scores[b] = s
        most = jnp.max(s.reshape(BLK // 8, 8, 128), axis=0)
        highest = jnp.maximum(highest, jnp.where(alive[b], most, -1e30))
    top = jnp.max(highest, axis=0, keepdims=True)
    total = jnp.zeros((8, 128), F32)
    for b in range(16):
        e = jnp.sum(jnp.exp(scores[b] - top).reshape(BLK // 8, 8, 128), axis=0)
        total = total + jnp.where(alive[b], e, 0.0)
    out_ref[0:1, :] = top
    out_ref[1:2, :] = jnp.sum(total, axis=0, keepdims=True)


def score(shard, pieces, gallery):
    hbm = pl.BlockSpec(memory_space=pltpu.HBM)
    return pl.pallas_call(
        score_kernel,
        out_shape=jax.ShapeDtypeStruct((2, 128), F32),
        in_specs=[pl.BlockSpec(memory_space=pltpu.SMEM)] + [hbm] * (len(pieces) + 1),
        out_specs=pl.BlockSpec(memory_space=pltpu.VMEM),
        scratch_shapes=[
            pltpu.VMEM((32, 16, 128), BF16),
            pltpu.VMEM(gallery.shape, BF16),
            pltpu.VMEM((16, BLK, 128), F32),
            pltpu.SemaphoreType.DMA((len(pieces) + 1,)),
        ],
        cost_estimate=pl.CostEstimate(flops=1000, bytes_accessed=1000, transcendentals=0),
        compiler_params=pltpu.CompilerParams(vmem_limit_bytes=12 * 1024 * 1024),
        name="score",
    )(shard, *pieces, gallery)


def finish_kernel(x_ref, c0, c1, c2, c3, weight_ref, states_ref, gain_ref, bias_ref, out_ref, main, low, high):
    @pl.when(pl.program_id(0) == 0)
    def _():
        low[...] = jnp.zeros_like(low)
        high[...] = jnp.zeros_like(high)
        for d in range(4):
            source = lax.rem(x_ref[0] + d, 4)
            main[d * 128 : (d + 1) * 128] = weight_ref[source, 0:128]
            low[d * 128 : d * 128 + 64] = weight_ref[source, 128:192]
            high[d * 128 + 64 : d * 128 + 128] = weight_ref[source, 128:192]

    parts = (c0, c1, c2, c3)
    count = c0.shape[0]
    first = jnp.concatenate([part[:, 0:32, :].reshape(count * 32, 128) for part in parts], axis=1)
    second = jnp.concatenate([part[:, 32:48, :].reshape(count * 16, 128) for part in parts], axis=1)
    mixed = jnp.dot(first, main[...], preferred_element_type=F32).reshape(count, 2, 16, 768)
    early = jnp.dot(second, low[...], preferred_element_type=F32).reshape(count, 16, 768)
    late = jnp.dot(second, high[...], preferred_element_type=F32).reshape(count, 16, 768)
    states = states_ref[0].astype(F32)
    gain = gain_ref[...]
    bias = bias_ref[...]
    for half, extra in ((0, early), (1, late)):
        hidden = mixed[:, half] + extra + states[half * 16 : (half + 1) * 16][None]
        average = jnp.mean(hidden, axis=-1, keepdims=True)
        centered = hidden - average
        variance = jnp.mean(centered * centered, axis=-1, keepdims=True)
        out_ref[0, :, half * 16 : (half + 1) * 16, :] = (
            centered * lax.rsqrt(variance + 1e-06) * gain + bias
        ).astype(BF16)


def finish(x, contexts, output_weight, query_states, gain, bias):
    per_step = 16
    each = pl.BlockSpec((per_step, 48, 128), lambda s, *_: (s, 0, 0))
    return pl.pallas_call(
        finish_kernel,
        out_shape=jax.ShapeDtypeStruct((4, 16, NQ, 768), BF16),
        grid_spec=pltpu.PrefetchScalarGridSpec(
            num_scalar_prefetch=1,
            grid=(64 // per_step,),
            in_specs=[each] * 4
            + [
                pl.BlockSpec((4, 192, 768), lambda s, *_: (0, 0, 0)),
                pl.BlockSpec((1, NQ, 768), lambda s, *_: (s, 0, 0)),
                pl.BlockSpec((1, 768), lambda s, *_: (0, 0)),
                pl.BlockSpec((1, 768), lambda s, *_: (0, 0)),
            ],
            out_specs=pl.BlockSpec((1, 16, NQ, 768), lambda s, *_: (s, 0, 0, 0)),
            scratch_shapes=[pltpu.VMEM((512, 768), BF16)] * 3,
        ),
        compiler_params=pltpu.CompilerParams(vmem_limit_bytes=32 * 1024 * 1024),
        name="finish",
    )(x, *contexts, output_weight.reshape(4, 192, 768), query_states, gain.reshape(1, 768), bias.reshape(1, 768))


def grid_moves(dy, dz):
    return [
        (y * 8 + z, ((y + dy) % 4) * 8 + (z + dz) % 8) for y in range(4) for z in range(8)
    ]


def group_moves(dx, flip=0):
    return [(2 * x + c, 2 * ((x + dx) % 4) + (c ^ flip)) for x in range(4) for c in range(2)]


def on_device(
    caption_embed,
    gallery_embed,
    probe_blocks,
    query_states,
    patches,
    candidates,
    query_weight,
    keyvalue_weight,
    output_weight,
    norm_gain,
    norm_bias,
):
    group_index = lax.axis_index("group")
    shard_index = lax.axis_index("shard")
    x, core = group_index // 2, group_index % 2
    my_y, my_z = shard_index // 8, shard_index % 8
    cap_dev, tokens, model_width = query_states.shape

    def along_shard(value, dy, dz):
        return lax.ppermute(value, "shard", grid_moves(dy, dz))

    def along_group(value, dx, flip=0):
        return lax.ppermute(value, "group", group_moves(dx, flip))

    sources = [patches, keyvalue_weight.T, caption_embed, probe_blocks, query_states, query_weight]
    block, messages = opening(group_index.reshape(1), sources, candidates)
    homes = [(k, 2 * k) for k in range(4)] + [(4 + k, 2 * k + 1) for k in range(4)]

    def homeward(dy):
        moves = [(g * 32 + a, h * 32 + b) for g, h in homes for a, b in grid_moves(dy, 0)]
        return lax.ppermute(block, ("group", "shard"), moves)

    arrived = [homeward(dy) for dy in range(4)]
    received = [messages[0]] + [along_group(messages[4 - d], 4 - d) for d in (1, 2, 3)]
    stack = jnp.stack(arrived)
    pair_images = jnp.stack([part[128:144, :4].T for part in received]).reshape(256).astype(jnp.int32)
    numbers = jnp.arange(256, dtype=jnp.int32)
    same = pair_images[:, None] == pair_images[None, :]
    rank = jnp.sum(jnp.logical_and(same, numbers[None, :] < numbers[:, None]), axis=1)
    position = pair_images * SLOTS + rank
    places = jnp.arange(32 * SLOTS, dtype=jnp.int32)
    table = jnp.sum(
        jnp.where(position[None, :] == places[:, None], numbers[None, :], 0), axis=1
    ).astype(jnp.int32)
    count = jnp.sum(
        pair_images[None, :] == jnp.arange(32, dtype=jnp.int32)[:, None], axis=1
    ).astype(jnp.int32)

    query = spread(received)
    def images(y_shifts, z_shift):
        return [((my_y - dy) % 4) * 8 + (my_z - z_shift) % 8 for dy in y_shifts]

    whole = (0, 1, 2, 3)
    piece_images = [images(whole, 0)]
    piece_images += [images(whole, k) + images(whole, -k) for k in (1, 2, 3)]
    piece_images += [images((0, 1), 4) + images((2, 3), -4)]
    piece_images = [jnp.stack(part).astype(jnp.int32) for part in piece_images]
    image_of = jnp.concatenate(piece_images)

    pieces = [[stack]]
    context = None
    right = left = stack
    for step in range(5):
        if step < 3:
            coming = [along_shard(right, 0, 1), along_shard(left, 0, -1)]
        elif step == 3:
            coming = [along_shard(right[:2], 0, 1), along_shard(left[2:], 0, -1)]
        own = pieces[-1]
        other = [along_group(part, 0, 1) for part in own]
        context, token, outs = attend(
            core.reshape(1), piece_images[step], count, table, query, own, other, context, step == 4
        )
        if step < 4:
            right, left = coming
            pieces.append([right, left])

    sent = [outs[0]] + [along_group(outs[4 - d], 4 - d) for d in (1, 2, 3)]

    partial = score(shard_index.reshape(1), [part for own in pieces for part in own], gallery_embed)
    order = jnp.arange(32, dtype=jnp.int32)
    pick = image_of[None, :] == order[:, None]
    partial = partial.reshape(2, 32, 4)
    partial = jnp.sum(jnp.where(pick[:, None, :, None], partial[None], 0.0), axis=2)
    partial = lax.all_to_all(partial, "shard", split_axis=0, concat_axis=0, tiled=True)
    top = jnp.max(partial[:, 0], axis=0)
    normalizer = top + jnp.log(jnp.sum(partial[:, 1] * jnp.exp(partial[:, 0] - top[None]), axis=0))
    normalizer = hold([jnp.pad(normalizer.reshape(1, 4), ((0, 7), (0, 124)))], sent[1:])[0]
    normalizer = lax.ppermute(normalizer, "group", [(h, g) for g, h in homes])[0, :4]

    layer_out = finish(x.reshape(1), sent, output_weight, query_states, norm_gain, norm_bias)
    return (layer_out, normalizer)


def solution(mesh):
    placed = (
        P(("group", "shard"), None),
        P("shard", None),
        P("group", None),
        P(("group", "shard"), None, None),
        P("shard", None, None),
        P(("group", "shard"), None, None),
        P(),
        P(None, "group"),
        P(),
        P(),
        P(),
    )
    return jax.shard_map(
        on_device,
        mesh=mesh,
        in_specs=placed,
        out_specs=(P(("group", "shard"), None, None, None), P(("group", "shard"))),
        check_vma=False,
    )
```

time: 215 us -> 147 us (0.68)
  Pallas kernels: 73.4 us -> 36.6 us
  starting transfers between devices: 58.6 us -> 43.9 us
  blocking collectives: 0 us -> 13.7 us
  waiting for transfers between devices: 49.8 us -> 36.2 us
  local copies, waits for them, and re-layouts: 19.5 us -> 11.4 us
  matrix products: 4.58 us -> 0 us
  other arithmetic: 7.1 us -> 3.41 us
    pallas_call x2 -> x9, Pallas kernels: 65.9 us -> 30.3 us  [the longest x5 25.6 us: attend(): pl.pallas_call(functools.partial(attend_kernel, sizes, 5, fresh, final),...]
    ppermute x11 -> x8, waiting for transfers between devices: 25.4 us -> 8.07 us  [along_shard(): return lax.ppermute(value, 'shard', grid_moves(dy, dz))]
    all_to_all x0 -> x1, blocking collectives: none -> 13.7 us  [on_device(): lax.all_to_all(partial, 'shard', split_axis=0, concat_axis=0, tiled=True)]
    ppermute x10 -> x15, starting transfers between devices: 25.5 us -> 13.4 us  [along_group(): return lax.ppermute(value, 'group', group_moves(dx, flip))]
    ppermute x10 -> x15, waiting for transfers between devices: 17 us -> 28.1 us  [along_group(): return lax.ppermute(value, 'group', group_moves(dx, flip))]
    ppermute x1 -> x5, starting transfers between devices: 4.64 us -> 14.8 us  [the longest x4 11.9 us: homeward(): return lax.ppermute(block, ('group', 'shard'), moves)]
    all_to_all x1 -> x0, starting transfers between devices: 8.4 us -> none  [on_device(): lax.all_to_all(partial, 'shard', split_axis=0, concat_axis=0, tiled=True)]
    all_to_all x1 -> x0, waiting for transfers between devices: 7.38 us -> none  [on_device(): lax.all_to_all(partial, 'shard', split_axis=0, concat_axis=0, tiled=True)]
  transfers between devices with their start and end apart: 23 -> 28, of which waited for: 11 -> 7; matrix products, arithmetic and copies ran while one was open for 10% -> 7% of each run, Pallas kernels for 0% -> 19%
where the time goes in v2:
time: 147 us; the launch traced here: 146 us
  starting transfers between devices  43.9 us (30%)
  Pallas kernels  36.6 us (25%)
  waiting for transfers between devices  36.2 us (25%)
  blocking collectives  13.7 us (9%)
  local copies, waits for them, and re-layouts  11.4 us (8%)
  other arithmetic  3.41 us (2%)
    ppermute x15, waiting for transfers between devices, along_group(): return lax.ppermute(value, 'group', group_moves(dx, flip))  28.1 us
    pallas_call x5, Pallas kernels, attend(): pl.pallas_call(functools.partial(attend_kernel, sizes, 5, fresh, final),...  25.6 us
    ppermute x8, starting transfers between devices, along_shard(): return lax.ppermute(value, 'shard', grid_moves(dy, dz))  15.7 us
    all_to_all x1, blocking collectives, on_device(): lax.all_to_all(partial, 'shard', split_axis=0, concat_axis=0, tiled=True)  13.7 us
    ppermute x15, starting transfers between devices, along_group(): return lax.ppermute(value, 'group', group_moves(dx, flip))  13.4 us
    ppermute x4, starting transfers between devices, homeward(): return lax.ppermute(block, ('group', 'shard'), moves)  11.9 us
    ppermute x8, waiting for transfers between devices, along_shard(): return lax.ppermute(value, 'shard', grid_moves(dy, dz))  8.07 us
    pallas_call x1, Pallas kernels, finish(): pl.pallas_call(finish_kernel, out_shape=jax.ShapeDtypeStruct((4, 16, NQ,...  6.35 us
  transfers between devices with their start and end apart: 28, of which 7 were waited for; matrix products, arithmetic and copies ran while one was open for 7% of the time, Pallas kernels for 19%

profile of v2, /device:TPU:1, one launch (start us, length us, event | category | flops | bytes accessed | tf_op | source)
XLA Modules:
  0.0 146.1 jit_solution(18410283039809609184)
XLA Ops:
  1.4 3.2 %opening.1 = (bf16[400,128]{1,0:T(8,128)(2,1)S(1)}, bf16[144,256]{1,0:T(8,128)(2,1)S(1)}, bf16[144,256]{1,0:T(8,128)(2,1)S(1)}, bf16[144,256]{1,0:T(8,128)(2,1)S(1)}, bf16[144,256]{1,0:T(8,128)(2,1)S(1)}) custom-call(s32[1]{0:T(128)} %bitcast.6.group_ref, bf16[1,257,1408]{2,1,0:T(8,128)(2,1)} %refs_0_.1, bf16[192,1408]{1,0:T(8,128)(2,1)} %bitcast.69, ...), custom_call_target="tpu_custom_call" | custom-call | tf_op jit(solution)/shard_map/opening/pallas_call | solution.py:93
  4.6 4.5 %collective-permute-start.3 = (bf16[400,128]{1,0:T(8,128)(2,1)S(1)}, bf16[400,128]{1,0:T(8,128)(2,1)S(1)}, u32[]{:S(2)}, u32[]{:S(2)}) collective-permute-start(bf16[400,128]{1,0:T(8,128)(2,1)S(1)} %get-tuple-element.19), channel_id=1, source_target_pairs={{0,0},{1,1},{2,2},{3,3},{4,4},{5,5},{6,6},{7,7},{8,8},{9,9},{10,10... | collective-permute-start | bytes 307208 | tf_op jit(solution)/shard_map/ppermute | solution.py:430
  9.1 2.6 %collective-permute-start.4 = (bf16[400,128]{1,0:T(8,128)(2,1)S(1)}, bf16[400,128]{1,0:T(8,128)(2,1)S(1)}, u32[]{:S(2)}, u32[]{:S(2)}) collective-permute-start(bf16[400,128]{1,0:T(8,128)(2,1)S(1)} %get-tuple-element.19), channel_id=1, source_target_pairs={{0,8},{1,9},{2,10},{3,11},{4,12},{5,13},{6,14},{7,15},{8,16},{9,17... | collective-permute-start | bytes 307208 | tf_op jit(solution)/shard_map/ppermute | solution.py:430
  11.7 2.3 %collective-permute-start.5 = (bf16[400,128]{1,0:T(8,128)(2,1)S(1)}, bf16[400,128]{1,0:T(8,128)(2,1)S(1)}, u32[]{:S(2)}, u32[]{:S(2)}) collective-permute-start(bf16[400,128]{1,0:T(8,128)(2,1)S(1)} %get-tuple-element.19), channel_id=1, source_target_pairs={{0,16},{1,17},{2,18},{3,19},{4,20},{5,21},{6,22},{7,23},{8,24},{9,... | collective-permute-start | bytes 307208 | tf_op jit(solution)/shard_map/ppermute | solution.py:430
  14.0 2.5 %collective-permute-start.6 = (bf16[400,128]{1,0:T(8,128)(2,1)S(1)}, bf16[400,128]{1,0:T(8,128)(2,1)S(1)}, u32[]{:S(2)}, u32[]{:S(2)}) collective-permute-start(bf16[400,128]{1,0:T(8,128)(2,1)S(1)} %get-tuple-element.19), channel_id=1, source_target_pairs={{0,24},{1,25},{2,26},{3,27},{4,28},{5,29},{6,30},{7,31},{8,0},{9,1... | collective-permute-start | bytes 307208 | tf_op jit(solution)/shard_map/ppermute | solution.py:430
  17.2 4.5 %collective-permute-done.q1 = bf16[144,256]{1,0:T(8,128)(2,1)S(1)} collective-permute-done((bf16[144,256]{1,0:T(8,128)(2,1)S(1)}, bf16[144,256]{1,0:T(8,128)(2,1)S(1)}, u32[]{:S(2)}, u32[]{:S(2)}) %collective-permute-start) | collective-permute-done | bytes 73760 | tf_op jit(solution)/shard_map/ppermute | solution.py:422
  21.7 5.5 %collective-permute-done.1.q2 = bf16[144,256]{1,0:T(8,128)(2,1)S(1)} collective-permute-done((bf16[144,256]{1,0:T(8,128)(2,1)S(1)}, bf16[144,256]{1,0:T(8,128)(2,1)S(1)}, u32[]{:S(2)}, u32[]{:S(2)}) %collective-permute-start.1) | collective-permute-done | bytes 73760 | tf_op jit(solution)/shard_map/ppermute | solution.py:422
  27.2 4.4 %collective-permute-done.2.q3 = bf16[144,256]{1,0:T(8,128)(2,1)S(1)} collective-permute-done((bf16[144,256]{1,0:T(8,128)(2,1)S(1)}, bf16[144,256]{1,0:T(8,128)(2,1)S(1)}, u32[]{:S(2)}, u32[]{:S(2)}) %collective-permute-start.2) | collective-permute-done | bytes 73760 | tf_op jit(solution)/shard_map/ppermute | solution.py:422
  32.0 1.7 %collective-permute-start.7 = (bf16[4,400,128]{2,1,0:T(8,128)(2,1)S(1)}, bf16[4,400,128]{2,1,0:T(8,128)(2,1)S(1)}, u32[]{:S(2)}, u32[]{:S(2)}) collective-permute-start(bf16[4,400,128]{2,1,0:T(8,128)(2,1)S(1)} %pad_maximum_fusion.refs_0_), channel_id=1, source_target_pairs={{0,1},{1,2},{2,3},{3,4},{4,5},{5,6},{6,7},{7,0},{8,9},{9,10},{10,1... | collective-permute-start | bytes 1228808 | tf_op jit(solution)/shard_map/ppermute | solution.py:419
  33.7 4.0 %collective-permute-start.11 = (bf16[4,400,128]{2,1,0:T(8,128)(2,1)S(1)}, bf16[4,400,128]{2,1,0:T(8,128)(2,1)S(1)}, u32[]{:S(2)}, u32[]{:S(2)}) collective-permute-start(bf16[4,400,128]{2,1,0:T(8,128)(2,1)S(1)} %pad_maximum_fusion.refs_0_), channel_id=1, source_target_pairs={{0,7},{1,0},{2,1},{3,2},{4,3},{5,4},{6,5},{7,6},{8,15},{9,8},{10,9... | collective-permute-start | bytes 1228808 | tf_op jit(solution)/shard_map/ppermute | solution.py:419
  38.2 2.2 %collective-permute-start.23 = (bf16[4,400,128]{2,1,0:T(8,128)(2,1)S(1)}, bf16[4,400,128]{2,1,0:T(8,128)(2,1)S(1)}, u32[]{:S(2)}, u32[]{:S(2)}) collective-permute-start(bf16[4,400,128]{2,1,0:T(8,128)(2,1)S(1)} %pad_maximum_fusion.refs_0_), channel_id=1, source_target_pairs={{0,32},{32,0},{64,96},{96,64},{128,160},{160,128},{192,224},{224,1... | collective-permute-start | bytes 1228808 | tf_op jit(solution)/shard_map/ppermute | solution.py:422
  40.4 5.2 %collective-permute-done.7.refs_0_.refs_1_ = bf16[4,400,128]{2,1,0:T(8,128)(2,1)S(1)} collective-permute-done((bf16[4,400,128]{2,1,0:T(8,128)(2,1)S(1)}, bf16[4,400,128]{2,1,0:T(8,128)(2,1)S(1)}, u32[]{:S(2)}, u32[]{:S(2)}) %collective-permute-start.7) | collective-permute-done | bytes 409632 | tf_op jit(solution)/shard_map/ppermute | solution.py:419
  45.6 2.5 %collective-permute-start.21 = (bf16[4,400,128]{2,1,0:T(8,128)(2,1)S(1)}, bf16[4,400,128]{2,1,0:T(8,128)(2,1)S(1)}, u32[]{:S(2)}, u32[]{:S(2)}) collective-permute-start(bf16[4,400,128]{2,1,0:T(8,128)(2,1)S(1)} %collective-permute-done.7.refs_0_.refs_1_), channel_id=1, source_target_pairs={{0,32},{32,0},{64,96},{96,64},{128,160},{160,128},{192,224},{224,1... | collective-permute-start | bytes 1228808 | tf_op jit(solution)/shard_map/ppermute | solution.py:422
  48.1 3.0 %collective-permute-start.12 = (bf16[4,400,128]{2,1,0:T(8,128)(2,1)S(1)}, bf16[4,400,128]{2,1,0:T(8,128)(2,1)S(1)}, u32[]{:S(2)}, u32[]{:S(2)}) collective-permute-start(bf16[4,400,128]{2,1,0:T(8,128)(2,1)S(1)} %collective-permute-done.11.refs_1_.refs_2_), channel_id=1, source_target_pairs={{0,7},{1,0},{2,1},{3,2},{4,3},{5,4},{6,5},{7,6},{8,15},{9,8},{10,9... | collective-permute-start | bytes 1228808 | tf_op jit(solution)/shard_map/ppermute | solution.py:419
  51.7 3.9 %attend.5 = (bf16[256,48,128]{2,1,0:T(8,128)(2,1)S(1)}, f32[8,128]{1,0:T(8,128)}) custom-call(s32[1]{0:T(128)} %bitcast.1.core_ref, s32[4]{0:T(128)S(1)} %pad_add_fusion.1.image_ref, s32[32]{0:T(128)S(1)} %convert_reduce_fusion.1.count_ref, s32[384]{0:T(512)S(1)} %select_reduce_fusion.table_ref, bf16[3,2,16,32,128]{4,3,2,1,0:T(8,128)(2,1)S(1)} %spread.1.query, ...), custom_call_target="tpu_custom_call" | custom-call | flops 2400000000 | bytes 3200000 | tf_op jit(solution)/shard_map/attend/pallas_call | solution.py:245
  55.6 3.1 %collective-permute-start.19 = (bf16[4,400,128]{2,1,0:T(8,128)(2,1)S(1)}, bf16[4,400,128]{2,1,0:T(8,128)(2,1)S(1)}, u32[]{:S(2)}, u32[]{:S(2)}) collective-permute-start(bf16[4,400,128]{2,1,0:T(8,128)(2,1)S(1)} %collective-permute-done.8.refs_0_.refs_3_), channel_id=1, source_target_pairs={{0,32},{32,0},{64,96},{96,64},{128,160},{160,128},{192,224},{224,1... | collective-permute-start | bytes 1228808 | tf_op jit(solution)/shard_map/ppermute | solution.py:422
  58.7 1.2 collective-permute-done.12.refs_1_.refs_4_
  59.9 3.4 %collective-permute-start.13 = (bf16[4,400,128]{2,1,0:T(8,128)(2,1)S(1)}, bf16[4,400,128]{2,1,0:T(8,128)(2,1)S(1)}, u32[]{:S(2)}, u32[]{:S(2)}) collective-permute-start(bf16[4,400,128]{2,1,0:T(8,128)(2,1)S(1)} %collective-permute-done.12.refs_1_.refs_4_), channel_id=1, source_target_pairs={{0,7},{1,0},{2,1},{3,2},{4,3},{5,4},{6,5},{7,6},{8,15},{9,8},{10,9... | collective-permute-start | bytes 1228808 | tf_op jit(solution)/shard_map/ppermute | solution.py:419
  63.3 1.1 collective-permute-start.20
  64.4 5.0 %attend.6 = (bf16[256,48,128]{2,1,0:T(8,128)(2,1)S(1)}, f32[8,128]{1,0:T(8,128)}) custom-call(s32[1]{0:T(128)} %bitcast.1.core_ref, s32[8]{0:T(128)S(1)} %stack.182.image_ref, s32[32]{0:T(128)S(1)} %convert_reduce_fusion.1.count_ref, s32[384]{0:T(512)S(1)} %select_reduce_fusion.table_ref, ...), custom_call_target="tpu_custom_call", output_to_operand_aliasing={{0}: (9, {})} | custom-call | flops 4800000000 | bytes 6400000 | tf_op jit(solution)/shard_map/attend/pallas_call | solution.py:245
  69.6 1.7 %collective-permute-done.13.refs_1_.refs_6_ = bf16[4,400,128]{2,1,0:T(8,128)(2,1)S(1)} collective-permute-done((bf16[4,400,128]{2,1,0:T(8,128)(2,1)S(1)}, bf16[4,400,128]{2,1,0:T(8,128)(2,1)S(1)}, u32[]{:S(2)}, u32[]{:S(2)}) %collective-permute-start.13) | collective-permute-done | bytes 409632 | tf_op jit(solution)/shard_map/ppermute | solution.py:419
  71.2 3.5 %collective-permute-start.14 = (bf16[2,400,128]{2,1,0:T(8,128)(2,1)S(1)}, bf16[2,400,128]{2,1,0:T(8,128)(2,1)S(1)}, u32[]{:S(2)}, u32[]{:S(2)}) collective-permute-start(bf16[2,400,128]{2,1,0:T(8,128)(2,1)S(1)} %slice.41), channel_id=1, source_target_pairs={{0,7},{1,0},{2,1},{3,2},{4,3},{5,4},{6,5},{7,6},{8,15},{9,8},{10,9... | collective-permute-start | bytes 614408 | tf_op jit(solution)/shard_map/ppermute | solution.py:419
  74.7 2.0 %collective-permute-start.17 = (bf16[4,400,128]{2,1,0:T(8,128)(2,1)S(1)}, bf16[4,400,128]{2,1,0:T(8,128)(2,1)S(1)}, u32[]{:S(2)}, u32[]{:S(2)}) collective-permute-start(bf16[4,400,128]{2,1,0:T(8,128)(2,1)S(1)} %collective-permute-done.9.refs_0_.refs_5_), channel_id=1, source_target_pairs={{0,32},{32,0},{64,96},{96,64},{128,160},{160,128},{192,224},{224,1... | collective-permute-start | bytes 1228808 | tf_op jit(solution)/shard_map/ppermute | solution.py:422
  76.8 5.0 %attend.7 = (bf16[256,48,128]{2,1,0:T(8,128)(2,1)S(1)}, f32[8,128]{1,0:T(8,128)}) custom-call(s32[1]{0:T(128)} %bitcast.1.core_ref, s32[8]{0:T(128)S(1)} %stack.173.image_ref, s32[32]{0:T(128)S(1)} %convert_reduce_fusion.1.count_ref, s32[384]{0:T(512)S(1)} %select_reduce_fusion.table_ref, ...), custom_call_target="tpu_custom_call", output_to_operand_aliasing={{0}: (9, {})} | custom-call | flops 4800000000 | bytes 6400000 | tf_op jit(solution)/shard_map/attend/pallas_call | solution.py:245
  82.4 6.1 %attend.8 = (bf16[256,48,128]{2,1,0:T(8,128)(2,1)S(1)}, f32[8,128]{1,0:T(8,128)}) custom-call(s32[1]{0:T(128)} %bitcast.1.core_ref, s32[8]{0:T(128)S(1)} %stack.164.image_ref, s32[32]{0:T(128)S(1)} %convert_reduce_fusion.1.count_ref, s32[384]{0:T(512)S(1)} %select_reduce_fusion.table_ref, ...), custom_call_target="tpu_custom_call", output_to_operand_aliasing={{0}: (9, {})} | custom-call | flops 4800000000 | bytes 6400000 | tf_op jit(solution)/shard_map/attend/pallas_call | solution.py:245
  88.6 5.5 %attend.9 = (bf16[256,48,128]{2,1,0:T(8,128)(2,1)S(1)}, f32[8,128]{1,0:T(8,128)}, bf16[64,48,128]{2,1,0:T(8,128)(2,1)S(1)}, bf16[64,48,128]{2,1,0:T(8,128)(2,1)}...) custom-call(s32[1]{0:T(128)} %bitcast.1.core_ref, ...), custom_call_target="tpu_custom_call", output_to_operand_aliasing={{0}: (9, {})} | custom-call | flops 2400000000 | bytes 3200000 | tf_op jit(solution)/shard_map/attend/pallas_call | solution.py:245
  96.4 1.4 score.1
  100.3 13.7 %all_to_all.5 = f32[32,2,4]{2,1,0:T(2,128)S(1)} all-to-all(f32[32,2,4]{2,1,0:T(2,128)} %copy.41), channel_id=1, replica_groups=mesh['group'=8,'shard'=32] {'shard'}, dimensions={0} | all-to-all | bytes 2048 | tf_op jit(solution)/shard_map/all_to_all | solution.py:483
  115.1 1.4 copy.42
  119.3 13.7 %collective-permute-done.26.c3.refs_3_ = bf16[64,48,128]{2,1,0:T(8,128)(2,1)S(1)} collective-permute-done((bf16[64,48,128]{2,1,0:T(8,128)(2,1)}, bf16[64,48,128]{2,1,0:T(8,128)(2,1)S(1)}, u32[]{:S(2)}, u32[]{:S(2)}) %collective-permute-start.26) | collective-permute-done | bytes 786464 | tf_op jit(solution)/shard_map/ppermute | solution.py:422
  133.0 2.8 %collective-permute-start.27 = (f32[8,128]{1,0:T(8,128)}, f32[8,128]{1,0:T(8,128)S(1)}, u32[]{:S(2)}, u32[]{:S(2)}) collective-permute-start(f32[8,128]{1,0:T(8,128)} %hold.1), channel_id=1, source_target_pairs={{0,0},{64,32},{128,64},{192,96},{32,128},{96,160},{160,192},{224,2... | collective-permute-start | bytes 12296 | tf_op jit(solution)/shard_map/ppermute | solution.py:487
  139.3 6.3 %finish.1 = bf16[4,16,32,768]{3,2,1,0:T(8,128)(2,1)} custom-call(s32[1]{0:T(128)} %bitcast.x_ref, bf16[64,48,128]{2,1,0:T(8,128)(2,1)S(1)} %copy-done.3, bf16[64,48,128]{2,1,0:T(8,128)(2,1)S(1)} %collective-permute-done.24.c1.refs_1_, bf16[64,48,128]{2,1,0:T(8,128)(2,1)S(1)} %collective-permute-done.25.c2.refs_2_, ...), custom_call_target="tpu_custom_call" | custom-call | tf_op jit(solution)/shard_map/finish/pallas_call | solution.py:368
  (87 shorter events, 16.2 us)
Async XLA Ops:
  4.6 27.3 %collective-permute-start.3 = (bf16[400,128]{1,0:T(8,128)(2,1)S(1)}, bf16[400,128]{1,0:T(8,128)(2,1)S(1)}, u32[]{:S(2)}, u32[]{:S(2)}) collective-permute-start(bf16[400,128]{1,0:T(8,128)(2,1)S(1)} %get-tuple-element.19), channel_id=1, source_target_pairs={{0,0},{1,1},{2,2},{3,3},{4,4},{5,5},{6,6},{7,7},{8,8},{9,9},{10,10... | collective-permute-start | bytes 307208 | tf_op jit(solution)/shard_map/ppermute | solution.py:430
  9.1 22.8 %collective-permute-start.4 = (bf16[400,128]{1,0:T(8,128)(2,1)S(1)}, bf16[400,128]{1,0:T(8,128)(2,1)S(1)}, u32[]{:S(2)}, u32[]{:S(2)}) collective-permute-start(bf16[400,128]{1,0:T(8,128)(2,1)S(1)} %get-tuple-element.19), channel_id=1, source_target_pairs={{0,8},{1,9},{2,10},{3,11},{4,12},{5,13},{6,14},{7,15},{8,16},{9,17... | collective-permute-start | bytes 307208 | tf_op jit(solution)/shard_map/ppermute | solution.py:430
  11.7 20.2 %collective-permute-start.5 = (bf16[400,128]{1,0:T(8,128)(2,1)S(1)}, bf16[400,128]{1,0:T(8,128)(2,1)S(1)}, u32[]{:S(2)}, u32[]{:S(2)}) collective-permute-start(bf16[400,128]{1,0:T(8,128)(2,1)S(1)} %get-tuple-element.19), channel_id=1, source_target_pairs={{0,16},{1,17},{2,18},{3,19},{4,20},{5,21},{6,22},{7,23},{8,24},{9,... | collective-permute-start | bytes 307208 | tf_op jit(solution)/shard_map/ppermute | solution.py:430
  14.0 17.9 %collective-permute-start.6 = (bf16[400,128]{1,0:T(8,128)(2,1)S(1)}, bf16[400,128]{1,0:T(8,128)(2,1)S(1)}, u32[]{:S(2)}, u32[]{:S(2)}) collective-permute-start(bf16[400,128]{1,0:T(8,128)(2,1)S(1)} %get-tuple-element.19), channel_id=1, source_target_pairs={{0,24},{1,25},{2,26},{3,27},{4,28},{5,29},{6,30},{7,31},{8,0},{9,1... | collective-permute-start | bytes 307208 | tf_op jit(solution)/shard_map/ppermute | solution.py:430
  16.5 5.2 %collective-permute-start = (bf16[144,256]{1,0:T(8,128)(2,1)S(1)}, bf16[144,256]{1,0:T(8,128)(2,1)S(1)}, u32[]{:S(2)}, u32[]{:S(2)}) collective-permute-start(bf16[144,256]{1,0:T(8,128)(2,1)S(1)} %get-tuple-element.16), channel_id=1, source_target_pairs={{0,192},{32,224},{64,0},{96,32},{128,64},{160,96},{192,128},{224,1... | collective-permute-start | bytes 221192 | tf_op jit(solution)/shard_map/ppermute | solution.py:422
  21.7 5.5 %collective-permute-start.1 = (bf16[144,256]{1,0:T(8,128)(2,1)S(1)}, bf16[144,256]{1,0:T(8,128)(2,1)S(1)}, u32[]{:S(2)}, u32[]{:S(2)}) collective-permute-start(bf16[144,256]{1,0:T(8,128)(2,1)S(1)} %get-tuple-element.17), channel_id=1, source_target_pairs={{0,128},{32,160},{64,192},{96,224},{128,0},{160,32},{192,64},{224,... | collective-permute-start | bytes 221192 | tf_op jit(solution)/shard_map/ppermute | solution.py:422
  27.2 4.4 %collective-permute-start.2 = (bf16[144,256]{1,0:T(8,128)(2,1)S(1)}, bf16[144,256]{1,0:T(8,128)(2,1)S(1)}, u32[]{:S(2)}, u32[]{:S(2)}) collective-permute-start(bf16[144,256]{1,0:T(8,128)(2,1)S(1)} %get-tuple-element.18), channel_id=1, source_target_pairs={{0,64},{32,96},{64,128},{96,160},{128,192},{160,224},{192,0},{224,... | collective-permute-start | bytes 221192 | tf_op jit(solution)/shard_map/ppermute | solution.py:422
  32.0 13.6 %collective-permute-start.7 = (bf16[4,400,128]{2,1,0:T(8,128)(2,1)S(1)}, bf16[4,400,128]{2,1,0:T(8,128)(2,1)S(1)}, u32[]{:S(2)}, u32[]{:S(2)}) collective-permute-start(bf16[4,400,128]{2,1,0:T(8,128)(2,1)S(1)} %pad_maximum_fusion.refs_0_), channel_id=1, source_target_pairs={{0,1},{1,2},{2,3},{3,4},{4,5},{5,6},{6,7},{7,0},{8,9},{9,10},{10,1... | collective-permute-start | bytes 1228808 | tf_op jit(solution)/shard_map/ppermute | solution.py:419
  33.7 14.4 %collective-permute-start.11 = (bf16[4,400,128]{2,1,0:T(8,128)(2,1)S(1)}, bf16[4,400,128]{2,1,0:T(8,128)(2,1)S(1)}, u32[]{:S(2)}, u32[]{:S(2)}) collective-permute-start(bf16[4,400,128]{2,1,0:T(8,128)(2,1)S(1)} %pad_maximum_fusion.refs_0_), channel_id=1, source_target_pairs={{0,7},{1,0},{2,1},{3,2},{4,3},{5,4},{6,5},{7,6},{8,15},{9,8},{10,9... | collective-permute-start | bytes 1228808 | tf_op jit(solution)/shard_map/ppermute | solution.py:419
  38.2 13.5 %collective-permute-start.23 = (bf16[4,400,128]{2,1,0:T(8,128)(2,1)S(1)}, bf16[4,400,128]{2,1,0:T(8,128)(2,1)S(1)}, u32[]{:S(2)}, u32[]{:S(2)}) collective-permute-start(bf16[4,400,128]{2,1,0:T(8,128)(2,1)S(1)} %pad_maximum_fusion.refs_0_), channel_id=1, source_target_pairs={{0,32},{32,0},{64,96},{96,64},{128,160},{160,128},{192,224},{224,1... | collective-permute-start | bytes 1228808 | tf_op jit(solution)/shard_map/ppermute | solution.py:422
  45.6 10.0 %collective-permute-start.8 = (bf16[4,400,128]{2,1,0:T(8,128)(2,1)S(1)}, bf16[4,400,128]{2,1,0:T(8,128)(2,1)S(1)}, u32[]{:S(2)}, u32[]{:S(2)}) collective-permute-start(bf16[4,400,128]{2,1,0:T(8,128)(2,1)S(1)} %collective-permute-done.7.refs_0_.refs_1_), channel_id=1, source_target_pairs={{0,1},{1,2},{2,3},{3,4},{4,5},{5,6},{6,7},{7,0},{8,9},{9,10},{10,1... | collective-permute-start | bytes 1228808 | tf_op jit(solution)/shard_map/ppermute | solution.py:419
  45.6 17.7 %collective-permute-start.21 = (bf16[4,400,128]{2,1,0:T(8,128)(2,1)S(1)}, bf16[4,400,128]{2,1,0:T(8,128)(2,1)S(1)}, u32[]{:S(2)}, u32[]{:S(2)}) collective-permute-start(bf16[4,400,128]{2,1,0:T(8,128)(2,1)S(1)} %collective-permute-done.7.refs_0_.refs_1_), channel_id=1, source_target_pairs={{0,32},{32,0},{64,96},{96,64},{128,160},{160,128},{192,224},{224,1... | collective-permute-start | bytes 1228808 | tf_op jit(solution)/shard_map/ppermute | solution.py:422
  48.1 16.4 %copy-start.5 = (bf16[4,400,128]{2,1,0:T(8,128)(2,1)}, bf16[4,400,128]{2,1,0:T(8,128)(2,1)S(1)}, u32[]{:S(2)}) copy-start(bf16[4,400,128]{2,1,0:T(8,128)(2,1)S(1)} %collective-permute-done.11.refs_1_.refs_2_) | copy-start | bytes 1228804
  48.1 11.8 %collective-permute-start.12 = (bf16[4,400,128]{2,1,0:T(8,128)(2,1)S(1)}, bf16[4,400,128]{2,1,0:T(8,128)(2,1)S(1)}, u32[]{:S(2)}, u32[]{:S(2)}) collective-permute-start(bf16[4,400,128]{2,1,0:T(8,128)(2,1)S(1)} %collective-permute-done.11.refs_1_.refs_2_), channel_id=1, source_target_pairs={{0,7},{1,0},{2,1},{3,2},{4,3},{5,4},{6,5},{7,6},{8,15},{9,8},{10,9... | collective-permute-start | bytes 1228808 | tf_op jit(solution)/shard_map/ppermute | solution.py:419
  51.1 13.4 %collective-permute-start.22 = (bf16[4,400,128]{2,1,0:T(8,128)(2,1)S(1)}, bf16[4,400,128]{2,1,0:T(8,128)(2,1)S(1)}, u32[]{:S(2)}, u32[]{:S(2)}) collective-permute-start(bf16[4,400,128]{2,1,0:T(8,128)(2,1)S(1)} %collective-permute-done.11.refs_1_.refs_2_), channel_id=1, source_target_pairs={{0,32},{32,0},{64,96},{96,64},{128,160},{160,128},{192,224},{224,1... | collective-permute-start | bytes 1228808 | tf_op jit(solution)/shard_map/ppermute | solution.py:422
  55.6 13.8 %collective-permute-start.9 = (bf16[4,400,128]{2,1,0:T(8,128)(2,1)S(1)}, bf16[4,400,128]{2,1,0:T(8,128)(2,1)S(1)}, u32[]{:S(2)}, u32[]{:S(2)}) collective-permute-start(bf16[4,400,128]{2,1,0:T(8,128)(2,1)S(1)} %collective-permute-done.8.refs_0_.refs_3_), channel_id=1, source_target_pairs={{0,1},{1,2},{2,3},{3,4},{4,5},{5,6},{6,7},{7,0},{8,9},{9,10},{10,1... | collective-permute-start | bytes 1228808 | tf_op jit(solution)/shard_map/ppermute | solution.py:419
  55.6 21.1 %collective-permute-start.19 = (bf16[4,400,128]{2,1,0:T(8,128)(2,1)S(1)}, bf16[4,400,128]{2,1,0:T(8,128)(2,1)S(1)}, u32[]{:S(2)}, u32[]{:S(2)}) collective-permute-start(bf16[4,400,128]{2,1,0:T(8,128)(2,1)S(1)} %collective-permute-done.8.refs_0_.refs_3_), channel_id=1, source_target_pairs={{0,32},{32,0},{64,96},{96,64},{128,160},{160,128},{192,224},{224,1... | collective-permute-start | bytes 1228808 | tf_op jit(solution)/shard_map/ppermute | solution.py:422
  59.9 11.3 %collective-permute-start.13 = (bf16[4,400,128]{2,1,0:T(8,128)(2,1)S(1)}, bf16[4,400,128]{2,1,0:T(8,128)(2,1)S(1)}, u32[]{:S(2)}, u32[]{:S(2)}) collective-permute-start(bf16[4,400,128]{2,1,0:T(8,128)(2,1)S(1)} %collective-permute-done.12.refs_1_.refs_4_), channel_id=1, source_target_pairs={{0,7},{1,0},{2,1},{3,2},{4,3},{5,4},{6,5},{7,6},{8,15},{9,8},{10,9... | collective-permute-start | bytes 1228808 | tf_op jit(solution)/shard_map/ppermute | solution.py:419
  63.3 13.5 %collective-permute-start.20 = (bf16[4,400,128]{2,1,0:T(8,128)(2,1)S(1)}, bf16[4,400,128]{2,1,0:T(8,128)(2,1)S(1)}, u32[]{:S(2)}, u32[]{:S(2)}) collective-permute-start(bf16[4,400,128]{2,1,0:T(8,128)(2,1)S(1)} %collective-permute-done.12.refs_1_.refs_4_), channel_id=1, source_target_pairs={{0,32},{32,0},{64,96},{96,64},{128,160},{160,128},{192,224},{224,1... | collective-permute-start | bytes 1228808 | tf_op jit(solution)/shard_map/ppermute | solution.py:422
  69.5 12.3 %collective-permute-start.10 = (bf16[2,400,128]{2,1,0:T(8,128)(2,1)S(1)}, bf16[2,400,128]{2,1,0:T(8,128)(2,1)S(1)}, u32[]{:S(2)}, u32[]{:S(2)}) collective-permute-start(bf16[2,400,128]{2,1,0:T(8,128)(2,1)S(1)} %slice.40), channel_id=1, source_target_pairs={{0,1},{1,2},{2,3},{3,4},{4,5},{5,6},{6,7},{7,0},{8,9},{9,10},{10,1... | collective-permute-start | bytes 614408 | tf_op jit(solution)/shard_map/ppermute | solution.py:419
  71.2 11.1 %collective-permute-start.14 = (bf16[2,400,128]{2,1,0:T(8,128)(2,1)S(1)}, bf16[2,400,128]{2,1,0:T(8,128)(2,1)S(1)}, u32[]{:S(2)}, u32[]{:S(2)}) collective-permute-start(bf16[2,400,128]{2,1,0:T(8,128)(2,1)S(1)} %slice.41), channel_id=1, source_target_pairs={{0,7},{1,0},{2,1},{3,2},{4,3},{5,4},{6,5},{7,6},{8,15},{9,8},{10,9... | collective-permute-start | bytes 614408 | tf_op jit(solution)/shard_map/ppermute | solution.py:419
  74.7 7.7 %collective-permute-start.17 = (bf16[4,400,128]{2,1,0:T(8,128)(2,1)S(1)}, bf16[4,400,128]{2,1,0:T(8,128)(2,1)S(1)}, u32[]{:S(2)}, u32[]{:S(2)}) collective-permute-start(bf16[4,400,128]{2,1,0:T(8,128)(2,1)S(1)} %collective-permute-done.9.refs_0_.refs_5_), channel_id=1, source_target_pairs={{0,32},{32,0},{64,96},{96,64},{128,160},{160,128},{192,224},{224,1... | collective-permute-start | bytes 1228808 | tf_op jit(solution)/shard_map/ppermute | solution.py:422
  76.8 5.6 %collective-permute-start.18 = (bf16[4,400,128]{2,1,0:T(8,128)(2,1)S(1)}, bf16[4,400,128]{2,1,0:T(8,128)(2,1)S(1)}, u32[]{:S(2)}, u32[]{:S(2)}) collective-permute-start(bf16[4,400,128]{2,1,0:T(8,128)(2,1)S(1)} %collective-permute-done.13.refs_1_.refs_6_), channel_id=1, source_target_pairs={{0,32},{32,0},{64,96},{96,64},{128,160},{160,128},{192,224},{224,1... | collective-permute-start | bytes 1228808 | tf_op jit(solution)/shard_map/ppermute | solution.py:422
  81.8 6.7 %collective-permute-start.15 = (bf16[2,400,128]{2,1,0:T(8,128)(2,1)S(1)}, bf16[2,400,128]{2,1,0:T(8,128)(2,1)S(1)}, u32[]{:S(2)}, u32[]{:S(2)}) collective-permute-start(bf16[2,400,128]{2,1,0:T(8,128)(2,1)S(1)} %collective-permute-done.10.refs_0_.refs_7_), channel_id=1, source_target_pairs={{0,32},{32,0},{64,96},{96,64},{128,160},{160,128},{192,224},{224,1... | collective-permute-start | bytes 614408 | tf_op jit(solution)/shard_map/ppermute | solution.py:422
  82.3 6.2 %collective-permute-start.16 = (bf16[2,400,128]{2,1,0:T(8,128)(2,1)S(1)}, bf16[2,400,128]{2,1,0:T(8,128)(2,1)S(1)}, u32[]{:S(2)}, u32[]{:S(2)}) collective-permute-start(bf16[2,400,128]{2,1,0:T(8,128)(2,1)S(1)} %collective-permute-done.14.refs_1_.refs_8_), channel_id=1, source_target_pairs={{0,32},{32,0},{64,96},{96,64},{128,160},{160,128},{192,224},{224,1... | collective-permute-start | bytes 614408 | tf_op jit(solution)/shard_map/ppermute | solution.py:422
  88.5 7.9 %copy-start = (bf16[4096,256]{1,0:T(8,128)(2,1)S(1)}, bf16[4096,256]{1,0:T(8,128)(2,1)}, u32[]{:S(2)}) copy-start(bf16[4096,256]{1,0:T(8,128)(2,1)} %refs_9_.1) | copy-start | bytes 6291460
  88.5 7.9 %copy-start.6 = (bf16[4,400,128]{2,1,0:T(8,128)(2,1)S(1)}, bf16[4,400,128]{2,1,0:T(8,128)(2,1)}, u32[]{:S(2)}) copy-start(bf16[4,400,128]{2,1,0:T(8,128)(2,1)} %copy-done.5) | copy-start | bytes 1228804
  94.9 24.3 %collective-permute-start.24 = (bf16[64,48,128]{2,1,0:T(8,128)(2,1)}, bf16[64,48,128]{2,1,0:T(8,128)(2,1)S(1)}, u32[]{:S(2)}, u32[]{:S(2)}) collective-permute-start(bf16[64,48,128]{2,1,0:T(8,128)(2,1)} %get-tuple-element.25), channel_id=1, source_target_pairs={{0,192},{32,224},{64,0},{96,32},{128,64},{160,96},{192,128},{224,1... | collective-permute-start | bytes 2359304 | tf_op jit(solution)/shard_map/ppermute | solution.py:422
  94.9 24.3 %collective-permute-start.25 = (bf16[64,48,128]{2,1,0:T(8,128)(2,1)}, bf16[64,48,128]{2,1,0:T(8,128)(2,1)S(1)}, u32[]{:S(2)}, u32[]{:S(2)}) collective-permute-start(bf16[64,48,128]{2,1,0:T(8,128)(2,1)} %get-tuple-element.26), channel_id=1, source_target_pairs={{0,128},{32,160},{64,192},{96,224},{128,0},{160,32},{192,64},{224,... | collective-permute-start | bytes 2359304 | tf_op jit(solution)/shard_map/ppermute | solution.py:422
  95.5 37.5 %collective-permute-start.26 = (bf16[64,48,128]{2,1,0:T(8,128)(2,1)}, bf16[64,48,128]{2,1,0:T(8,128)(2,1)S(1)}, u32[]{:S(2)}, u32[]{:S(2)}) collective-permute-start(bf16[64,48,128]{2,1,0:T(8,128)(2,1)} %get-tuple-element.27), channel_id=1, source_target_pairs={{0,64},{32,96},{64,128},{96,160},{128,192},{160,224},{192,0},{224,... | collective-permute-start | bytes 2359304 | tf_op jit(solution)/shard_map/ppermute | solution.py:422
  97.8 39.4 %copy-start.1 = (bf16[768,768]{1,0:T(8,128)(2,1)S(1)}, bf16[768,768]{1,0:T(8,128)(2,1)}, u32[]{:S(2)}) copy-start(bf16[768,768]{1,0:T(8,128)(2,1)} %param.19) | copy-start | bytes 3538948
  133.0 12.7 %collective-permute-start.27 = (f32[8,128]{1,0:T(8,128)}, f32[8,128]{1,0:T(8,128)S(1)}, u32[]{:S(2)}, u32[]{:S(2)}) collective-permute-start(f32[8,128]{1,0:T(8,128)} %hold.1), channel_id=1, source_target_pairs={{0,0},{64,32},{128,64},{192,96},{32,128},{96,160},{160,192},{224,2... | collective-permute-start | bytes 12296 | tf_op jit(solution)/shard_map/ppermute | solution.py:487
  (3 other events, 3.0 us)

commit v3 on v2

--- a/solution.py
+++ b/solution.py
@@ -16,7 +16,8 @@
 TAIL = 3 * 128
 BROWS = TAIL + 16
 EXP_SCALE = math.log2(math.e) / math.sqrt(HD)
-PARTS = ((0, 64), (64, 64), (128, 64), (192, 64))
+PARTS = ((64, 64), (128, 64), (192, 64))
+IMAGE_AT, COUNT_AT, TABLE_AT = 1, 33, 65
 F32 = jnp.float32
 BF16 = jnp.bfloat16
 
@@ -97,7 +98,7 @@
         in_specs=[pl.BlockSpec(memory_space=pltpu.SMEM)] + [hbm] * 6 + [vmem],
         out_specs=[vmem] * 5,
         scratch_shapes=[pltpu.VMEM(source.shape, source.dtype) for source in sources]
-        + [pltpu.SemaphoreType.DMA((6,))],
+        + [pltpu.SemaphoreType.DMA((7,))],
         compiler_params=pltpu.CompilerParams(vmem_limit_bytes=12 * 1024 * 1024),
         name="opening",
     )(group, *[in_hbm(source) for source in sources], candidates)
@@ -108,17 +109,18 @@
     pass
 
 
-def hold(values, after):
-    hbm = pl.BlockSpec(memory_space=pltpu.HBM)
+def hold(values, after, near=0):
+    anywhere, vmem = pl.BlockSpec(memory_space=pl.ANY), pl.BlockSpec(memory_space=pltpu.VMEM)
+    specs = [anywhere] * (len(values) - near) + [vmem] * near
     return pl.pallas_call(
         hold_kernel,
         out_shape=[jax.ShapeDtypeStruct(value.shape, value.dtype) for value in values],
-        in_specs=[hbm] * (len(values) + len(after)),
-        out_specs=[hbm] * len(values),
+        in_specs=specs + [anywhere] * len(after),
+        out_specs=specs,
         input_output_aliases={k: k for k in range(len(values))},
         compiler_params=pltpu.CompilerParams(vmem_limit_bytes=1024 * 1024),
         name="hold",
-    )(*[in_hbm(value) for value in values], *after)
+    )(*values, *after)
 
 
 def spread_kernel(q0, q1, q2, q3, query):
@@ -150,27 +152,32 @@
     )(*messages)
 
 
-def attend_kernel(sizes, unroll, fresh, final, core_ref, image_ref, count_ref, table_ref, query, *refs):
+def attend_kernel(sizes, first_image, unroll, fresh, final, plan_ref, query_ref, *refs):
     parts = len(sizes)
     own_refs, other_refs = refs[:parts], refs[parts : 2 * parts]
     refs = refs[2 * parts + (0 if fresh else 1) :]
-    context, token = refs[0:2]
-    outs = refs[2:6] if final else ()
-    held, column, tiles = refs[2 + len(outs) : 5 + len(outs)]
+    context = refs[0]
+    outs = refs[1:4] if final else ()
+    query, held, column, tiles, sems = refs[1 + len(outs) :]
     images = sum(sizes)
-    first_core = core_ref[0] == 0
+    core = plan_ref[0]
+    copies = [pltpu.make_async_copy(query_ref, query, sems.at[2 * parts])]
+    start = 0
+    for part, size in enumerate(sizes):
+        for k, (source, kind) in enumerate(((own_refs[part], core), (other_refs[part], 1 - core))):
+            target = held.at[kind, pl.ds(start, size)]
+            copies.append(pltpu.make_async_copy(source, target, sems.at[2 * part + k]))
+        start += size
+    for copy in copies:
+        copy.start()
     total = jnp.int32(0)
     for i in range(images):
         for t in range(3):
             tiles[total + t] = 4 * i + t
-        total = total + lax.shift_right_logical(count_ref[image_ref[i]] + 3, 2)
-    start = 0
-    for part, size in enumerate(sizes):
-        for k in range(size):
-            mine, theirs = own_refs[part][k], other_refs[part][k]
-            held[0, start + k] = jnp.where(first_core, mine, theirs)
-            held[1, start + k] = jnp.where(first_core, theirs, mine)
-        start += size
+        amount = plan_ref[COUNT_AT + plan_ref[IMAGE_AT + first_image + i]]
+        total = total + lax.shift_right_logical(amount + 3, 2)
+    for copy in copies:
+        copy.wait()
     for i in range(images):
         turned = held[1, i, TAIL:BROWS, :].astype(F32).T
         for h in range(3):
@@ -178,10 +185,10 @@
 
     def scores(code):
         i = lax.shift_right_logical(code, 2)
-        image = image_ref[i]
-        last = count_ref[image] - 1
+        image = plan_ref[IMAGE_AT + first_image + i]
+        last = plan_ref[COUNT_AT + image] - 1
         first = (code & 3) * 4
-        pairs = [table_ref[image * SLOTS + jnp.minimum(first + j, last)] for j in range(4)]
+        pairs = [plan_ref[TABLE_AT + image * SLOTS + jnp.minimum(first + j, last)] for j in range(4)]
         caps = [lax.shift_right_logical(p, 4) for p in pairs]
         found = []
         for h in range(3):
@@ -230,45 +237,51 @@
         return carry
 
     lax.fori_loop(0, lax.div(total + unroll - 1, unroll), group, 0)
-    token[...] = jnp.zeros_like(token)
     if final:
-        fetched([context.at[pl.ds(at, size)] for at, size in PARTS], outs, refs[-1])
-
-
-def attend(core, image_of, count, table, query, own, other, context, final):
+        fetched([context.at[pl.ds(at, size)] for at, size in PARTS], outs, sems)
+
+
+def attend(plan, first_image, query, own, other, context, final):
     sizes = tuple(part.shape[0] for part in own)
     images = sum(sizes)
     fresh = context is None
-    smem, vmem = pl.BlockSpec(memory_space=pltpu.SMEM), pl.BlockSpec(memory_space=pltpu.VMEM)
-    operands = [core, image_of, count, table, query, *own, *other] + ([] if fresh else [context])
+    vmem, anywhere = pl.BlockSpec(memory_space=pltpu.VMEM), pl.BlockSpec(memory_space=pl.ANY)
+    pieces = [*own, *[in_hbm(part) for part in other]]
+    operands = [in_hbm(plan), in_hbm(query), *pieces] + ([] if fresh else [context])
     parts = PARTS if final else ()
     outs = pl.pallas_call(
-        functools.partial(attend_kernel, sizes, 5, fresh, final),
-        out_shape=[jax.ShapeDtypeStruct((256, 48, 128), BF16), jax.ShapeDtypeStruct((8, 128), F32)]
+        functools.partial(attend_kernel, sizes, first_image, 5, fresh, final),
+        out_shape=[jax.ShapeDtypeStruct((256, 48, 128), BF16)]
         + [jax.ShapeDtypeStruct((size, 48, 128), BF16) for _, size in parts],
-        in_specs=[smem] * 4 + [vmem] * (len(operands) - 4),
-        out_specs=[vmem, vmem] + [pl.BlockSpec(memory_space=pltpu.HBM)] * len(parts),
+        in_specs=[pl.BlockSpec(memory_space=pltpu.SMEM)]
+        + [anywhere] * (1 + len(pieces))
+        + ([] if fresh else [vmem]),
+        out_specs=[vmem] + [pl.BlockSpec(memory_space=pltpu.HBM)] * len(parts),
         input_output_aliases={} if fresh else {len(operands) - 1: 0},
         scratch_shapes=[
+            pltpu.VMEM(query.shape, BF16),
             pltpu.VMEM((2, images, BROWS, 128), BF16),
             pltpu.VMEM((images, 3, HD, 128), F32),
             pltpu.SMEM((images * 3 + 4,), jnp.int32),
-        ]
-        + ([pltpu.SemaphoreType.DMA((4,))] if final else []),
+            pltpu.SemaphoreType.DMA((7,)),
+        ],
         cost_estimate=pl.CostEstimate(
             flops=images * 600_000_000, bytes_accessed=images * 800_000, transcendentals=images * 800_000
         ),
         compiler_params=pltpu.CompilerParams(vmem_limit_bytes=14 * 1024 * 1024),
         name="attend",
     )(*operands)
-    return outs[0], outs[1], outs[2:]
+    return outs[0], outs[1:]
 
 
 def score_kernel(shard_ref, *refs):
-    count = len(refs) - 6
-    pieces, gallery, out_ref = refs[:count], refs[count], refs[count + 1]
-    tails, rows, scores, sems = refs[count + 2 :]
-    copies = [pltpu.make_async_copy(gallery, rows, sems.at[count])]
+    count = len(refs) - 10
+    pieces, gallery, context = refs[:count], refs[count], refs[count + 1]
+    out_ref, kept, tails, rows, scores, sems = refs[count + 4 :]
+    copies = [
+        pltpu.make_async_copy(gallery, rows, sems.at[count]),
+        pltpu.make_async_copy(context.at[pl.ds(0, 64)], kept, sems.at[count + 1]),
+    ]
     start = 0
     for k, piece in enumerate(pieces):
         images = piece.shape[0]
@@ -312,43 +325,44 @@
     out_ref[1:2, :] = jnp.sum(total, axis=0, keepdims=True)
 
 
-def score(shard, pieces, gallery):
-    hbm = pl.BlockSpec(memory_space=pltpu.HBM)
+def score(shard, pieces, gallery, context, ready):
+    hbm, vmem, anywhere = (pl.BlockSpec(memory_space=space) for space in (pltpu.HBM, pltpu.VMEM, pl.ANY))
     return pl.pallas_call(
         score_kernel,
-        out_shape=jax.ShapeDtypeStruct((2, 128), F32),
-        in_specs=[pl.BlockSpec(memory_space=pltpu.SMEM)] + [hbm] * (len(pieces) + 1),
-        out_specs=pl.BlockSpec(memory_space=pltpu.VMEM),
+        out_shape=[jax.ShapeDtypeStruct((2, 128), F32), jax.ShapeDtypeStruct((64, 48, 128), BF16)],
+        in_specs=[pl.BlockSpec(memory_space=pltpu.SMEM)] + [anywhere] * (len(pieces) + 1) + [vmem] + [anywhere] * len(ready),
+        out_specs=[vmem, hbm],
         scratch_shapes=[
             pltpu.VMEM((32, 16, 128), BF16),
             pltpu.VMEM(gallery.shape, BF16),
             pltpu.VMEM((16, BLK, 128), F32),
-            pltpu.SemaphoreType.DMA((len(pieces) + 1,)),
+            pltpu.SemaphoreType.DMA((len(pieces) + 2,)),
         ],
         cost_estimate=pl.CostEstimate(flops=1000, bytes_accessed=1000, transcendentals=0),
         compiler_params=pltpu.CompilerParams(vmem_limit_bytes=12 * 1024 * 1024),
         name="score",
-    )(shard, *pieces, gallery)
-
-
-def finish_kernel(x_ref, c0, c1, c2, c3, weight_ref, states_ref, gain_ref, bias_ref, out_ref, main, low, high):
+    )(shard, *pieces, gallery, context, *ready)
+
+
+def finish_kernel(x_ref, c0, c1, c2, c3, weight_ref, states_ref, gain_ref, bias_ref, out_ref, main, third):
     @pl.when(pl.program_id(0) == 0)
     def _():
-        low[...] = jnp.zeros_like(low)
-        high[...] = jnp.zeros_like(high)
         for d in range(4):
             source = lax.rem(x_ref[0] + d, 4)
             main[d * 128 : (d + 1) * 128] = weight_ref[source, 0:128]
-            low[d * 128 : d * 128 + 64] = weight_ref[source, 128:192]
-            high[d * 128 + 64 : d * 128 + 128] = weight_ref[source, 128:192]
+            third[d * 64 : (d + 1) * 64] = weight_ref[source, 128:192]
 
     parts = (c0, c1, c2, c3)
     count = c0.shape[0]
     first = jnp.concatenate([part[:, 0:32, :].reshape(count * 32, 128) for part in parts], axis=1)
-    second = jnp.concatenate([part[:, 32:48, :].reshape(count * 16, 128) for part in parts], axis=1)
+    second = [part[:, 32:48, :].reshape(count * 16, 128) for part in parts]
+    left = lax.broadcasted_iota(jnp.int32, second[0].shape, 1) < HD
+    pairs = ((second[0], second[1]), (second[2], second[3]))
+    lows = [jnp.where(left, one, jnp.concatenate([two[:, HD:], two[:, :HD]], axis=1)) for one, two in pairs]
+    highs = [jnp.where(left, jnp.concatenate([one[:, HD:], one[:, :HD]], axis=1), two) for one, two in pairs]
     mixed = jnp.dot(first, main[...], preferred_element_type=F32).reshape(count, 2, 16, 768)
-    early = jnp.dot(second, low[...], preferred_element_type=F32).reshape(count, 16, 768)
-    late = jnp.dot(second, high[...], preferred_element_type=F32).reshape(count, 16, 768)
+    early = jnp.dot(jnp.concatenate(lows, axis=1), third[...], preferred_element_type=F32).reshape(count, 16, 768)
+    late = jnp.dot(jnp.concatenate(highs, axis=1), third[...], preferred_element_type=F32).reshape(count, 16, 768)
     states = states_ref[0].astype(F32)
     gain = gain_ref[...]
     bias = bias_ref[...]
@@ -379,11 +393,11 @@
                 pl.BlockSpec((1, 768), lambda s, *_: (0, 0)),
             ],
             out_specs=pl.BlockSpec((1, 16, NQ, 768), lambda s, *_: (s, 0, 0, 0)),
-            scratch_shapes=[pltpu.VMEM((512, 768), BF16)] * 3,
+            scratch_shapes=[pltpu.VMEM((512, 768), BF16), pltpu.VMEM((256, 768), BF16)],
         ),
         compiler_params=pltpu.CompilerParams(vmem_limit_bytes=32 * 1024 * 1024),
         name="finish",
-    )(x, *contexts, output_weight.reshape(4, 192, 768), query_states, gain.reshape(1, 768), bias.reshape(1, 768))
+    )(x, *[in_hbm(part) for part in (*contexts, output_weight.reshape(4, 192, 768), query_states, gain, bias)])
 
 
 def grid_moves(dy, dz):
@@ -430,6 +444,7 @@
         return lax.ppermute(block, ("group", "shard"), moves)
 
     arrived = [homeward(dy) for dy in range(4)]
+    messages = hold(messages, arrived[:2])
     received = [messages[0]] + [along_group(messages[4 - d], 4 - d) for d in (1, 2, 3)]
     stack = jnp.stack(arrived)
     pair_images = jnp.stack([part[128:144, :4].T for part in received]).reshape(256).astype(jnp.int32)
@@ -450,32 +465,39 @@
         return [((my_y - dy) % 4) * 8 + (my_z - z_shift) % 8 for dy in y_shifts]
 
     whole = (0, 1, 2, 3)
-    piece_images = [images(whole, 0)]
-    piece_images += [images(whole, k) + images(whole, -k) for k in (1, 2, 3)]
-    piece_images += [images((0, 1), 4) + images((2, 3), -4)]
-    piece_images = [jnp.stack(part).astype(jnp.int32) for part in piece_images]
-    image_of = jnp.concatenate(piece_images)
+    arrivals = images(whole, 0)
+    for k in (1, 2, 3):
+        arrivals += images(whole, k) + images(whole, -k)
+    arrivals += images((0, 1), 4) + images((2, 3), -4)
+    image_of = jnp.stack(arrivals).astype(jnp.int32)
+    plan = jnp.concatenate([core.reshape(1).astype(jnp.int32), image_of, count, table, jnp.zeros((63,), jnp.int32)])
 
     pieces = [[stack]]
-    context = None
+    waiting = []
+    context, first_image = None, 0
     right = left = stack
     for step in range(5):
         if step < 3:
             coming = [along_shard(right, 0, 1), along_shard(left, 0, -1)]
         elif step == 3:
             coming = [along_shard(right[:2], 0, 1), along_shard(left[2:], 0, -1)]
-        own = pieces[-1]
-        other = [along_group(part, 0, 1) for part in own]
-        context, token, outs = attend(
-            core.reshape(1), piece_images[step], count, table, query, own, other, context, step == 4
-        )
+        waiting += pieces[-1]
+        if step > 0:
+            other = [along_group(part, 0, 1) for part in waiting]
+            context, outs = attend(plan, first_image, query, waiting, other, context, step == 4)
+            first_image += sum(part.shape[0] for part in waiting)
+            waiting = []
         if step < 4:
             right, left = coming
+            if step > 0:
+                right, left, context = hold([*coming, context], [], 1)
             pieces.append([right, left])
 
-    sent = [outs[0]] + [along_group(outs[4 - d], 4 - d) for d in (1, 2, 3)]
-
-    partial = score(shard_index.reshape(1), [part for own in pieces for part in own], gallery_embed)
+    sent = [along_group(outs[3 - d], 4 - d) for d in (1, 2, 3)]
+
+    gain, bias = norm_gain.reshape(1, 768), norm_bias.reshape(1, 768)
+    own_parts = [part for own in pieces for part in own]
+    partial, kept = score(shard_index.reshape(1), own_parts, gallery_embed, context, [gain, bias])
     order = jnp.arange(32, dtype=jnp.int32)
     pick = image_of[None, :] == order[:, None]
     partial = partial.reshape(2, 32, 4)
@@ -483,10 +505,10 @@
     partial = lax.all_to_all(partial, "shard", split_axis=0, concat_axis=0, tiled=True)
     top = jnp.max(partial[:, 0], axis=0)
     normalizer = top + jnp.log(jnp.sum(partial[:, 1] * jnp.exp(partial[:, 0] - top[None]), axis=0))
-    normalizer = hold([jnp.pad(normalizer.reshape(1, 4), ((0, 7), (0, 124)))], sent[1:])[0]
+    normalizer = hold([jnp.pad(normalizer.reshape(1, 4), ((0, 7), (0, 124)))], sent)[0]
     normalizer = lax.ppermute(normalizer, "group", [(h, g) for g, h in homes])[0, :4]
 
-    layer_out = finish(x.reshape(1), sent, output_weight, query_states, norm_gain, norm_bias)
+    layer_out = finish(x.reshape(1), [kept, *sent], output_weight, query_states, gain, bias)
     return (layer_out, normalizer)
 
 

time: 147 us -> 140 us (0.952)
  waiting for transfers between devices: 36.2 us -> 27.4 us
  Pallas kernels: 36.6 us -> 42.3 us
  starting transfers between devices: 43.9 us -> 39.4 us
  blocking collectives: 13.7 us -> 17.1 us
  local copies, waits for them, and re-layouts: 11.4 us -> 9.86 us
    ppermute x8, waiting for transfers between devices: 8.07 us -> 1.28 us  [along_shard(): return lax.ppermute(value, 'shard', grid_moves(dy, dz))]
    ppermute x15, waiting for transfers between devices: 28.1 us -> 22.2 us  [along_group(): return lax.ppermute(value, 'group', group_moves(dx, flip))]
    pallas_call x6 -> x5, Pallas kernels: 27 us -> 31 us  [the longest x4 28.9 us: attend(): pl.pallas_call(functools.partial(attend_kernel, sizes, first_image, 5, fr...]
    ppermute x4, waiting for transfers between devices: 0.01 us -> 3.98 us  [homeward(): return lax.ppermute(block, ('group', 'shard'), moves)]
    all_to_all x1, blocking collectives: 13.7 us -> 17.1 us  [on_device(): lax.all_to_all(partial, 'shard', split_axis=0, concat_axis=0, tiled=True)]
    unnamed x15 -> x47, local copies, waits for them, and re-layouts: 3.74 us -> 6.42 us
    ppermute x15, starting transfers between devices: 13.4 us -> 10.7 us  [along_group(): return lax.ppermute(value, 'group', group_moves(dx, flip))]
    ppermute x8, starting transfers between devices: 15.7 us -> 13.8 us  [along_shard(): return lax.ppermute(value, 'shard', grid_moves(dy, dz))]
  transfers between devices with their start and end apart: 28 -> 28, of which waited for: 7 -> 10; matrix products, arithmetic and copies ran while one was open for 7% -> 4% of each run, Pallas kernels for 19% -> 23%
where the time goes in v3:
time: 140 us; the launch traced here: 139 us
  Pallas kernels  42.3 us (30%)
  starting transfers between devices  39.4 us (28%)
  waiting for transfers between devices  27.4 us (20%)
  blocking collectives  17.1 us (12%)
  local copies, waits for them, and re-layouts  9.86 us (7%)
  other arithmetic  2.17 us (2%)
    pallas_call x4, Pallas kernels, attend(): pl.pallas_call(functools.partial(attend_kernel, sizes, first_image, 5, fr...  28.9 us
    ppermute x15, waiting for transfers between devices, along_group(): return lax.ppermute(value, 'group', group_moves(dx, flip))  22.2 us
    all_to_all x1, blocking collectives, on_device(): lax.all_to_all(partial, 'shard', split_axis=0, concat_axis=0, tiled=True)  17.1 us
    ppermute x8, starting transfers between devices, along_shard(): return lax.ppermute(value, 'shard', grid_moves(dy, dz))  13.8 us
    ppermute x4, starting transfers between devices, homeward(): return lax.ppermute(block, ('group', 'shard'), moves)  11.9 us
    ppermute x15, starting transfers between devices, along_group(): return lax.ppermute(value, 'group', group_moves(dx, flip))  10.7 us
    pallas_call x1, Pallas kernels, finish(): pl.pallas_call(finish_kernel, out_shape=jax.ShapeDtypeStruct((4, 16, NQ,...  7.91 us
    unnamed x47, local copies, waits for them, and re-layouts  6.42 us
  transfers between devices with their start and end apart: 28, of which 10 were waited for; matrix products, arithmetic and copies ran while one was open for 4% of the time, Pallas kernels for 23%

profile of v3, /device:TPU:1, one launch (start us, length us, event | category | flops | bytes accessed | tf_op | source)
XLA Modules:
  0.0 139.3 jit_solution(738906056691275708)
XLA Ops:
  1.4 3.2 %opening.1 = (bf16[400,128]{1,0:T(8,128)(2,1)S(1)}, bf16[144,256]{1,0:T(8,128)(2,1)S(1)}, bf16[144,256]{1,0:T(8,128)(2,1)S(1)}, bf16[144,256]{1,0:T(8,128)(2,1)S(1)}, bf16[144,256]{1,0:T(8,128)(2,1)S(1)}) custom-call(s32[1]{0:T(128)} %bitcast.2.group_ref, bf16[1,257,1408]{2,1,0:T(8,128)(2,1)} %refs_0_.1, bf16[192,1408]{1,0:T(8,128)(2,1)} %bitcast.71, ...), custom_call_target="tpu_custom_call" | custom-call | tf_op jit(solution)/shard_map/opening/pallas_call | solution.py:94
  4.6 4.5 %collective-permute-start = (bf16[400,128]{1,0:T(8,128)(2,1)S(1)}, bf16[400,128]{1,0:T(8,128)(2,1)S(1)}, u32[]{:S(2)}, u32[]{:S(2)}) collective-permute-start(bf16[400,128]{1,0:T(8,128)(2,1)S(1)} %get-tuple-element.26), channel_id=1, source_target_pairs={{0,0},{1,1},{2,2},{3,3},{4,4},{5,5},{6,6},{7,7},{8,8},{9,9},{10,10... | collective-permute-start | bytes 307208 | tf_op jit(solution)/shard_map/ppermute | solution.py:444
  9.1 2.6 %collective-permute-start.1 = (bf16[400,128]{1,0:T(8,128)(2,1)S(1)}, bf16[400,128]{1,0:T(8,128)(2,1)S(1)}, u32[]{:S(2)}, u32[]{:S(2)}) collective-permute-start(bf16[400,128]{1,0:T(8,128)(2,1)S(1)} %get-tuple-element.26), channel_id=1, source_target_pairs={{0,8},{1,9},{2,10},{3,11},{4,12},{5,13},{6,14},{7,15},{8,16},{9,17... | collective-permute-start | bytes 307208 | tf_op jit(solution)/shard_map/ppermute | solution.py:444
  11.7 2.3 %collective-permute-start.2 = (bf16[400,128]{1,0:T(8,128)(2,1)S(1)}, bf16[400,128]{1,0:T(8,128)(2,1)S(1)}, u32[]{:S(2)}, u32[]{:S(2)}) collective-permute-start(bf16[400,128]{1,0:T(8,128)(2,1)S(1)} %get-tuple-element.26), channel_id=1, source_target_pairs={{0,16},{1,17},{2,18},{3,19},{4,20},{5,21},{6,22},{7,23},{8,24},{9,... | collective-permute-start | bytes 307208 | tf_op jit(solution)/shard_map/ppermute | solution.py:444
  14.0 2.5 %collective-permute-start.3 = (bf16[400,128]{1,0:T(8,128)(2,1)S(1)}, bf16[400,128]{1,0:T(8,128)(2,1)S(1)}, u32[]{:S(2)}, u32[]{:S(2)}) collective-permute-start(bf16[400,128]{1,0:T(8,128)(2,1)S(1)} %get-tuple-element.26), channel_id=1, source_target_pairs={{0,24},{1,25},{2,26},{3,27},{4,28},{5,29},{6,30},{7,31},{8,0},{9,1... | collective-permute-start | bytes 307208 | tf_op jit(solution)/shard_map/ppermute | solution.py:444
  16.9 2.8 %collective-permute-done.2 = bf16[400,128]{1,0:T(8,128)(2,1)S(1)} collective-permute-done((bf16[400,128]{1,0:T(8,128)(2,1)S(1)}, bf16[400,128]{1,0:T(8,128)(2,1)S(1)}, u32[]{:S(2)}, u32[]{:S(2)}) %collective-permute-start.2) | collective-permute-done | bytes 102432 | tf_op jit(solution)/shard_map/ppermute | solution.py:444
  20.6 1.7 %collective-permute-start.4 = (bf16[4,400,128]{2,1,0:T(8,128)(2,1)S(1)}, bf16[4,400,128]{2,1,0:T(8,128)(2,1)}, u32[]{:S(2)}, u32[]{:S(2)}) collective-permute-start(bf16[4,400,128]{2,1,0:T(8,128)(2,1)S(1)} %pad_maximum_fusion.refs_0_), channel_id=1, source_target_pairs={{0,1},{1,2},{2,3},{3,4},{4,5},{5,6},{6,7},{7,0},{8,9},{9,10},{10,1... | collective-permute-start | bytes 1228808 | tf_op jit(solution)/shard_map/ppermute | solution.py:433
  22.3 4.0 %collective-permute-start.5 = (bf16[4,400,128]{2,1,0:T(8,128)(2,1)S(1)}, bf16[4,400,128]{2,1,0:T(8,128)(2,1)}, u32[]{:S(2)}, u32[]{:S(2)}) collective-permute-start(bf16[4,400,128]{2,1,0:T(8,128)(2,1)S(1)} %pad_maximum_fusion.refs_0_), channel_id=1, source_target_pairs={{0,7},{1,0},{2,1},{3,2},{4,3},{5,4},{6,5},{7,6},{8,15},{9,8},{10,9... | collective-permute-start | bytes 1228808 | tf_op jit(solution)/shard_map/ppermute | solution.py:433
  26.3 3.1 %collective-permute-start.8 = (bf16[144,256]{1,0:T(8,128)(2,1)S(1)}, bf16[144,256]{1,0:T(8,128)(2,1)S(1)}, u32[]{:S(2)}, u32[]{:S(2)}) collective-permute-start(bf16[144,256]{1,0:T(8,128)(2,1)S(1)} %get-tuple-element.32), channel_id=1, source_target_pairs={{0,192},{32,224},{64,0},{96,32},{128,64},{160,96},{192,128},{224,1... | collective-permute-start | bytes 221192 | tf_op jit(solution)/shard_map/ppermute | solution.py:436
  29.5 3.0 %collective-permute-done.8.q1 = bf16[144,256]{1,0:T(8,128)(2,1)S(1)} collective-permute-done((bf16[144,256]{1,0:T(8,128)(2,1)S(1)}, bf16[144,256]{1,0:T(8,128)(2,1)S(1)}, u32[]{:S(2)}, u32[]{:S(2)}) %collective-permute-start.8) | collective-permute-done | bytes 73760 | tf_op jit(solution)/shard_map/ppermute | solution.py:436
  32.6 1.9 %collective-permute-done.9.q2 = bf16[144,256]{1,0:T(8,128)(2,1)S(1)} collective-permute-done((bf16[144,256]{1,0:T(8,128)(2,1)S(1)}, bf16[144,256]{1,0:T(8,128)(2,1)S(1)}, u32[]{:S(2)}, u32[]{:S(2)}) %collective-permute-start.9) | collective-permute-done | bytes 73760 | tf_op jit(solution)/shard_map/ppermute | solution.py:436
  34.7 3.2 %collective-permute-done.10.q3 = bf16[144,256]{1,0:T(8,128)(2,1)S(1)} collective-permute-done((bf16[144,256]{1,0:T(8,128)(2,1)S(1)}, bf16[144,256]{1,0:T(8,128)(2,1)S(1)}, u32[]{:S(2)}, u32[]{:S(2)}) %collective-permute-start.10) | collective-permute-done | bytes 73760 | tf_op jit(solution)/shard_map/ppermute | solution.py:436
  38.3 1.7 %collective-permute-start.12 = (bf16[4,400,128]{2,1,0:T(8,128)(2,1)}, bf16[4,400,128]{2,1,0:T(8,128)(2,1)S(1)}, u32[]{:S(2)}, u32[]{:S(2)}) collective-permute-start(bf16[4,400,128]{2,1,0:T(8,128)(2,1)} %collective-permute-done.4.refs_1_), channel_id=1, source_target_pairs={{0,32},{32,0},{64,96},{96,64},{128,160},{160,128},{192,224},{224,1... | collective-permute-start | bytes 1228808 | tf_op jit(solution)/shard_map/ppermute | solution.py:436
  42.1 2.7 %collective-permute-start.7 = (bf16[4,400,128]{2,1,0:T(8,128)(2,1)}, bf16[4,400,128]{2,1,0:T(8,128)(2,1)S(1)}, u32[]{:S(2)}, u32[]{:S(2)}) collective-permute-start(bf16[4,400,128]{2,1,0:T(8,128)(2,1)} %collective-permute-done.5.refs_2_), channel_id=1, source_target_pairs={{0,7},{1,0},{2,1},{3,2},{4,3},{5,4},{6,5},{7,6},{8,15},{9,8},{10,9... | collective-permute-start | bytes 1228808 | tf_op jit(solution)/shard_map/ppermute | solution.py:433
  46.3 8.6 %attend.4.refs_2_ = bf16[256,48,128]{2,1,0:T(8,128)(2,1)S(1)} custom-call(s32[512]{0:T(512)} %concatenate.4.plan_ref, bf16[3,2,16,32,128]{4,3,2,1,0:T(8,128)(2,1)} %copy-done.10, bf16[4,400,128]{2,1,0:T(8,128)(2,1)S(1)} %pad_maximum_fusion.refs_0_, bf16[4,400,128]{2,1,0:T(8,128)(2,1)} %collective-permute-done.4.refs_1_, ...), custom_call_target="tpu_custom_call" | custom-call | flops 7200000000 | bytes 9600000 | tf_op jit(solution)/shard_map/attend/pallas_call | solution.py:252
  55.0 1.1 collective-permute-start.16
  56.1 2.7 %collective-permute-start.15 = (bf16[4,400,128]{2,1,0:T(8,128)(2,1)S(1)}, bf16[4,400,128]{2,1,0:T(8,128)(2,1)S(1)}, u32[]{:S(2)}, u32[]{:S(2)}) collective-permute-start(bf16[4,400,128]{2,1,0:T(8,128)(2,1)S(1)} %get-tuple-element.36.refs_1_.refs_4_), channel_id=1, source_target_pairs={{0,7},{1,0},{2,1},{3,2},{4,3},{5,4},{6,5},{7,6},{8,15},{9,8},{10,9... | collective-permute-start | bytes 1228808 | tf_op jit(solution)/shard_map/ppermute | solution.py:433
  59.7 7.0 %attend.5.refs_2_ = bf16[256,48,128]{2,1,0:T(8,128)(2,1)S(1)} custom-call(s32[512]{0:T(512)} %concatenate.4.plan_ref, bf16[3,2,16,32,128]{4,3,2,1,0:T(8,128)(2,1)} %copy-done.10, bf16[4,400,128]{2,1,0:T(8,128)(2,1)S(1)} %get-tuple-element.35.refs_0_.refs_3_, ...), custom_call_target="tpu_custom_call", output_to_operand_aliasing={{}: (6, {})} | custom-call | flops 4800000000 | bytes 6400000 | tf_op jit(solution)/shard_map/attend/pallas_call | solution.py:252
  66.7 1.3 collective-permute-done.14.refs_0_
  68.0 1.2 collective-permute-start.20
  69.4 1.8 %collective-permute-start.18 = (bf16[2,400,128]{2,1,0:T(8,128)(2,1)S(1)}, bf16[2,400,128]{2,1,0:T(8,128)(2,1)}, u32[]{:S(2)}, u32[]{:S(2)}) collective-permute-start(bf16[2,400,128]{2,1,0:T(8,128)(2,1)S(1)} %slice.32), channel_id=1, source_target_pairs={{0,1},{1,2},{2,3},{3,4},{4,5},{5,6},{6,7},{7,0},{8,9},{9,10},{10,1... | collective-permute-start | bytes 614408 | tf_op jit(solution)/shard_map/ppermute | solution.py:433
  71.1 1.0 collective-permute-start.19
  73.0 7.0 %attend.6.refs_2_ = bf16[256,48,128]{2,1,0:T(8,128)(2,1)S(1)} custom-call(s32[512]{0:T(512)} %concatenate.4.plan_ref, bf16[3,2,16,32,128]{4,3,2,1,0:T(8,128)(2,1)} %copy-done.10, bf16[4,400,128]{2,1,0:T(8,128)(2,1)S(1)} %get-tuple-element.38.refs_0_.refs_5_, ...), custom_call_target="tpu_custom_call", output_to_operand_aliasing={{}: (6, {})} | custom-call | flops 4800000000 | bytes 6400000 | tf_op jit(solution)/shard_map/attend/pallas_call | solution.py:252
  82.3 6.4 %attend.7 = (bf16[256,48,128]{2,1,0:T(8,128)(2,1)S(1)}, bf16[64,48,128]{2,1,0:T(8,128)(2,1)}, bf16[64,48,128]{2,1,0:T(8,128)(2,1)}, bf16[64,48,128]{2,1,0:T(8,128)(2,1)}) custom-call(s32[512]{0:T(512)} %concatenate.4.plan_ref, bf16[3,2,16,32,128]{4,3,2,1,0:T(8,128)(2,1)} %copy-done.10, ...), custom_call_target="tpu_custom_call", output_to_operand_aliasing={{0}: (6, {})} | custom-call | flops 2400000000 | bytes 3200000 | tf_op jit(solution)/shard_map/attend/pallas_call | solution.py:252
  88.6 1.8 %collective-permute-start.24 = (bf16[64,48,128]{2,1,0:T(8,128)(2,1)}, bf16[64,48,128]{2,1,0:T(8,128)(2,1)}, u32[]{:S(2)}, u32[]{:S(2)}) collective-permute-start(bf16[64,48,128]{2,1,0:T(8,128)(2,1)} %get-tuple-element.46), channel_id=1, source_target_pairs={{0,192},{32,224},{64,0},{96,32},{128,64},{160,96},{192,128},{224,1... | collective-permute-start | bytes 2359304 | tf_op jit(solution)/shard_map/ppermute | solution.py:436
  90.5 0.9 collective-permute-start.26
  92.1 2.2 %score.1 = (f32[2,128]{1,0:T(2,128)S(1)}, bf16[64,48,128]{2,1,0:T(8,128)(2,1)S(1)}) custom-call(s32[1]{0:T(128)} %bitcast.1.shard_ref, bf16[4,400,128]{2,1,0:T(8,128)(2,1)S(1)} %copy-done.4, bf16[4,400,128]{2,1,0:T(8,128)(2,1)} %collective-permute-done.4.refs_1_, bf16[4,400,128]{2,1,0:T(8,128)(2,1)} %collective-permute-done.5.refs_2_, ...), custom_call_target="tpu_custom_call" | custom-call | flops 1000 | bytes 1000 | tf_op jit(solution)/shard_map/score/pallas_call | solution.py:330
  94.3 0.9 copy-done.9
  97.4 17.1 %all_to_all.5 = f32[32,2,4]{2,1,0:T(2,128)S(1)} all-to-all(f32[32,2,4]{2,1,0:T(2,128)S(1)} %copy.53), channel_id=1, replica_groups=mesh['group'=8,'shard'=32] {'shard'}, dimensions={0} | all-to-all | bytes 2048 | tf_op jit(solution)/shard_map/all_to_all | solution.py:505
  115.0 13.1 %collective-permute-done.26.c3.refs_3_ = bf16[64,48,128]{2,1,0:T(8,128)(2,1)} collective-permute-done((bf16[64,48,128]{2,1,0:T(8,128)(2,1)}, bf16[64,48,128]{2,1,0:T(8,128)(2,1)}, u32[]{:S(2)}, u32[]{:S(2)}) %collective-permute-start.26) | collective-permute-done | bytes 786464 | tf_op jit(solution)/shard_map/ppermute | solution.py:436
  128.0 2.8 %collective-permute-start.27 = (f32[8,128]{1,0:T(8,128)S(1)}, f32[8,128]{1,0:T(8,128)S(1)}, u32[]{:S(2)}, u32[]{:S(2)}) collective-permute-start(f32[8,128]{1,0:T(8,128)S(1)} %hold.9), channel_id=1, source_target_pairs={{0,0},{64,32},{128,64},{192,96},{32,128},{96,160},{160,192},{224,2... | collective-permute-start | bytes 12296 | tf_op jit(solution)/shard_map/ppermute | solution.py:509
  130.9 7.9 %finish.1 = bf16[4,16,32,768]{3,2,1,0:T(8,128)(2,1)} custom-call(s32[1]{0:T(128)} %bitcast.x_ref, bf16[64,48,128]{2,1,0:T(8,128)(2,1)} %copy-done.9, bf16[64,48,128]{2,1,0:T(8,128)(2,1)} %collective-permute-done.24.c1.refs_1_, bf16[64,48,128]{2,1,0:T(8,128)(2,1)} %collective-permute-done.25.c2.refs_2_, ...), custom_call_target="tpu_custom_call" | custom-call | tf_op jit(solution)/shard_map/finish/pallas_call | solution.py:382
  (119 shorter events, 14.3 us)
Async XLA Ops:
  4.6 11.9 %collective-permute-start = (bf16[400,128]{1,0:T(8,128)(2,1)S(1)}, bf16[400,128]{1,0:T(8,128)(2,1)S(1)}, u32[]{:S(2)}, u32[]{:S(2)}) collective-permute-start(bf16[400,128]{1,0:T(8,128)(2,1)S(1)} %get-tuple-element.26), channel_id=1, source_target_pairs={{0,0},{1,1},{2,2},{3,3},{4,4},{5,5},{6,6},{7,7},{8,8},{9,9},{10,10... | collective-permute-start | bytes 307208 | tf_op jit(solution)/shard_map/ppermute | solution.py:444
  9.1 7.8 %collective-permute-start.1 = (bf16[400,128]{1,0:T(8,128)(2,1)S(1)}, bf16[400,128]{1,0:T(8,128)(2,1)S(1)}, u32[]{:S(2)}, u32[]{:S(2)}) collective-permute-start(bf16[400,128]{1,0:T(8,128)(2,1)S(1)} %get-tuple-element.26), channel_id=1, source_target_pairs={{0,8},{1,9},{2,10},{3,11},{4,12},{5,13},{6,14},{7,15},{8,16},{9,17... | collective-permute-start | bytes 307208 | tf_op jit(solution)/shard_map/ppermute | solution.py:444
  11.7 8.0 %collective-permute-start.2 = (bf16[400,128]{1,0:T(8,128)(2,1)S(1)}, bf16[400,128]{1,0:T(8,128)(2,1)S(1)}, u32[]{:S(2)}, u32[]{:S(2)}) collective-permute-start(bf16[400,128]{1,0:T(8,128)(2,1)S(1)} %get-tuple-element.26), channel_id=1, source_target_pairs={{0,16},{1,17},{2,18},{3,19},{4,20},{5,21},{6,22},{7,23},{8,24},{9,... | collective-permute-start | bytes 307208 | tf_op jit(solution)/shard_map/ppermute | solution.py:444
  14.0 6.5 %collective-permute-start.3 = (bf16[400,128]{1,0:T(8,128)(2,1)S(1)}, bf16[400,128]{1,0:T(8,128)(2,1)S(1)}, u32[]{:S(2)}, u32[]{:S(2)}) collective-permute-start(bf16[400,128]{1,0:T(8,128)(2,1)S(1)} %get-tuple-element.26), channel_id=1, source_target_pairs={{0,24},{1,25},{2,26},{3,27},{4,28},{5,29},{6,30},{7,31},{8,0},{9,1... | collective-permute-start | bytes 307208 | tf_op jit(solution)/shard_map/ppermute | solution.py:444
  20.6 34.3 %copy-start.3 = (bf16[4,400,128]{2,1,0:T(8,128)(2,1)}, bf16[4,400,128]{2,1,0:T(8,128)(2,1)S(1)}, u32[]{:S(2)}) copy-start(bf16[4,400,128]{2,1,0:T(8,128)(2,1)S(1)} %pad_maximum_fusion.refs_0_) | copy-start | bytes 1228804
  20.6 17.7 %collective-permute-start.4 = (bf16[4,400,128]{2,1,0:T(8,128)(2,1)S(1)}, bf16[4,400,128]{2,1,0:T(8,128)(2,1)}, u32[]{:S(2)}, u32[]{:S(2)}) collective-permute-start(bf16[4,400,128]{2,1,0:T(8,128)(2,1)S(1)} %pad_maximum_fusion.refs_0_), channel_id=1, source_target_pairs={{0,1},{1,2},{2,3},{3,4},{4,5},{5,6},{6,7},{7,0},{8,9},{9,10},{10,1... | collective-permute-start | bytes 1228808 | tf_op jit(solution)/shard_map/ppermute | solution.py:433
  22.3 17.7 %collective-permute-start.5 = (bf16[4,400,128]{2,1,0:T(8,128)(2,1)S(1)}, bf16[4,400,128]{2,1,0:T(8,128)(2,1)}, u32[]{:S(2)}, u32[]{:S(2)}) collective-permute-start(bf16[4,400,128]{2,1,0:T(8,128)(2,1)S(1)} %pad_maximum_fusion.refs_0_), channel_id=1, source_target_pairs={{0,7},{1,0},{2,1},{3,2},{4,3},{5,4},{6,5},{7,6},{8,15},{9,8},{10,9... | collective-permute-start | bytes 1228808 | tf_op jit(solution)/shard_map/ppermute | solution.py:433
  26.3 18.5 %collective-permute-start.11 = (bf16[4,400,128]{2,1,0:T(8,128)(2,1)S(1)}, bf16[4,400,128]{2,1,0:T(8,128)(2,1)S(1)}, u32[]{:S(2)}, u32[]{:S(2)}) collective-permute-start(bf16[4,400,128]{2,1,0:T(8,128)(2,1)S(1)} %pad_maximum_fusion.refs_0_), channel_id=1, source_target_pairs={{0,32},{32,0},{64,96},{96,64},{128,160},{160,128},{192,224},{224,1... | collective-permute-start | bytes 1228808 | tf_op jit(solution)/shard_map/ppermute | solution.py:436
  26.3 6.2 %collective-permute-start.8 = (bf16[144,256]{1,0:T(8,128)(2,1)S(1)}, bf16[144,256]{1,0:T(8,128)(2,1)S(1)}, u32[]{:S(2)}, u32[]{:S(2)}) collective-permute-start(bf16[144,256]{1,0:T(8,128)(2,1)S(1)} %get-tuple-element.32), channel_id=1, source_target_pairs={{0,192},{32,224},{64,0},{96,32},{128,64},{160,96},{192,128},{224,1... | collective-permute-start | bytes 221192 | tf_op jit(solution)/shard_map/ppermute | solution.py:436
  29.4 5.1 %collective-permute-start.9 = (bf16[144,256]{1,0:T(8,128)(2,1)S(1)}, bf16[144,256]{1,0:T(8,128)(2,1)S(1)}, u32[]{:S(2)}, u32[]{:S(2)}) collective-permute-start(bf16[144,256]{1,0:T(8,128)(2,1)S(1)} %get-tuple-element.33), channel_id=1, source_target_pairs={{0,128},{32,160},{64,192},{96,224},{128,0},{160,32},{192,64},{224,... | collective-permute-start | bytes 221192 | tf_op jit(solution)/shard_map/ppermute | solution.py:436
  32.6 5.3 %collective-permute-start.10 = (bf16[144,256]{1,0:T(8,128)(2,1)S(1)}, bf16[144,256]{1,0:T(8,128)(2,1)S(1)}, u32[]{:S(2)}, u32[]{:S(2)}) collective-permute-start(bf16[144,256]{1,0:T(8,128)(2,1)S(1)} %get-tuple-element.34), channel_id=1, source_target_pairs={{0,64},{32,96},{64,128},{96,160},{128,192},{160,224},{192,0},{224,... | collective-permute-start | bytes 221192 | tf_op jit(solution)/shard_map/ppermute | solution.py:436
  38.3 6.5 %collective-permute-start.12 = (bf16[4,400,128]{2,1,0:T(8,128)(2,1)}, bf16[4,400,128]{2,1,0:T(8,128)(2,1)S(1)}, u32[]{:S(2)}, u32[]{:S(2)}) collective-permute-start(bf16[4,400,128]{2,1,0:T(8,128)(2,1)} %collective-permute-done.4.refs_1_), channel_id=1, source_target_pairs={{0,32},{32,0},{64,96},{96,64},{128,160},{160,128},{192,224},{224,1... | collective-permute-start | bytes 1228808 | tf_op jit(solution)/shard_map/ppermute | solution.py:436
  40.0 6.3 %collective-permute-start.13 = (bf16[4,400,128]{2,1,0:T(8,128)(2,1)}, bf16[4,400,128]{2,1,0:T(8,128)(2,1)}, u32[]{:S(2)}, u32[]{:S(2)}) collective-permute-start(bf16[4,400,128]{2,1,0:T(8,128)(2,1)} %collective-permute-done.5.refs_2_), channel_id=1, source_target_pairs={{0,32},{32,0},{64,96},{96,64},{128,160},{160,128},{192,224},{224,1... | collective-permute-start | bytes 1228808 | tf_op jit(solution)/shard_map/ppermute | solution.py:436
  42.1 12.8 %collective-permute-start.6 = (bf16[4,400,128]{2,1,0:T(8,128)(2,1)}, bf16[4,400,128]{2,1,0:T(8,128)(2,1)S(1)}, u32[]{:S(2)}, u32[]{:S(2)}) collective-permute-start(bf16[4,400,128]{2,1,0:T(8,128)(2,1)} %collective-permute-done.4.refs_1_), channel_id=1, source_target_pairs={{0,1},{1,2},{2,3},{3,4},{4,5},{5,6},{6,7},{7,0},{8,9},{9,10},{10,1... | collective-permute-start | bytes 1228808 | tf_op jit(solution)/shard_map/ppermute | solution.py:433
  42.1 12.8 %collective-permute-start.7 = (bf16[4,400,128]{2,1,0:T(8,128)(2,1)}, bf16[4,400,128]{2,1,0:T(8,128)(2,1)S(1)}, u32[]{:S(2)}, u32[]{:S(2)}) collective-permute-start(bf16[4,400,128]{2,1,0:T(8,128)(2,1)} %collective-permute-done.5.refs_2_), channel_id=1, source_target_pairs={{0,7},{1,0},{2,1},{3,2},{4,3},{5,4},{6,5},{7,6},{8,15},{9,8},{10,9... | collective-permute-start | bytes 1228808 | tf_op jit(solution)/shard_map/ppermute | solution.py:433
  54.9 11.8 %copy-start.5 = (bf16[4,400,128]{2,1,0:T(8,128)(2,1)}, bf16[4,400,128]{2,1,0:T(8,128)(2,1)S(1)}, u32[]{:S(2)}) copy-start(bf16[4,400,128]{2,1,0:T(8,128)(2,1)S(1)} %get-tuple-element.35.refs_0_.refs_3_) | copy-start | bytes 1228804
  54.9 11.8 %copy-start.7 = (bf16[4,400,128]{2,1,0:T(8,128)(2,1)}, bf16[4,400,128]{2,1,0:T(8,128)(2,1)S(1)}, u32[]{:S(2)}) copy-start(bf16[4,400,128]{2,1,0:T(8,128)(2,1)S(1)} %get-tuple-element.36.refs_1_.refs_4_) | copy-start | bytes 1228804
  55.0 3.8 %collective-permute-start.16 = (bf16[4,400,128]{2,1,0:T(8,128)(2,1)S(1)}, bf16[4,400,128]{2,1,0:T(8,128)(2,1)S(1)}, u32[]{:S(2)}, u32[]{:S(2)}) collective-permute-start(bf16[4,400,128]{2,1,0:T(8,128)(2,1)S(1)} %get-tuple-element.35.refs_0_.refs_3_), channel_id=1, source_target_pairs={{0,32},{32,0},{64,96},{96,64},{128,160},{160,128},{192,224},{224,1... | collective-permute-start | bytes 1228808 | tf_op jit(solution)/shard_map/ppermute | solution.py:436
  56.0 2.8 %collective-permute-start.17 = (bf16[4,400,128]{2,1,0:T(8,128)(2,1)S(1)}, bf16[4,400,128]{2,1,0:T(8,128)(2,1)S(1)}, u32[]{:S(2)}, u32[]{:S(2)}) collective-permute-start(bf16[4,400,128]{2,1,0:T(8,128)(2,1)S(1)} %get-tuple-element.36.refs_1_.refs_4_), channel_id=1, source_target_pairs={{0,32},{32,0},{64,96},{96,64},{128,160},{160,128},{192,224},{224,1... | collective-permute-start | bytes 1228808 | tf_op jit(solution)/shard_map/ppermute | solution.py:436
  56.1 11.8 %collective-permute-start.14 = (bf16[4,400,128]{2,1,0:T(8,128)(2,1)S(1)}, bf16[4,400,128]{2,1,0:T(8,128)(2,1)S(1)}, u32[]{:S(2)}, u32[]{:S(2)}) collective-permute-start(bf16[4,400,128]{2,1,0:T(8,128)(2,1)S(1)} %get-tuple-element.35.refs_0_.refs_3_), channel_id=1, source_target_pairs={{0,1},{1,2},{2,3},{3,4},{4,5},{5,6},{6,7},{7,0},{8,9},{9,10},{10,1... | collective-permute-start | bytes 1228808 | tf_op jit(solution)/shard_map/ppermute | solution.py:433
  56.1 11.8 %collective-permute-start.15 = (bf16[4,400,128]{2,1,0:T(8,128)(2,1)S(1)}, bf16[4,400,128]{2,1,0:T(8,128)(2,1)S(1)}, u32[]{:S(2)}, u32[]{:S(2)}) collective-permute-start(bf16[4,400,128]{2,1,0:T(8,128)(2,1)S(1)} %get-tuple-element.36.refs_1_.refs_4_), channel_id=1, source_target_pairs={{0,7},{1,0},{2,1},{3,2},{4,3},{5,4},{6,5},{7,6},{8,15},{9,8},{10,9... | collective-permute-start | bytes 1228808 | tf_op jit(solution)/shard_map/ppermute | solution.py:433
  68.0 12.0 %copy-start = (bf16[4,400,128]{2,1,0:T(8,128)(2,1)}, bf16[4,400,128]{2,1,0:T(8,128)(2,1)S(1)}, u32[]{:S(2)}) copy-start(bf16[4,400,128]{2,1,0:T(8,128)(2,1)S(1)} %get-tuple-element.39.refs_1_.refs_6_) | copy-start | bytes 1228804
  68.0 4.1 %collective-permute-start.20 = (bf16[4,400,128]{2,1,0:T(8,128)(2,1)S(1)}, bf16[4,400,128]{2,1,0:T(8,128)(2,1)S(1)}, u32[]{:S(2)}, u32[]{:S(2)}) collective-permute-start(bf16[4,400,128]{2,1,0:T(8,128)(2,1)S(1)} %get-tuple-element.38.refs_0_.refs_5_), channel_id=1, source_target_pairs={{0,32},{32,0},{64,96},{96,64},{128,160},{160,128},{192,224},{224,1... | collective-permute-start | bytes 1228808 | tf_op jit(solution)/shard_map/ppermute | solution.py:436
  69.2 2.9 %collective-permute-start.21 = (bf16[4,400,128]{2,1,0:T(8,128)(2,1)S(1)}, bf16[4,400,128]{2,1,0:T(8,128)(2,1)S(1)}, u32[]{:S(2)}, u32[]{:S(2)}) collective-permute-start(bf16[4,400,128]{2,1,0:T(8,128)(2,1)S(1)} %get-tuple-element.39.refs_1_.refs_6_), channel_id=1, source_target_pairs={{0,32},{32,0},{64,96},{96,64},{128,160},{160,128},{192,224},{224,1... | collective-permute-start | bytes 1228808 | tf_op jit(solution)/shard_map/ppermute | solution.py:436
  69.4 10.7 %collective-permute-start.18 = (bf16[2,400,128]{2,1,0:T(8,128)(2,1)S(1)}, bf16[2,400,128]{2,1,0:T(8,128)(2,1)}, u32[]{:S(2)}, u32[]{:S(2)}) collective-permute-start(bf16[2,400,128]{2,1,0:T(8,128)(2,1)S(1)} %slice.32), channel_id=1, source_target_pairs={{0,1},{1,2},{2,3},{3,4},{4,5},{5,6},{6,7},{7,0},{8,9},{9,10},{10,1... | collective-permute-start | bytes 614408 | tf_op jit(solution)/shard_map/ppermute | solution.py:433
  71.1 8.9 %collective-permute-start.19 = (bf16[2,400,128]{2,1,0:T(8,128)(2,1)S(1)}, bf16[2,400,128]{2,1,0:T(8,128)(2,1)}, u32[]{:S(2)}, u32[]{:S(2)}) collective-permute-start(bf16[2,400,128]{2,1,0:T(8,128)(2,1)S(1)} %slice.33), channel_id=1, source_target_pairs={{0,7},{1,0},{2,1},{3,2},{4,3},{5,4},{6,5},{7,6},{8,15},{9,8},{10,9... | collective-permute-start | bytes 614408 | tf_op jit(solution)/shard_map/ppermute | solution.py:433
  80.0 1.9 %collective-permute-start.22 = (bf16[2,400,128]{2,1,0:T(8,128)(2,1)}, bf16[2,400,128]{2,1,0:T(8,128)(2,1)}, u32[]{:S(2)}, u32[]{:S(2)}) collective-permute-start(bf16[2,400,128]{2,1,0:T(8,128)(2,1)} %get-tuple-element.41.refs_0_.refs_7_), channel_id=1, source_target_pairs={{0,32},{32,0},{64,96},{96,64},{128,160},{160,128},{192,224},{224,1... | collective-permute-start | bytes 614408 | tf_op jit(solution)/shard_map/ppermute | solution.py:436
  80.1 2.1 %collective-permute-start.23 = (bf16[2,400,128]{2,1,0:T(8,128)(2,1)}, bf16[2,400,128]{2,1,0:T(8,128)(2,1)}, u32[]{:S(2)}, u32[]{:S(2)}) collective-permute-start(bf16[2,400,128]{2,1,0:T(8,128)(2,1)} %get-tuple-element.42.refs_1_.refs_8_), channel_id=1, source_target_pairs={{0,32},{32,0},{64,96},{96,64},{128,160},{160,128},{192,224},{224,1... | collective-permute-start | bytes 614408 | tf_op jit(solution)/shard_map/ppermute | solution.py:436
  88.6 26.3 %collective-permute-start.24 = (bf16[64,48,128]{2,1,0:T(8,128)(2,1)}, bf16[64,48,128]{2,1,0:T(8,128)(2,1)}, u32[]{:S(2)}, u32[]{:S(2)}) collective-permute-start(bf16[64,48,128]{2,1,0:T(8,128)(2,1)} %get-tuple-element.46), channel_id=1, source_target_pairs={{0,192},{32,224},{64,0},{96,32},{128,64},{160,96},{192,128},{224,1... | collective-permute-start | bytes 2359304 | tf_op jit(solution)/shard_map/ppermute | solution.py:436
  90.5 24.5 %collective-permute-start.25 = (bf16[64,48,128]{2,1,0:T(8,128)(2,1)}, bf16[64,48,128]{2,1,0:T(8,128)(2,1)}, u32[]{:S(2)}, u32[]{:S(2)}) collective-permute-start(bf16[64,48,128]{2,1,0:T(8,128)(2,1)} %get-tuple-element.47), channel_id=1, source_target_pairs={{0,128},{32,160},{64,192},{96,224},{128,0},{160,32},{192,64},{224,... | collective-permute-start | bytes 2359304 | tf_op jit(solution)/shard_map/ppermute | solution.py:436
  90.5 37.6 %collective-permute-start.26 = (bf16[64,48,128]{2,1,0:T(8,128)(2,1)}, bf16[64,48,128]{2,1,0:T(8,128)(2,1)}, u32[]{:S(2)}, u32[]{:S(2)}) collective-permute-start(bf16[64,48,128]{2,1,0:T(8,128)(2,1)} %get-tuple-element.48), channel_id=1, source_target_pairs={{0,64},{32,96},{64,128},{96,160},{128,192},{160,224},{192,0},{224,... | collective-permute-start | bytes 2359304 | tf_op jit(solution)/shard_map/ppermute | solution.py:436
  128.0 10.8 %collective-permute-start.27 = (f32[8,128]{1,0:T(8,128)S(1)}, f32[8,128]{1,0:T(8,128)S(1)}, u32[]{:S(2)}, u32[]{:S(2)}) collective-permute-start(f32[8,128]{1,0:T(8,128)S(1)} %hold.9), channel_id=1, source_target_pairs={{0,0},{64,32},{128,64},{192,96},{32,128},{96,160},{160,192},{224,2... | collective-permute-start | bytes 12296 | tf_op jit(solution)/shard_map/ppermute | solution.py:509
  (19 other events, 89.3 us)

commit v4 on v3

--- a/solution.py
+++ b/solution.py
@@ -38,9 +38,9 @@
 
 
 def open_kernel(group_ref, *refs):
-    candidate_ref, block_ref, messages = refs[6], refs[7], refs[8:12]
-    patches_ref, weight_ref, caption_ref, probe_ref, states_ref, ask_ref, sems = refs[12:]
-    fetched(refs[:6], refs[12:18], sems)
+    block_ref, messages = refs[6], refs[7:11]
+    patches_ref, weight_ref, caption_ref, probe_ref, states_ref, ask_ref, sems = refs[11:]
+    fetched(refs[:6], refs[11:17], sems)
     across = (((1,), (1,)), ((), ()))
     patches = patches_ref[0]
     weight = weight_ref[...]
@@ -73,8 +73,6 @@
             block_ref[h * 128 + HD : (h + 1) * 128] = rows[:, 128:]
 
     queries = jnp.dot(states_ref[...].reshape(128, 768), ask_ref[...], preferred_element_type=F32)
-    ids = jnp.concatenate([candidate_ref[c] for c in range(4)], axis=1).astype(F32)
-    tail = jnp.concatenate([ids, jnp.zeros((16, 252), F32)], axis=1).astype(BF16)
     pad = jnp.zeros((128, HD), F32)
     x = lax.shift_right_logical(group_ref[0], 1)
     for k in range(4):
@@ -85,23 +83,20 @@
             def _():
                 messages[d][0:128, :] = rows
 
-    for d in range(4):
-        messages[d][128:144, :] = tail
-
-
-def opening(group, sources, candidates):
+
+def opening(group, sources):
     vmem, hbm = pl.BlockSpec(memory_space=pltpu.VMEM), pl.BlockSpec(memory_space=pltpu.HBM)
     outs = pl.pallas_call(
         open_kernel,
         out_shape=[jax.ShapeDtypeStruct((BROWS, 128), BF16)]
         + [jax.ShapeDtypeStruct((144, 256), BF16)] * 4,
-        in_specs=[pl.BlockSpec(memory_space=pltpu.SMEM)] + [hbm] * 6 + [vmem],
+        in_specs=[pl.BlockSpec(memory_space=pltpu.SMEM)] + [hbm] * 6,
         out_specs=[vmem] * 5,
         scratch_shapes=[pltpu.VMEM(source.shape, source.dtype) for source in sources]
         + [pltpu.SemaphoreType.DMA((7,))],
         compiler_params=pltpu.CompilerParams(vmem_limit_bytes=12 * 1024 * 1024),
         name="opening",
-    )(group, *[in_hbm(source) for source in sources], candidates)
+    )(group, *[in_hbm(source) for source in sources])
     return outs[0], outs[1:]
 
 
@@ -121,6 +116,27 @@
         compiler_params=pltpu.CompilerParams(vmem_limit_bytes=1024 * 1024),
         name="hold",
     )(*values, *after)
+
+
+def seal_kernel(*refs):
+    candidate_ref, messages = refs[4], refs[-4:]
+    ids = jnp.concatenate([candidate_ref[c] for c in range(4)], axis=1).astype(F32)
+    tail = jnp.concatenate([ids, jnp.zeros((16, 252), F32)], axis=1).astype(BF16)
+    for message in messages:
+        message[128:144, :] = tail
+
+
+def seal(messages, candidates, after):
+    anywhere, vmem = pl.BlockSpec(memory_space=pl.ANY), pl.BlockSpec(memory_space=pltpu.VMEM)
+    return pl.pallas_call(
+        seal_kernel,
+        out_shape=[jax.ShapeDtypeStruct((144, 256), BF16)] * 4,
+        in_specs=[vmem] * 5 + [anywhere] * len(after),
+        out_specs=[vmem] * 4,
+        input_output_aliases={k: k for k in range(4)},
+        compiler_params=pltpu.CompilerParams(vmem_limit_bytes=4 * 1024 * 1024),
+        name="seal",
+    )(*messages, candidates, *after)
 
 
 def spread_kernel(q0, q1, q2, q3, query):
@@ -436,7 +452,7 @@
         return lax.ppermute(value, "group", group_moves(dx, flip))
 
     sources = [patches, keyvalue_weight.T, caption_embed, probe_blocks, query_states, query_weight]
-    block, messages = opening(group_index.reshape(1), sources, candidates)
+    block, messages = opening(group_index.reshape(1), sources)
     homes = [(k, 2 * k) for k in range(4)] + [(4 + k, 2 * k + 1) for k in range(4)]
 
     def homeward(dy):
@@ -444,7 +460,7 @@
         return lax.ppermute(block, ("group", "shard"), moves)
 
     arrived = [homeward(dy) for dy in range(4)]
-    messages = hold(messages, arrived[:2])
+    messages = seal(messages, candidates, arrived[:2])
     received = [messages[0]] + [along_group(messages[4 - d], 4 - d) for d in (1, 2, 3)]
     stack = jnp.stack(arrived)
     pair_images = jnp.stack([part[128:144, :4].T for part in received]).reshape(256).astype(jnp.int32)
@@ -483,10 +499,12 @@
             coming = [along_shard(right[:2], 0, 1), along_shard(left[2:], 0, -1)]
         waiting += pieces[-1]
         if step > 0:
-            other = [along_group(part, 0, 1) for part in waiting]
-            context, outs = attend(plan, first_image, query, waiting, other, context, step == 4)
-            first_image += sum(part.shape[0] for part in waiting)
-            waiting = []
+            if step == 1:
+                waiting = [*hold([stack], received[1:]), *waiting[1:]]
+            now, waiting = (waiting[:2], waiting[2:]) if step == 1 else (waiting, [])
+            other = [along_group(part, 0, 1) for part in now]
+            context, outs = attend(plan, first_image, query, now, other, context, step == 4)
+            first_image += sum(part.shape[0] for part in now)
         if step < 4:
             right, left = coming
             if step > 0:

time: 140 us -> 136 us (0.971)
  waiting for transfers between devices: 27.4 us -> 18.8 us
  blocking collectives: 17.1 us -> 19.6 us
  starting transfers between devices: 39.4 us -> 41.4 us
    ppermute x15, waiting for transfers between devices: 22.2 us -> 15.6 us  [along_group(): return lax.ppermute(value, 'group', group_moves(dx, flip))]
    all_to_all x1, blocking collectives: 17.1 us -> 19.6 us  [on_device(): lax.all_to_all(partial, 'shard', split_axis=0, concat_axis=0, tiled=True)]
    unnamed x47 -> x52, local copies, waits for them, and re-layouts: 6.42 us -> 6.85 us
  transfers between devices with their start and end apart: 28 -> 28, of which waited for: 10 -> 8; matrix products, arithmetic and copies ran while one was open for 4% -> 4% of each run, Pallas kernels for 23% -> 24%
where the time goes in v4:
time: 136 us; the launch traced here: 135 us
  starting transfers between devices  41.4 us (30%)
  Pallas kernels  41.2 us (30%)
  blocking collectives  19.6 us (14%)
  waiting for transfers between devices  18.8 us (14%)
  local copies, waits for them, and re-layouts  10.3 us (8%)
  other arithmetic  2.16 us (2%)
    pallas_call x4, Pallas kernels, attend(): pl.pallas_call(functools.partial(attend_kernel, sizes, first_image, 5, fr...  27.8 us
    all_to_all x1, blocking collectives, on_device(): lax.all_to_all(partial, 'shard', split_axis=0, concat_axis=0, tiled=True)  19.6 us
    ppermute x15, waiting for transfers between devices, along_group(): return lax.ppermute(value, 'group', group_moves(dx, flip))  15.6 us
    ppermute x8, starting transfers between devices, along_shard(): return lax.ppermute(value, 'shard', grid_moves(dy, dz))  13.8 us
    ppermute x4, starting transfers between devices, homeward(): return lax.ppermute(block, ('group', 'shard'), moves)  11.9 us
    ppermute x15, starting transfers between devices, along_group(): return lax.ppermute(value, 'group', group_moves(dx, flip))  11.9 us
    pallas_call x1, Pallas kernels, finish(): pl.pallas_call(finish_kernel, out_shape=jax.ShapeDtypeStruct((4, 16, NQ,...  7.91 us
    unnamed x52, local copies, waits for them, and re-layouts  6.85 us
  transfers between devices with their start and end apart: 28, of which 8 were waited for; matrix products, arithmetic and copies ran while one was open for 4% of the time, Pallas kernels for 24%

profile of v4, /device:TPU:1, one launch (start us, length us, event | category | flops | bytes accessed | tf_op | source)
XLA Modules:
  0.0 134.7 jit_solution(18384383427354927926)
XLA Ops:
  0.6 3.2 %opening.1 = (bf16[400,128]{1,0:T(8,128)(2,1)S(1)}, bf16[144,256]{1,0:T(8,128)(2,1)S(1)}, bf16[144,256]{1,0:T(8,128)(2,1)S(1)}, bf16[144,256]{1,0:T(8,128)(2,1)S(1)}, bf16[144,256]{1,0:T(8,128)(2,1)S(1)}) custom-call(s32[1]{0:T(128)} %bitcast.2.group_ref, bf16[1,257,1408]{2,1,0:T(8,128)(2,1)} %refs_0_.1, bf16[192,1408]{1,0:T(8,128)(2,1)} %bitcast.71, ...), custom_call_target="tpu_custom_call" | custom-call | tf_op jit(solution)/shard_map/opening/pallas_call | solution.py:89
  3.8 4.5 %collective-permute-start = (bf16[400,128]{1,0:T(8,128)(2,1)S(1)}, bf16[400,128]{1,0:T(8,128)(2,1)S(1)}, u32[]{:S(2)}, u32[]{:S(2)}) collective-permute-start(bf16[400,128]{1,0:T(8,128)(2,1)S(1)} %get-tuple-element.26), channel_id=1, source_target_pairs={{0,0},{1,1},{2,2},{3,3},{4,4},{5,5},{6,6},{7,7},{8,8},{9,9},{10,10... | collective-permute-start | bytes 307208 | tf_op jit(solution)/shard_map/ppermute | solution.py:460
  8.3 2.6 %collective-permute-start.1 = (bf16[400,128]{1,0:T(8,128)(2,1)S(1)}, bf16[400,128]{1,0:T(8,128)(2,1)S(1)}, u32[]{:S(2)}, u32[]{:S(2)}) collective-permute-start(bf16[400,128]{1,0:T(8,128)(2,1)S(1)} %get-tuple-element.26), channel_id=1, source_target_pairs={{0,8},{1,9},{2,10},{3,11},{4,12},{5,13},{6,14},{7,15},{8,16},{9,17... | collective-permute-start | bytes 307208 | tf_op jit(solution)/shard_map/ppermute | solution.py:460
  10.9 2.3 %collective-permute-start.2 = (bf16[400,128]{1,0:T(8,128)(2,1)S(1)}, bf16[400,128]{1,0:T(8,128)(2,1)S(1)}, u32[]{:S(2)}, u32[]{:S(2)}) collective-permute-start(bf16[400,128]{1,0:T(8,128)(2,1)S(1)} %get-tuple-element.26), channel_id=1, source_target_pairs={{0,16},{1,17},{2,18},{3,19},{4,20},{5,21},{6,22},{7,23},{8,24},{9,... | collective-permute-start | bytes 307208 | tf_op jit(solution)/shard_map/ppermute | solution.py:460
  13.3 2.5 %collective-permute-start.3 = (bf16[400,128]{1,0:T(8,128)(2,1)S(1)}, bf16[400,128]{1,0:T(8,128)(2,1)S(1)}, u32[]{:S(2)}, u32[]{:S(2)}) collective-permute-start(bf16[400,128]{1,0:T(8,128)(2,1)S(1)} %get-tuple-element.26), channel_id=1, source_target_pairs={{0,24},{1,25},{2,26},{3,27},{4,28},{5,29},{6,30},{7,31},{8,0},{9,1... | collective-permute-start | bytes 307208 | tf_op jit(solution)/shard_map/ppermute | solution.py:460
  16.5 2.4 %collective-permute-done.2 = bf16[400,128]{1,0:T(8,128)(2,1)S(1)} collective-permute-done((bf16[400,128]{1,0:T(8,128)(2,1)S(1)}, bf16[400,128]{1,0:T(8,128)(2,1)S(1)}, u32[]{:S(2)}, u32[]{:S(2)}) %collective-permute-start.2) | collective-permute-done | bytes 102432 | tf_op jit(solution)/shard_map/ppermute | solution.py:460
  19.8 1.7 %collective-permute-start.4 = (bf16[4,400,128]{2,1,0:T(8,128)(2,1)S(1)}, bf16[4,400,128]{2,1,0:T(8,128)(2,1)}, u32[]{:S(2)}, u32[]{:S(2)}) collective-permute-start(bf16[4,400,128]{2,1,0:T(8,128)(2,1)S(1)} %pad_maximum_fusion.refs_0_), channel_id=1, source_target_pairs={{0,1},{1,2},{2,3},{3,4},{4,5},{5,6},{6,7},{7,0},{8,9},{9,10},{10,1... | collective-permute-start | bytes 1228808 | tf_op jit(solution)/shard_map/ppermute | solution.py:449
  21.6 4.0 %collective-permute-start.5 = (bf16[4,400,128]{2,1,0:T(8,128)(2,1)S(1)}, bf16[4,400,128]{2,1,0:T(8,128)(2,1)}, u32[]{:S(2)}, u32[]{:S(2)}) collective-permute-start(bf16[4,400,128]{2,1,0:T(8,128)(2,1)S(1)} %pad_maximum_fusion.refs_0_), channel_id=1, source_target_pairs={{0,7},{1,0},{2,1},{3,2},{4,3},{5,4},{6,5},{7,6},{8,15},{9,8},{10,9... | collective-permute-start | bytes 1228808 | tf_op jit(solution)/shard_map/ppermute | solution.py:449
  25.7 2.1 %collective-permute-start.9 = (bf16[144,256]{1,0:T(8,128)(2,1)S(1)}, bf16[144,256]{1,0:T(8,128)(2,1)S(1)}, u32[]{:S(2)}, u32[]{:S(2)}) collective-permute-start(bf16[144,256]{1,0:T(8,128)(2,1)S(1)} %get-tuple-element.33), channel_id=1, source_target_pairs={{0,128},{32,160},{64,192},{96,224},{128,0},{160,32},{192,64},{224,... | collective-permute-start | bytes 221192 | tf_op jit(solution)/shard_map/ppermute | solution.py:452
  27.9 1.6 %collective-permute-done.8.q1.refs_1_ = bf16[144,256]{1,0:T(8,128)(2,1)S(1)} collective-permute-done((bf16[144,256]{1,0:T(8,128)(2,1)S(1)}, bf16[144,256]{1,0:T(8,128)(2,1)S(1)}, u32[]{:S(2)}, u32[]{:S(2)}) %collective-permute-start.8) | collective-permute-done | bytes 73760 | tf_op jit(solution)/shard_map/ppermute | solution.py:452
  29.5 1.0 collective-permute-done.9.q2.refs_2_
  30.7 1.5 %collective-permute-done.10.q3.refs_3_ = bf16[144,256]{1,0:T(8,128)(2,1)S(1)} collective-permute-done((bf16[144,256]{1,0:T(8,128)(2,1)S(1)}, bf16[144,256]{1,0:T(8,128)(2,1)S(1)}, u32[]{:S(2)}, u32[]{:S(2)}) %collective-permute-start.10) | collective-permute-done | bytes 73760 | tf_op jit(solution)/shard_map/ppermute | solution.py:452
  32.4 3.3 %collective-permute-start.11 = (bf16[4,400,128]{2,1,0:T(8,128)(2,1)S(1)}, bf16[4,400,128]{2,1,0:T(8,128)(2,1)S(1)}, u32[]{:S(2)}, u32[]{:S(2)}) collective-permute-start(bf16[4,400,128]{2,1,0:T(8,128)(2,1)S(1)} %hold.5.refs_0_), channel_id=1, source_target_pairs={{0,32},{32,0},{64,96},{96,64},{128,160},{160,128},{192,224},{224,1... | collective-permute-start | bytes 1228808 | tf_op jit(solution)/shard_map/ppermute | solution.py:452
  37.2 0.9 copy-done.12
  38.0 2.7 %collective-permute-start.7 = (bf16[4,400,128]{2,1,0:T(8,128)(2,1)}, bf16[4,400,128]{2,1,0:T(8,128)(2,1)S(1)}, u32[]{:S(2)}, u32[]{:S(2)}) collective-permute-start(bf16[4,400,128]{2,1,0:T(8,128)(2,1)} %collective-permute-done.5.refs_0_.refs_2_), channel_id=1, source_target_pairs={{0,7},{1,0},{2,1},{3,2},{4,3},{5,4},{6,5},{7,6},{8,15},{9,8},{10,9... | collective-permute-start | bytes 1228808 | tf_op jit(solution)/shard_map/ppermute | solution.py:449
  40.7 1.1 collective-permute-start.15
  42.5 1.0 copy-done.6
  43.5 7.2 %attend.4.refs_2_ = bf16[256,48,128]{2,1,0:T(8,128)(2,1)S(1)} custom-call(s32[512]{0:T(512)} %concatenate.4.plan_ref, bf16[3,2,16,32,128]{4,3,2,1,0:T(8,128)(2,1)} %copy-done.12, bf16[4,400,128]{2,1,0:T(8,128)(2,1)S(1)} %copy-done.6, bf16[4,400,128]{2,1,0:T(8,128)(2,1)} %collective-permute-done.4.refs_1_, bf16[4,400,128]{2,1,0:T(8,128)(2,1)} %copy-done.20, ...), custom_call_target="tpu_custom_call" | custom-call | flops 4800000000 | bytes 6400000 | tf_op jit(solution)/shard_map/attend/pallas_call | solution.py:268
  51.5 2.7 %collective-permute-start.14 = (bf16[4,400,128]{2,1,0:T(8,128)(2,1)S(1)}, bf16[4,400,128]{2,1,0:T(8,128)(2,1)S(1)}, u32[]{:S(2)}, u32[]{:S(2)}) collective-permute-start(bf16[4,400,128]{2,1,0:T(8,128)(2,1)S(1)} %get-tuple-element.36.refs_2_.refs_4_), channel_id=1, source_target_pairs={{0,7},{1,0},{2,1},{3,2},{4,3},{5,4},{6,5},{7,6},{8,15},{9,8},{10,9... | collective-permute-start | bytes 1228808 | tf_op jit(solution)/shard_map/ppermute | solution.py:449
  55.3 8.3 %attend.5.refs_2_ = bf16[256,48,128]{2,1,0:T(8,128)(2,1)S(1)} custom-call(s32[512]{0:T(512)} %concatenate.4.plan_ref, bf16[3,2,16,32,128]{4,3,2,1,0:T(8,128)(2,1)} %copy-done.12, bf16[4,400,128]{2,1,0:T(8,128)(2,1)} %collective-permute-done.5.refs_0_.refs_2_, ...), custom_call_target="tpu_custom_call", output_to_operand_aliasing={{}: (8, {})} | custom-call | flops 7200000000 | bytes 9600000 | tf_op jit(solution)/shard_map/attend/pallas_call | solution.py:268
  63.7 1.0 collective-permute-start.20
  64.9 2.3 %collective-permute-start.18 = (bf16[2,400,128]{2,1,0:T(8,128)(2,1)S(1)}, bf16[2,400,128]{2,1,0:T(8,128)(2,1)}, u32[]{:S(2)}, u32[]{:S(2)}) collective-permute-start(bf16[2,400,128]{2,1,0:T(8,128)(2,1)S(1)} %slice.32), channel_id=1, source_target_pairs={{0,1},{1,2},{2,3},{3,4},{4,5},{5,6},{6,7},{7,0},{8,9},{9,10},{10,1... | collective-permute-start | bytes 614408 | tf_op jit(solution)/shard_map/ppermute | solution.py:449
  68.5 5.9 %attend.6.refs_2_ = bf16[256,48,128]{2,1,0:T(8,128)(2,1)S(1)} custom-call(s32[512]{0:T(512)} %concatenate.4.plan_ref, bf16[3,2,16,32,128]{4,3,2,1,0:T(8,128)(2,1)} %copy-done.12, bf16[4,400,128]{2,1,0:T(8,128)(2,1)S(1)} %get-tuple-element.38.refs_0_.refs_5_, ...), custom_call_target="tpu_custom_call", output_to_operand_aliasing={{}: (6, {})} | custom-call | flops 4800000000 | bytes 6400000 | tf_op jit(solution)/shard_map/attend/pallas_call | solution.py:268
  74.5 1.1 collective-permute-start.22
  77.4 6.4 %attend.7 = (bf16[256,48,128]{2,1,0:T(8,128)(2,1)S(1)}, bf16[64,48,128]{2,1,0:T(8,128)(2,1)}, bf16[64,48,128]{2,1,0:T(8,128)(2,1)}, bf16[64,48,128]{2,1,0:T(8,128)(2,1)}) custom-call(s32[512]{0:T(512)} %concatenate.4.plan_ref, bf16[3,2,16,32,128]{4,3,2,1,0:T(8,128)(2,1)} %copy-done.12, ...), custom_call_target="tpu_custom_call", output_to_operand_aliasing={{0}: (6, {})} | custom-call | flops 2400000000 | bytes 3200000 | tf_op jit(solution)/shard_map/attend/pallas_call | solution.py:268
  84.4 1.5 %collective-permute-start.25 = (bf16[64,48,128]{2,1,0:T(8,128)(2,1)}, bf16[64,48,128]{2,1,0:T(8,128)(2,1)}, u32[]{:S(2)}, u32[]{:S(2)}) collective-permute-start(bf16[64,48,128]{2,1,0:T(8,128)(2,1)} %get-tuple-element.47), channel_id=1, source_target_pairs={{0,128},{32,160},{64,192},{96,224},{128,0},{160,32},{192,64},{224,... | collective-permute-start | bytes 2359304 | tf_op jit(solution)/shard_map/ppermute | solution.py:452
  86.7 2.2 %score.1 = (f32[2,128]{1,0:T(2,128)S(1)}, bf16[64,48,128]{2,1,0:T(8,128)(2,1)S(1)}) custom-call(s32[1]{0:T(128)} %bitcast.1.shard_ref, bf16[4,400,128]{2,1,0:T(8,128)(2,1)S(1)} %pad_maximum_fusion.refs_0_, bf16[4,400,128]{2,1,0:T(8,128)(2,1)} %collective-permute-done.4.refs_1_, bf16[4,400,128]{2,1,0:T(8,128)(2,1)} %collective-permute-done.5.refs_0_.refs_2_, ...), custom_call_target="tpu_custom_call" | custom-call | flops 1000 | bytes 1000 | tf_op jit(solution)/shard_map/score/pallas_call | solution.py:346
  88.8 0.9 copy-done.11
  92.0 19.6 %all_to_all.5 = f32[32,2,4]{2,1,0:T(2,128)S(1)} all-to-all(f32[32,2,4]{2,1,0:T(2,128)S(1)} %copy.54), channel_id=1, replica_groups=mesh['group'=8,'shard'=32] {'shard'}, dimensions={0} | all-to-all | bytes 2048 | tf_op jit(solution)/shard_map/all_to_all | solution.py:523
  112.1 10.5 %collective-permute-done.26.c3.refs_3_ = bf16[64,48,128]{2,1,0:T(8,128)(2,1)} collective-permute-done((bf16[64,48,128]{2,1,0:T(8,128)(2,1)}, bf16[64,48,128]{2,1,0:T(8,128)(2,1)}, u32[]{:S(2)}, u32[]{:S(2)}) %collective-permute-start.26) | collective-permute-done | bytes 786464 | tf_op jit(solution)/shard_map/ppermute | solution.py:452
  122.5 3.7 %collective-permute-start.27 = (f32[8,128]{1,0:T(8,128)S(1)}, f32[8,128]{1,0:T(8,128)S(1)}, u32[]{:S(2)}, u32[]{:S(2)}) collective-permute-start(f32[8,128]{1,0:T(8,128)S(1)} %hold.9), channel_id=1, source_target_pairs={{0,0},{64,32},{128,64},{192,96},{32,128},{96,160},{160,192},{224,2... | collective-permute-start | bytes 12296 | tf_op jit(solution)/shard_map/ppermute | solution.py:527
  126.3 7.9 %finish.1 = bf16[4,16,32,768]{3,2,1,0:T(8,128)(2,1)} custom-call(s32[1]{0:T(128)} %bitcast.x_ref, bf16[64,48,128]{2,1,0:T(8,128)(2,1)} %copy-done.11, bf16[64,48,128]{2,1,0:T(8,128)(2,1)} %collective-permute-done.24.c1.refs_1_, bf16[64,48,128]{2,1,0:T(8,128)(2,1)} %collective-permute-done.25.c2.refs_2_, ...), custom_call_target="tpu_custom_call" | custom-call | tf_op jit(solution)/shard_map/finish/pallas_call | solution.py:398
  (125 shorter events, 14.1 us)
Async XLA Ops:
  3.8 12.7 %collective-permute-start = (bf16[400,128]{1,0:T(8,128)(2,1)S(1)}, bf16[400,128]{1,0:T(8,128)(2,1)S(1)}, u32[]{:S(2)}, u32[]{:S(2)}) collective-permute-start(bf16[400,128]{1,0:T(8,128)(2,1)S(1)} %get-tuple-element.26), channel_id=1, source_target_pairs={{0,0},{1,1},{2,2},{3,3},{4,4},{5,5},{6,6},{7,7},{8,8},{9,9},{10,10... | collective-permute-start | bytes 307208 | tf_op jit(solution)/shard_map/ppermute | solution.py:460
  8.3 8.2 %collective-permute-start.1 = (bf16[400,128]{1,0:T(8,128)(2,1)S(1)}, bf16[400,128]{1,0:T(8,128)(2,1)S(1)}, u32[]{:S(2)}, u32[]{:S(2)}) collective-permute-start(bf16[400,128]{1,0:T(8,128)(2,1)S(1)} %get-tuple-element.26), channel_id=1, source_target_pairs={{0,8},{1,9},{2,10},{3,11},{4,12},{5,13},{6,14},{7,15},{8,16},{9,17... | collective-permute-start | bytes 307208 | tf_op jit(solution)/shard_map/ppermute | solution.py:460
  10.9 8.0 %collective-permute-start.2 = (bf16[400,128]{1,0:T(8,128)(2,1)S(1)}, bf16[400,128]{1,0:T(8,128)(2,1)S(1)}, u32[]{:S(2)}, u32[]{:S(2)}) collective-permute-start(bf16[400,128]{1,0:T(8,128)(2,1)S(1)} %get-tuple-element.26), channel_id=1, source_target_pairs={{0,16},{1,17},{2,18},{3,19},{4,20},{5,21},{6,22},{7,23},{8,24},{9,... | collective-permute-start | bytes 307208 | tf_op jit(solution)/shard_map/ppermute | solution.py:460
  13.3 6.5 %collective-permute-start.3 = (bf16[400,128]{1,0:T(8,128)(2,1)S(1)}, bf16[400,128]{1,0:T(8,128)(2,1)S(1)}, u32[]{:S(2)}, u32[]{:S(2)}) collective-permute-start(bf16[400,128]{1,0:T(8,128)(2,1)S(1)} %get-tuple-element.26), channel_id=1, source_target_pairs={{0,24},{1,25},{2,26},{3,27},{4,28},{5,29},{6,30},{7,31},{8,0},{9,1... | collective-permute-start | bytes 307208 | tf_op jit(solution)/shard_map/ppermute | solution.py:460
  19.8 16.1 %collective-permute-start.4 = (bf16[4,400,128]{2,1,0:T(8,128)(2,1)S(1)}, bf16[4,400,128]{2,1,0:T(8,128)(2,1)}, u32[]{:S(2)}, u32[]{:S(2)}) collective-permute-start(bf16[4,400,128]{2,1,0:T(8,128)(2,1)S(1)} %pad_maximum_fusion.refs_0_), channel_id=1, source_target_pairs={{0,1},{1,2},{2,3},{3,4},{4,5},{5,6},{6,7},{7,0},{8,9},{9,10},{10,1... | collective-permute-start | bytes 1228808 | tf_op jit(solution)/shard_map/ppermute | solution.py:449
  21.6 16.5 %collective-permute-start.5 = (bf16[4,400,128]{2,1,0:T(8,128)(2,1)S(1)}, bf16[4,400,128]{2,1,0:T(8,128)(2,1)}, u32[]{:S(2)}, u32[]{:S(2)}) collective-permute-start(bf16[4,400,128]{2,1,0:T(8,128)(2,1)S(1)} %pad_maximum_fusion.refs_0_), channel_id=1, source_target_pairs={{0,7},{1,0},{2,1},{3,2},{4,3},{5,4},{6,5},{7,6},{8,15},{9,8},{10,9... | collective-permute-start | bytes 1228808 | tf_op jit(solution)/shard_map/ppermute | solution.py:449
  25.7 3.9 %collective-permute-start.8 = (bf16[144,256]{1,0:T(8,128)(2,1)S(1)}, bf16[144,256]{1,0:T(8,128)(2,1)S(1)}, u32[]{:S(2)}, u32[]{:S(2)}) collective-permute-start(bf16[144,256]{1,0:T(8,128)(2,1)S(1)} %get-tuple-element.32), channel_id=1, source_target_pairs={{0,192},{32,224},{64,0},{96,32},{128,64},{160,96},{192,128},{224,1... | collective-permute-start | bytes 221192 | tf_op jit(solution)/shard_map/ppermute | solution.py:452
  25.7 4.8 %collective-permute-start.9 = (bf16[144,256]{1,0:T(8,128)(2,1)S(1)}, bf16[144,256]{1,0:T(8,128)(2,1)S(1)}, u32[]{:S(2)}, u32[]{:S(2)}) collective-permute-start(bf16[144,256]{1,0:T(8,128)(2,1)S(1)} %get-tuple-element.33), channel_id=1, source_target_pairs={{0,128},{32,160},{64,192},{96,224},{128,0},{160,32},{192,64},{224,... | collective-permute-start | bytes 221192 | tf_op jit(solution)/shard_map/ppermute | solution.py:452
  27.8 4.4 %collective-permute-start.10 = (bf16[144,256]{1,0:T(8,128)(2,1)S(1)}, bf16[144,256]{1,0:T(8,128)(2,1)S(1)}, u32[]{:S(2)}, u32[]{:S(2)}) collective-permute-start(bf16[144,256]{1,0:T(8,128)(2,1)S(1)} %get-tuple-element.34), channel_id=1, source_target_pairs={{0,64},{32,96},{64,128},{96,160},{128,192},{160,224},{192,0},{224,... | collective-permute-start | bytes 221192 | tf_op jit(solution)/shard_map/ppermute | solution.py:452
  32.4 9.4 %collective-permute-start.11 = (bf16[4,400,128]{2,1,0:T(8,128)(2,1)S(1)}, bf16[4,400,128]{2,1,0:T(8,128)(2,1)S(1)}, u32[]{:S(2)}, u32[]{:S(2)}) collective-permute-start(bf16[4,400,128]{2,1,0:T(8,128)(2,1)S(1)} %hold.5.refs_0_), channel_id=1, source_target_pairs={{0,32},{32,0},{64,96},{96,64},{128,160},{160,128},{192,224},{224,1... | collective-permute-start | bytes 1228808 | tf_op jit(solution)/shard_map/ppermute | solution.py:452
  35.9 6.6 %collective-permute-start.12 = (bf16[4,400,128]{2,1,0:T(8,128)(2,1)}, bf16[4,400,128]{2,1,0:T(8,128)(2,1)}, u32[]{:S(2)}, u32[]{:S(2)}) collective-permute-start(bf16[4,400,128]{2,1,0:T(8,128)(2,1)} %collective-permute-done.4.refs_1_), channel_id=1, source_target_pairs={{0,32},{32,0},{64,96},{96,64},{128,160},{160,128},{192,224},{224,1... | collective-permute-start | bytes 1228808 | tf_op jit(solution)/shard_map/ppermute | solution.py:452
  38.0 12.7 %collective-permute-start.6 = (bf16[4,400,128]{2,1,0:T(8,128)(2,1)}, bf16[4,400,128]{2,1,0:T(8,128)(2,1)S(1)}, u32[]{:S(2)}, u32[]{:S(2)}) collective-permute-start(bf16[4,400,128]{2,1,0:T(8,128)(2,1)} %collective-permute-done.4.refs_1_), channel_id=1, source_target_pairs={{0,1},{1,2},{2,3},{3,4},{4,5},{5,6},{6,7},{7,0},{8,9},{9,10},{10,1... | collective-permute-start | bytes 1228808 | tf_op jit(solution)/shard_map/ppermute | solution.py:449
  38.0 12.7 %collective-permute-start.7 = (bf16[4,400,128]{2,1,0:T(8,128)(2,1)}, bf16[4,400,128]{2,1,0:T(8,128)(2,1)S(1)}, u32[]{:S(2)}, u32[]{:S(2)}) collective-permute-start(bf16[4,400,128]{2,1,0:T(8,128)(2,1)} %collective-permute-done.5.refs_0_.refs_2_), channel_id=1, source_target_pairs={{0,7},{1,0},{2,1},{3,2},{4,3},{5,4},{6,5},{7,6},{8,15},{9,8},{10,9... | collective-permute-start | bytes 1228808 | tf_op jit(solution)/shard_map/ppermute | solution.py:449
  40.7 13.5 %collective-permute-start.15 = (bf16[4,400,128]{2,1,0:T(8,128)(2,1)}, bf16[4,400,128]{2,1,0:T(8,128)(2,1)S(1)}, u32[]{:S(2)}, u32[]{:S(2)}) collective-permute-start(bf16[4,400,128]{2,1,0:T(8,128)(2,1)} %collective-permute-done.5.refs_0_.refs_2_), channel_id=1, source_target_pairs={{0,32},{32,0},{64,96},{96,64},{128,160},{160,128},{192,224},{224,1... | collective-permute-start | bytes 1228808 | tf_op jit(solution)/shard_map/ppermute | solution.py:452
  50.7 12.9 %copy-start.7 = (bf16[4,400,128]{2,1,0:T(8,128)(2,1)}, bf16[4,400,128]{2,1,0:T(8,128)(2,1)S(1)}, u32[]{:S(2)}) copy-start(bf16[4,400,128]{2,1,0:T(8,128)(2,1)S(1)} %get-tuple-element.35.refs_1_.refs_3_) | copy-start | bytes 1228804
  50.8 12.9 %copy-start.9 = (bf16[4,400,128]{2,1,0:T(8,128)(2,1)}, bf16[4,400,128]{2,1,0:T(8,128)(2,1)S(1)}, u32[]{:S(2)}) copy-start(bf16[4,400,128]{2,1,0:T(8,128)(2,1)S(1)} %get-tuple-element.36.refs_2_.refs_4_) | copy-start | bytes 1228804
  50.8 3.5 %collective-permute-start.16 = (bf16[4,400,128]{2,1,0:T(8,128)(2,1)S(1)}, bf16[4,400,128]{2,1,0:T(8,128)(2,1)S(1)}, u32[]{:S(2)}, u32[]{:S(2)}) collective-permute-start(bf16[4,400,128]{2,1,0:T(8,128)(2,1)S(1)} %get-tuple-element.35.refs_1_.refs_3_), channel_id=1, source_target_pairs={{0,32},{32,0},{64,96},{96,64},{128,160},{160,128},{192,224},{224,1... | collective-permute-start | bytes 1228808 | tf_op jit(solution)/shard_map/ppermute | solution.py:452
  51.4 2.8 %collective-permute-start.17 = (bf16[4,400,128]{2,1,0:T(8,128)(2,1)S(1)}, bf16[4,400,128]{2,1,0:T(8,128)(2,1)S(1)}, u32[]{:S(2)}, u32[]{:S(2)}) collective-permute-start(bf16[4,400,128]{2,1,0:T(8,128)(2,1)S(1)} %get-tuple-element.36.refs_2_.refs_4_), channel_id=1, source_target_pairs={{0,32},{32,0},{64,96},{96,64},{128,160},{160,128},{192,224},{224,1... | collective-permute-start | bytes 1228808 | tf_op jit(solution)/shard_map/ppermute | solution.py:452
  51.5 12.1 %collective-permute-start.13 = (bf16[4,400,128]{2,1,0:T(8,128)(2,1)S(1)}, bf16[4,400,128]{2,1,0:T(8,128)(2,1)S(1)}, u32[]{:S(2)}, u32[]{:S(2)}) collective-permute-start(bf16[4,400,128]{2,1,0:T(8,128)(2,1)S(1)} %get-tuple-element.35.refs_1_.refs_3_), channel_id=1, source_target_pairs={{0,1},{1,2},{2,3},{3,4},{4,5},{5,6},{6,7},{7,0},{8,9},{9,10},{10,1... | collective-permute-start | bytes 1228808 | tf_op jit(solution)/shard_map/ppermute | solution.py:449
  51.5 12.1 %collective-permute-start.14 = (bf16[4,400,128]{2,1,0:T(8,128)(2,1)S(1)}, bf16[4,400,128]{2,1,0:T(8,128)(2,1)S(1)}, u32[]{:S(2)}, u32[]{:S(2)}) collective-permute-start(bf16[4,400,128]{2,1,0:T(8,128)(2,1)S(1)} %get-tuple-element.36.refs_2_.refs_4_), channel_id=1, source_target_pairs={{0,7},{1,0},{2,1},{3,2},{4,3},{5,4},{6,5},{7,6},{8,15},{9,8},{10,9... | collective-permute-start | bytes 1228808 | tf_op jit(solution)/shard_map/ppermute | solution.py:449
  63.7 10.8 %copy-start = (bf16[4,400,128]{2,1,0:T(8,128)(2,1)}, bf16[4,400,128]{2,1,0:T(8,128)(2,1)S(1)}, u32[]{:S(2)}) copy-start(bf16[4,400,128]{2,1,0:T(8,128)(2,1)S(1)} %get-tuple-element.38.refs_0_.refs_5_) | copy-start | bytes 1228804
  63.7 10.8 %copy-start.2 = (bf16[4,400,128]{2,1,0:T(8,128)(2,1)}, bf16[4,400,128]{2,1,0:T(8,128)(2,1)S(1)}, u32[]{:S(2)}) copy-start(bf16[4,400,128]{2,1,0:T(8,128)(2,1)S(1)} %get-tuple-element.39.refs_1_.refs_6_) | copy-start | bytes 1228804
  63.7 3.9 %collective-permute-start.20 = (bf16[4,400,128]{2,1,0:T(8,128)(2,1)S(1)}, bf16[4,400,128]{2,1,0:T(8,128)(2,1)S(1)}, u32[]{:S(2)}, u32[]{:S(2)}) collective-permute-start(bf16[4,400,128]{2,1,0:T(8,128)(2,1)S(1)} %get-tuple-element.38.refs_0_.refs_5_), channel_id=1, source_target_pairs={{0,32},{32,0},{64,96},{96,64},{128,160},{160,128},{192,224},{224,1... | collective-permute-start | bytes 1228808 | tf_op jit(solution)/shard_map/ppermute | solution.py:452
  64.7 2.9 %collective-permute-start.21 = (bf16[4,400,128]{2,1,0:T(8,128)(2,1)S(1)}, bf16[4,400,128]{2,1,0:T(8,128)(2,1)S(1)}, u32[]{:S(2)}, u32[]{:S(2)}) collective-permute-start(bf16[4,400,128]{2,1,0:T(8,128)(2,1)S(1)} %get-tuple-element.39.refs_1_.refs_6_), channel_id=1, source_target_pairs={{0,32},{32,0},{64,96},{96,64},{128,160},{160,128},{192,224},{224,1... | collective-permute-start | bytes 1228808 | tf_op jit(solution)/shard_map/ppermute | solution.py:452
  64.9 9.6 %collective-permute-start.18 = (bf16[2,400,128]{2,1,0:T(8,128)(2,1)S(1)}, bf16[2,400,128]{2,1,0:T(8,128)(2,1)}, u32[]{:S(2)}, u32[]{:S(2)}) collective-permute-start(bf16[2,400,128]{2,1,0:T(8,128)(2,1)S(1)} %slice.32), channel_id=1, source_target_pairs={{0,1},{1,2},{2,3},{3,4},{4,5},{5,6},{6,7},{7,0},{8,9},{9,10},{10,1... | collective-permute-start | bytes 614408 | tf_op jit(solution)/shard_map/ppermute | solution.py:449
  67.1 7.3 %collective-permute-start.19 = (bf16[2,400,128]{2,1,0:T(8,128)(2,1)S(1)}, bf16[2,400,128]{2,1,0:T(8,128)(2,1)}, u32[]{:S(2)}, u32[]{:S(2)}) collective-permute-start(bf16[2,400,128]{2,1,0:T(8,128)(2,1)S(1)} %slice.33), channel_id=1, source_target_pairs={{0,7},{1,0},{2,1},{3,2},{4,3},{5,4},{6,5},{7,6},{8,15},{9,8},{10,9... | collective-permute-start | bytes 614408 | tf_op jit(solution)/shard_map/ppermute | solution.py:449
  74.5 2.5 %collective-permute-start.22 = (bf16[2,400,128]{2,1,0:T(8,128)(2,1)}, bf16[2,400,128]{2,1,0:T(8,128)(2,1)}, u32[]{:S(2)}, u32[]{:S(2)}) collective-permute-start(bf16[2,400,128]{2,1,0:T(8,128)(2,1)} %get-tuple-element.41.refs_0_.refs_7_), channel_id=1, source_target_pairs={{0,32},{32,0},{64,96},{96,64},{128,160},{160,128},{192,224},{224,1... | collective-permute-start | bytes 614408 | tf_op jit(solution)/shard_map/ppermute | solution.py:452
  75.5 1.8 %collective-permute-start.23 = (bf16[2,400,128]{2,1,0:T(8,128)(2,1)}, bf16[2,400,128]{2,1,0:T(8,128)(2,1)}, u32[]{:S(2)}, u32[]{:S(2)}) collective-permute-start(bf16[2,400,128]{2,1,0:T(8,128)(2,1)} %get-tuple-element.42.refs_1_.refs_8_), channel_id=1, source_target_pairs={{0,32},{32,0},{64,96},{96,64},{128,160},{160,128},{192,224},{224,1... | collective-permute-start | bytes 614408 | tf_op jit(solution)/shard_map/ppermute | solution.py:452
  83.8 28.3 %collective-permute-start.24 = (bf16[64,48,128]{2,1,0:T(8,128)(2,1)}, bf16[64,48,128]{2,1,0:T(8,128)(2,1)}, u32[]{:S(2)}, u32[]{:S(2)}) collective-permute-start(bf16[64,48,128]{2,1,0:T(8,128)(2,1)} %get-tuple-element.46), channel_id=1, source_target_pairs={{0,192},{32,224},{64,0},{96,32},{128,64},{160,96},{192,128},{224,1... | collective-permute-start | bytes 2359304 | tf_op jit(solution)/shard_map/ppermute | solution.py:452
  84.4 27.7 %collective-permute-start.25 = (bf16[64,48,128]{2,1,0:T(8,128)(2,1)}, bf16[64,48,128]{2,1,0:T(8,128)(2,1)}, u32[]{:S(2)}, u32[]{:S(2)}) collective-permute-start(bf16[64,48,128]{2,1,0:T(8,128)(2,1)} %get-tuple-element.47), channel_id=1, source_target_pairs={{0,128},{32,160},{64,192},{96,224},{128,0},{160,32},{192,64},{224,... | collective-permute-start | bytes 2359304 | tf_op jit(solution)/shard_map/ppermute | solution.py:452
  85.9 36.6 %collective-permute-start.26 = (bf16[64,48,128]{2,1,0:T(8,128)(2,1)}, bf16[64,48,128]{2,1,0:T(8,128)(2,1)}, u32[]{:S(2)}, u32[]{:S(2)}) collective-permute-start(bf16[64,48,128]{2,1,0:T(8,128)(2,1)} %get-tuple-element.48), channel_id=1, source_target_pairs={{0,64},{32,96},{64,128},{96,160},{128,192},{160,224},{192,0},{224,... | collective-permute-start | bytes 2359304 | tf_op jit(solution)/shard_map/ppermute | solution.py:452
  122.5 11.7 %collective-permute-start.27 = (f32[8,128]{1,0:T(8,128)S(1)}, f32[8,128]{1,0:T(8,128)S(1)}, u32[]{:S(2)}, u32[]{:S(2)}) collective-permute-start(f32[8,128]{1,0:T(8,128)S(1)} %hold.9), channel_id=1, source_target_pairs={{0,0},{64,32},{128,64},{192,96},{32,128},{96,160},{160,192},{224,2... | collective-permute-start | bytes 12296 | tf_op jit(solution)/shard_map/ppermute | solution.py:527
  (21 other events, 95.7 us)

commit v5 on v4

--- a/solution.py
+++ b/solution.py
@@ -262,7 +262,7 @@
     images = sum(sizes)
     fresh = context is None
     vmem, anywhere = pl.BlockSpec(memory_space=pltpu.VMEM), pl.BlockSpec(memory_space=pl.ANY)
-    pieces = [*own, *[in_hbm(part) for part in other]]
+    pieces = [*own, *other]
     operands = [in_hbm(plan), in_hbm(query), *pieces] + ([] if fresh else [context])
     parts = PARTS if final else ()
     outs = pl.pallas_call(
@@ -503,6 +503,8 @@
                 waiting = [*hold([stack], received[1:]), *waiting[1:]]
             now, waiting = (waiting[:2], waiting[2:]) if step == 1 else (waiting, [])
             other = [along_group(part, 0, 1) for part in now]
+            if step not in (2, 3):
+                other = [in_hbm(part) for part in other]
             context, outs = attend(plan, first_image, query, now, other, context, step == 4)
             first_image += sum(part.shape[0] for part in now)
         if step < 4:

time: 136 us -> 135 us (level)
  waiting for transfers between devices: 18.8 us -> 21.2 us
  local copies, waits for them, and re-layouts: 10.3 us -> 8.51 us
    unnamed x52 -> x42, local copies, waits for them, and re-layouts: 6.85 us -> 4.98 us
  transfers between devices with their start and end apart: 28 -> 28, of which waited for: 8 -> 9; matrix products, arithmetic and copies ran while one was open for 4% -> 4% of each run, Pallas kernels for 24% -> 24%
where the time goes in v5:
time: 135 us
  starting transfers between devices  41.6 us (31%)
  Pallas kernels  41.5 us (31%)
  waiting for transfers between devices  21.2 us (16%)
  blocking collectives  18.5 us (14%)
  local copies, waits for them, and re-layouts  8.51 us (6%)
  other arithmetic  2.16 us (2%)
    pallas_call x4, Pallas kernels, attend(): pl.pallas_call(functools.partial(attend_kernel, sizes, first_image, 5, fr...  28 us
    all_to_all x1, blocking collectives, on_device(): lax.all_to_all(partial, 'shard', split_axis=0, concat_axis=0, tiled=True)  18.5 us
    ppermute x15, waiting for transfers between devices, along_group(): return lax.ppermute(value, 'group', group_moves(dx, flip))  16.7 us
    ppermute x8, starting transfers between devices, along_shard(): return lax.ppermute(value, 'shard', grid_moves(dy, dz))  13.8 us
    ppermute x15, starting transfers between devices, along_group(): return lax.ppermute(value, 'group', group_moves(dx, flip))  12.1 us
    ppermute x4, starting transfers between devices, homeward(): return lax.ppermute(block, ('group', 'shard'), moves)  11.9 us
    pallas_call x1, Pallas kernels, finish(): pl.pallas_call(finish_kernel, out_shape=jax.ShapeDtypeStruct((4, 16, NQ,...  7.91 us
    unnamed x42, local copies, waits for them, and re-layouts  4.98 us
  transfers between devices with their start and end apart: 28, of which 9 were waited for; matrix products, arithmetic and copies ran while one was open for 4% of the time, Pallas kernels for 24%

profile of v5, /device:TPU:1, one launch (start us, length us, event | category | flops | bytes accessed | tf_op | source)
XLA Modules:
  0.0 134.6 jit_solution(5283346260621296811)
XLA Ops:
  0.6 3.2 %opening.1 = (bf16[400,128]{1,0:T(8,128)(2,1)S(1)}, bf16[144,256]{1,0:T(8,128)(2,1)S(1)}, bf16[144,256]{1,0:T(8,128)(2,1)S(1)}, bf16[144,256]{1,0:T(8,128)(2,1)S(1)}, bf16[144,256]{1,0:T(8,128)(2,1)S(1)}) custom-call(s32[1]{0:T(128)} %bitcast.2.group_ref, bf16[1,257,1408]{2,1,0:T(8,128)(2,1)} %refs_0_.1, bf16[192,1408]{1,0:T(8,128)(2,1)} %bitcast.71, ...), custom_call_target="tpu_custom_call" | custom-call | tf_op jit(solution)/shard_map/opening/pallas_call | solution.py:89
  3.8 4.5 %collective-permute-start = (bf16[400,128]{1,0:T(8,128)(2,1)S(1)}, bf16[400,128]{1,0:T(8,128)(2,1)S(1)}, u32[]{:S(2)}, u32[]{:S(2)}) collective-permute-start(bf16[400,128]{1,0:T(8,128)(2,1)S(1)} %get-tuple-element.26), channel_id=1, source_target_pairs={{0,0},{1,1},{2,2},{3,3},{4,4},{5,5},{6,6},{7,7},{8,8},{9,9},{10,10... | collective-permute-start | bytes 307208 | tf_op jit(solution)/shard_map/ppermute | solution.py:460
  8.3 2.6 %collective-permute-start.1 = (bf16[400,128]{1,0:T(8,128)(2,1)S(1)}, bf16[400,128]{1,0:T(8,128)(2,1)S(1)}, u32[]{:S(2)}, u32[]{:S(2)}) collective-permute-start(bf16[400,128]{1,0:T(8,128)(2,1)S(1)} %get-tuple-element.26), channel_id=1, source_target_pairs={{0,8},{1,9},{2,10},{3,11},{4,12},{5,13},{6,14},{7,15},{8,16},{9,17... | collective-permute-start | bytes 307208 | tf_op jit(solution)/shard_map/ppermute | solution.py:460
  10.9 2.3 %collective-permute-start.2 = (bf16[400,128]{1,0:T(8,128)(2,1)S(1)}, bf16[400,128]{1,0:T(8,128)(2,1)S(1)}, u32[]{:S(2)}, u32[]{:S(2)}) collective-permute-start(bf16[400,128]{1,0:T(8,128)(2,1)S(1)} %get-tuple-element.26), channel_id=1, source_target_pairs={{0,16},{1,17},{2,18},{3,19},{4,20},{5,21},{6,22},{7,23},{8,24},{9,... | collective-permute-start | bytes 307208 | tf_op jit(solution)/shard_map/ppermute | solution.py:460
  13.3 2.5 %collective-permute-start.3 = (bf16[400,128]{1,0:T(8,128)(2,1)S(1)}, bf16[400,128]{1,0:T(8,128)(2,1)S(1)}, u32[]{:S(2)}, u32[]{:S(2)}) collective-permute-start(bf16[400,128]{1,0:T(8,128)(2,1)S(1)} %get-tuple-element.26), channel_id=1, source_target_pairs={{0,24},{1,25},{2,26},{3,27},{4,28},{5,29},{6,30},{7,31},{8,0},{9,1... | collective-permute-start | bytes 307208 | tf_op jit(solution)/shard_map/ppermute | solution.py:460
  16.5 2.4 %collective-permute-done.2 = bf16[400,128]{1,0:T(8,128)(2,1)S(1)} collective-permute-done((bf16[400,128]{1,0:T(8,128)(2,1)S(1)}, bf16[400,128]{1,0:T(8,128)(2,1)S(1)}, u32[]{:S(2)}, u32[]{:S(2)}) %collective-permute-start.2) | collective-permute-done | bytes 102432 | tf_op jit(solution)/shard_map/ppermute | solution.py:460
  19.8 1.7 %collective-permute-start.4 = (bf16[4,400,128]{2,1,0:T(8,128)(2,1)S(1)}, bf16[4,400,128]{2,1,0:T(8,128)(2,1)}, u32[]{:S(2)}, u32[]{:S(2)}) collective-permute-start(bf16[4,400,128]{2,1,0:T(8,128)(2,1)S(1)} %pad_maximum_fusion.refs_0_), channel_id=1, source_target_pairs={{0,1},{1,2},{2,3},{3,4},{4,5},{5,6},{6,7},{7,0},{8,9},{9,10},{10,1... | collective-permute-start | bytes 1228808 | tf_op jit(solution)/shard_map/ppermute | solution.py:449
  21.6 4.0 %collective-permute-start.5 = (bf16[4,400,128]{2,1,0:T(8,128)(2,1)S(1)}, bf16[4,400,128]{2,1,0:T(8,128)(2,1)}, u32[]{:S(2)}, u32[]{:S(2)}) collective-permute-start(bf16[4,400,128]{2,1,0:T(8,128)(2,1)S(1)} %pad_maximum_fusion.refs_0_), channel_id=1, source_target_pairs={{0,7},{1,0},{2,1},{3,2},{4,3},{5,4},{6,5},{7,6},{8,15},{9,8},{10,9... | collective-permute-start | bytes 1228808 | tf_op jit(solution)/shard_map/ppermute | solution.py:449
  25.7 2.1 %collective-permute-start.9 = (bf16[144,256]{1,0:T(8,128)(2,1)S(1)}, bf16[144,256]{1,0:T(8,128)(2,1)S(1)}, u32[]{:S(2)}, u32[]{:S(2)}) collective-permute-start(bf16[144,256]{1,0:T(8,128)(2,1)S(1)} %get-tuple-element.33), channel_id=1, source_target_pairs={{0,128},{32,160},{64,192},{96,224},{128,0},{160,32},{192,64},{224,... | collective-permute-start | bytes 221192 | tf_op jit(solution)/shard_map/ppermute | solution.py:452
  27.9 1.6 %collective-permute-done.8.q1.refs_1_ = bf16[144,256]{1,0:T(8,128)(2,1)S(1)} collective-permute-done((bf16[144,256]{1,0:T(8,128)(2,1)S(1)}, bf16[144,256]{1,0:T(8,128)(2,1)S(1)}, u32[]{:S(2)}, u32[]{:S(2)}) %collective-permute-start.8) | collective-permute-done | bytes 73760 | tf_op jit(solution)/shard_map/ppermute | solution.py:452
  29.5 1.0 collective-permute-done.9.q2.refs_2_
  30.7 1.5 %collective-permute-done.10.q3.refs_3_ = bf16[144,256]{1,0:T(8,128)(2,1)S(1)} collective-permute-done((bf16[144,256]{1,0:T(8,128)(2,1)S(1)}, bf16[144,256]{1,0:T(8,128)(2,1)S(1)}, u32[]{:S(2)}, u32[]{:S(2)}) %collective-permute-start.10) | collective-permute-done | bytes 73760 | tf_op jit(solution)/shard_map/ppermute | solution.py:452
  32.4 3.3 %collective-permute-start.11 = (bf16[4,400,128]{2,1,0:T(8,128)(2,1)S(1)}, bf16[4,400,128]{2,1,0:T(8,128)(2,1)S(1)}, u32[]{:S(2)}, u32[]{:S(2)}) collective-permute-start(bf16[4,400,128]{2,1,0:T(8,128)(2,1)S(1)} %hold.5.refs_0_), channel_id=1, source_target_pairs={{0,32},{32,0},{64,96},{96,64},{128,160},{160,128},{192,224},{224,1... | collective-permute-start | bytes 1228808 | tf_op jit(solution)/shard_map/ppermute | solution.py:452
  38.1 2.7 %collective-permute-start.7 = (bf16[4,400,128]{2,1,0:T(8,128)(2,1)}, bf16[4,400,128]{2,1,0:T(8,128)(2,1)S(1)}, u32[]{:S(2)}, u32[]{:S(2)}) collective-permute-start(bf16[4,400,128]{2,1,0:T(8,128)(2,1)} %collective-permute-done.5.refs_0_.refs_2_), channel_id=1, source_target_pairs={{0,7},{1,0},{2,1},{3,2},{4,3},{5,4},{6,5},{7,6},{8,15},{9,8},{10,9... | collective-permute-start | bytes 1228808 | tf_op jit(solution)/shard_map/ppermute | solution.py:449
  40.7 1.1 collective-permute-start.15
  42.6 1.0 copy-done.6
  43.6 7.2 %attend.4.refs_2_ = bf16[256,48,128]{2,1,0:T(8,128)(2,1)S(1)} custom-call(s32[512]{0:T(512)} %concatenate.4.plan_ref, bf16[3,2,16,32,128]{4,3,2,1,0:T(8,128)(2,1)} %copy-done.12, bf16[4,400,128]{2,1,0:T(8,128)(2,1)S(1)} %copy-done.6, bf16[4,400,128]{2,1,0:T(8,128)(2,1)} %collective-permute-done.4.refs_1_, bf16[4,400,128]{2,1,0:T(8,128)(2,1)} %copy-done.19, ...), custom_call_target="tpu_custom_call" | custom-call | flops 4800000000 | bytes 6400000 | tf_op jit(solution)/shard_map/attend/pallas_call | solution.py:268
  51.6 2.7 %collective-permute-start.14 = (bf16[4,400,128]{2,1,0:T(8,128)(2,1)S(1)}, bf16[4,400,128]{2,1,0:T(8,128)(2,1)S(1)}, u32[]{:S(2)}, u32[]{:S(2)}) collective-permute-start(bf16[4,400,128]{2,1,0:T(8,128)(2,1)S(1)} %get-tuple-element.36.refs_2_.refs_4_), channel_id=1, source_target_pairs={{0,7},{1,0},{2,1},{3,2},{4,3},{5,4},{6,5},{7,6},{8,15},{9,8},{10,9... | collective-permute-start | bytes 1228808 | tf_op jit(solution)/shard_map/ppermute | solution.py:449
  54.2 7.9 %attend.5.refs_2_ = bf16[256,48,128]{2,1,0:T(8,128)(2,1)S(1)} custom-call(s32[512]{0:T(512)} %concatenate.4.plan_ref, bf16[3,2,16,32,128]{4,3,2,1,0:T(8,128)(2,1)} %copy-done.12, bf16[4,400,128]{2,1,0:T(8,128)(2,1)} %collective-permute-done.5.refs_0_.refs_2_, ...), custom_call_target="tpu_custom_call", output_to_operand_aliasing={{}: (8, {})} | custom-call | flops 7200000000 | bytes 9600000 | tf_op jit(solution)/shard_map/attend/pallas_call | solution.py:268
  62.1 1.3 collective-permute-done.13.refs_0_
  63.4 1.3 collective-permute-start.20
  64.9 2.3 %collective-permute-start.18 = (bf16[2,400,128]{2,1,0:T(8,128)(2,1)S(1)}, bf16[2,400,128]{2,1,0:T(8,128)(2,1)}, u32[]{:S(2)}, u32[]{:S(2)}) collective-permute-start(bf16[2,400,128]{2,1,0:T(8,128)(2,1)S(1)} %slice.32), channel_id=1, source_target_pairs={{0,1},{1,2},{2,3},{3,4},{4,5},{5,6},{6,7},{7,0},{8,9},{9,10},{10,1... | collective-permute-start | bytes 614408 | tf_op jit(solution)/shard_map/ppermute | solution.py:449
  67.6 6.6 %attend.6.refs_2_ = bf16[256,48,128]{2,1,0:T(8,128)(2,1)S(1)} custom-call(s32[512]{0:T(512)} %concatenate.4.plan_ref, bf16[3,2,16,32,128]{4,3,2,1,0:T(8,128)(2,1)} %copy-done.12, bf16[4,400,128]{2,1,0:T(8,128)(2,1)S(1)} %get-tuple-element.38.refs_0_.refs_5_, ...), custom_call_target="tpu_custom_call", output_to_operand_aliasing={{}: (6, {})} | custom-call | flops 4800000000 | bytes 6400000 | tf_op jit(solution)/shard_map/attend/pallas_call | solution.py:268
  74.3 1.1 collective-permute-start.22
  77.2 6.4 %attend.7 = (bf16[256,48,128]{2,1,0:T(8,128)(2,1)S(1)}, bf16[64,48,128]{2,1,0:T(8,128)(2,1)}, bf16[64,48,128]{2,1,0:T(8,128)(2,1)}, bf16[64,48,128]{2,1,0:T(8,128)(2,1)}) custom-call(s32[512]{0:T(512)} %concatenate.4.plan_ref, bf16[3,2,16,32,128]{4,3,2,1,0:T(8,128)(2,1)} %copy-done.12, ...), custom_call_target="tpu_custom_call", output_to_operand_aliasing={{0}: (6, {})} | custom-call | flops 2400000000 | bytes 3200000 | tf_op jit(solution)/shard_map/attend/pallas_call | solution.py:268
  84.2 1.5 %collective-permute-start.25 = (bf16[64,48,128]{2,1,0:T(8,128)(2,1)}, bf16[64,48,128]{2,1,0:T(8,128)(2,1)}, u32[]{:S(2)}, u32[]{:S(2)}) collective-permute-start(bf16[64,48,128]{2,1,0:T(8,128)(2,1)} %get-tuple-element.47), channel_id=1, source_target_pairs={{0,128},{32,160},{64,192},{96,224},{128,0},{160,32},{192,64},{224,... | collective-permute-start | bytes 2359304 | tf_op jit(solution)/shard_map/ppermute | solution.py:452
  86.5 2.2 %score.1 = (f32[2,128]{1,0:T(2,128)S(1)}, bf16[64,48,128]{2,1,0:T(8,128)(2,1)S(1)}) custom-call(s32[1]{0:T(128)} %bitcast.1.shard_ref, bf16[4,400,128]{2,1,0:T(8,128)(2,1)S(1)} %pad_maximum_fusion.refs_0_, bf16[4,400,128]{2,1,0:T(8,128)(2,1)} %collective-permute-done.4.refs_1_, bf16[4,400,128]{2,1,0:T(8,128)(2,1)} %collective-permute-done.5.refs_0_.refs_2_, ...), custom_call_target="tpu_custom_call" | custom-call | flops 1000 | bytes 1000 | tf_op jit(solution)/shard_map/score/pallas_call | solution.py:346
  88.7 0.9 copy-done.11
  91.9 18.5 %all_to_all.5 = f32[32,2,4]{2,1,0:T(2,128)S(1)} all-to-all(f32[32,2,4]{2,1,0:T(2,128)S(1)} %copy.54), channel_id=1, replica_groups=mesh['group'=8,'shard'=32] {'shard'}, dimensions={0} | all-to-all | bytes 2048 | tf_op jit(solution)/shard_map/all_to_all | solution.py:525
  110.8 11.5 %collective-permute-done.26.c3.refs_3_ = bf16[64,48,128]{2,1,0:T(8,128)(2,1)} collective-permute-done((bf16[64,48,128]{2,1,0:T(8,128)(2,1)}, bf16[64,48,128]{2,1,0:T(8,128)(2,1)}, u32[]{:S(2)}, u32[]{:S(2)}) %collective-permute-start.26) | collective-permute-done | bytes 786464 | tf_op jit(solution)/shard_map/ppermute | solution.py:452
  122.4 3.7 %collective-permute-start.27 = (f32[8,128]{1,0:T(8,128)S(1)}, f32[8,128]{1,0:T(8,128)S(1)}, u32[]{:S(2)}, u32[]{:S(2)}) collective-permute-start(f32[8,128]{1,0:T(8,128)S(1)} %hold.9), channel_id=1, source_target_pairs={{0,0},{64,32},{128,64},{192,96},{32,128},{96,160},{160,192},{224,2... | collective-permute-start | bytes 12296 | tf_op jit(solution)/shard_map/ppermute | solution.py:529
  126.1 7.9 %finish.1 = bf16[4,16,32,768]{3,2,1,0:T(8,128)(2,1)} custom-call(s32[1]{0:T(128)} %bitcast.x_ref, bf16[64,48,128]{2,1,0:T(8,128)(2,1)} %copy-done.11, bf16[64,48,128]{2,1,0:T(8,128)(2,1)} %collective-permute-done.24.c1.refs_1_, bf16[64,48,128]{2,1,0:T(8,128)(2,1)} %collective-permute-done.25.c2.refs_2_, ...), custom_call_target="tpu_custom_call" | custom-call | tf_op jit(solution)/shard_map/finish/pallas_call | solution.py:398
  (115 shorter events, 13.1 us)
Async XLA Ops:
  3.8 12.7 %collective-permute-start = (bf16[400,128]{1,0:T(8,128)(2,1)S(1)}, bf16[400,128]{1,0:T(8,128)(2,1)S(1)}, u32[]{:S(2)}, u32[]{:S(2)}) collective-permute-start(bf16[400,128]{1,0:T(8,128)(2,1)S(1)} %get-tuple-element.26), channel_id=1, source_target_pairs={{0,0},{1,1},{2,2},{3,3},{4,4},{5,5},{6,6},{7,7},{8,8},{9,9},{10,10... | collective-permute-start | bytes 307208 | tf_op jit(solution)/shard_map/ppermute | solution.py:460
  8.3 8.2 %collective-permute-start.1 = (bf16[400,128]{1,0:T(8,128)(2,1)S(1)}, bf16[400,128]{1,0:T(8,128)(2,1)S(1)}, u32[]{:S(2)}, u32[]{:S(2)}) collective-permute-start(bf16[400,128]{1,0:T(8,128)(2,1)S(1)} %get-tuple-element.26), channel_id=1, source_target_pairs={{0,8},{1,9},{2,10},{3,11},{4,12},{5,13},{6,14},{7,15},{8,16},{9,17... | collective-permute-start | bytes 307208 | tf_op jit(solution)/shard_map/ppermute | solution.py:460
  10.9 8.0 %collective-permute-start.2 = (bf16[400,128]{1,0:T(8,128)(2,1)S(1)}, bf16[400,128]{1,0:T(8,128)(2,1)S(1)}, u32[]{:S(2)}, u32[]{:S(2)}) collective-permute-start(bf16[400,128]{1,0:T(8,128)(2,1)S(1)} %get-tuple-element.26), channel_id=1, source_target_pairs={{0,16},{1,17},{2,18},{3,19},{4,20},{5,21},{6,22},{7,23},{8,24},{9,... | collective-permute-start | bytes 307208 | tf_op jit(solution)/shard_map/ppermute | solution.py:460
  13.3 6.5 %collective-permute-start.3 = (bf16[400,128]{1,0:T(8,128)(2,1)S(1)}, bf16[400,128]{1,0:T(8,128)(2,1)S(1)}, u32[]{:S(2)}, u32[]{:S(2)}) collective-permute-start(bf16[400,128]{1,0:T(8,128)(2,1)S(1)} %get-tuple-element.26), channel_id=1, source_target_pairs={{0,24},{1,25},{2,26},{3,27},{4,28},{5,29},{6,30},{7,31},{8,0},{9,1... | collective-permute-start | bytes 307208 | tf_op jit(solution)/shard_map/ppermute | solution.py:460
  19.8 16.1 %collective-permute-start.4 = (bf16[4,400,128]{2,1,0:T(8,128)(2,1)S(1)}, bf16[4,400,128]{2,1,0:T(8,128)(2,1)}, u32[]{:S(2)}, u32[]{:S(2)}) collective-permute-start(bf16[4,400,128]{2,1,0:T(8,128)(2,1)S(1)} %pad_maximum_fusion.refs_0_), channel_id=1, source_target_pairs={{0,1},{1,2},{2,3},{3,4},{4,5},{5,6},{6,7},{7,0},{8,9},{9,10},{10,1... | collective-permute-start | bytes 1228808 | tf_op jit(solution)/shard_map/ppermute | solution.py:449
  21.6 16.5 %collective-permute-start.5 = (bf16[4,400,128]{2,1,0:T(8,128)(2,1)S(1)}, bf16[4,400,128]{2,1,0:T(8,128)(2,1)}, u32[]{:S(2)}, u32[]{:S(2)}) collective-permute-start(bf16[4,400,128]{2,1,0:T(8,128)(2,1)S(1)} %pad_maximum_fusion.refs_0_), channel_id=1, source_target_pairs={{0,7},{1,0},{2,1},{3,2},{4,3},{5,4},{6,5},{7,6},{8,15},{9,8},{10,9... | collective-permute-start | bytes 1228808 | tf_op jit(solution)/shard_map/ppermute | solution.py:449
  25.7 3.9 %collective-permute-start.8 = (bf16[144,256]{1,0:T(8,128)(2,1)S(1)}, bf16[144,256]{1,0:T(8,128)(2,1)S(1)}, u32[]{:S(2)}, u32[]{:S(2)}) collective-permute-start(bf16[144,256]{1,0:T(8,128)(2,1)S(1)} %get-tuple-element.32), channel_id=1, source_target_pairs={{0,192},{32,224},{64,0},{96,32},{128,64},{160,96},{192,128},{224,1... | collective-permute-start | bytes 221192 | tf_op jit(solution)/shard_map/ppermute | solution.py:452
  25.7 4.8 %collective-permute-start.9 = (bf16[144,256]{1,0:T(8,128)(2,1)S(1)}, bf16[144,256]{1,0:T(8,128)(2,1)S(1)}, u32[]{:S(2)}, u32[]{:S(2)}) collective-permute-start(bf16[144,256]{1,0:T(8,128)(2,1)S(1)} %get-tuple-element.33), channel_id=1, source_target_pairs={{0,128},{32,160},{64,192},{96,224},{128,0},{160,32},{192,64},{224,... | collective-permute-start | bytes 221192 | tf_op jit(solution)/shard_map/ppermute | solution.py:452
  27.8 4.4 %collective-permute-start.10 = (bf16[144,256]{1,0:T(8,128)(2,1)S(1)}, bf16[144,256]{1,0:T(8,128)(2,1)S(1)}, u32[]{:S(2)}, u32[]{:S(2)}) collective-permute-start(bf16[144,256]{1,0:T(8,128)(2,1)S(1)} %get-tuple-element.34), channel_id=1, source_target_pairs={{0,64},{32,96},{64,128},{96,160},{128,192},{160,224},{192,0},{224,... | collective-permute-start | bytes 221192 | tf_op jit(solution)/shard_map/ppermute | solution.py:452
  32.4 9.4 %collective-permute-start.11 = (bf16[4,400,128]{2,1,0:T(8,128)(2,1)S(1)}, bf16[4,400,128]{2,1,0:T(8,128)(2,1)S(1)}, u32[]{:S(2)}, u32[]{:S(2)}) collective-permute-start(bf16[4,400,128]{2,1,0:T(8,128)(2,1)S(1)} %hold.5.refs_0_), channel_id=1, source_target_pairs={{0,32},{32,0},{64,96},{96,64},{128,160},{160,128},{192,224},{224,1... | collective-permute-start | bytes 1228808 | tf_op jit(solution)/shard_map/ppermute | solution.py:452
  35.9 6.6 %collective-permute-start.12 = (bf16[4,400,128]{2,1,0:T(8,128)(2,1)}, bf16[4,400,128]{2,1,0:T(8,128)(2,1)}, u32[]{:S(2)}, u32[]{:S(2)}) collective-permute-start(bf16[4,400,128]{2,1,0:T(8,128)(2,1)} %collective-permute-done.4.refs_1_), channel_id=1, source_target_pairs={{0,32},{32,0},{64,96},{96,64},{128,160},{160,128},{192,224},{224,1... | collective-permute-start | bytes 1228808 | tf_op jit(solution)/shard_map/ppermute | solution.py:452
  38.1 12.7 %collective-permute-start.6 = (bf16[4,400,128]{2,1,0:T(8,128)(2,1)}, bf16[4,400,128]{2,1,0:T(8,128)(2,1)S(1)}, u32[]{:S(2)}, u32[]{:S(2)}) collective-permute-start(bf16[4,400,128]{2,1,0:T(8,128)(2,1)} %collective-permute-done.4.refs_1_), channel_id=1, source_target_pairs={{0,1},{1,2},{2,3},{3,4},{4,5},{5,6},{6,7},{7,0},{8,9},{9,10},{10,1... | collective-permute-start | bytes 1228808 | tf_op jit(solution)/shard_map/ppermute | solution.py:449
  38.1 12.7 %collective-permute-start.7 = (bf16[4,400,128]{2,1,0:T(8,128)(2,1)}, bf16[4,400,128]{2,1,0:T(8,128)(2,1)S(1)}, u32[]{:S(2)}, u32[]{:S(2)}) collective-permute-start(bf16[4,400,128]{2,1,0:T(8,128)(2,1)} %collective-permute-done.5.refs_0_.refs_2_), channel_id=1, source_target_pairs={{0,7},{1,0},{2,1},{3,2},{4,3},{5,4},{6,5},{7,6},{8,15},{9,8},{10,9... | collective-permute-start | bytes 1228808 | tf_op jit(solution)/shard_map/ppermute | solution.py:449
  40.7 13.5 %collective-permute-start.15 = (bf16[4,400,128]{2,1,0:T(8,128)(2,1)}, bf16[4,400,128]{2,1,0:T(8,128)(2,1)S(1)}, u32[]{:S(2)}, u32[]{:S(2)}) collective-permute-start(bf16[4,400,128]{2,1,0:T(8,128)(2,1)} %collective-permute-done.5.refs_0_.refs_2_), channel_id=1, source_target_pairs={{0,32},{32,0},{64,96},{96,64},{128,160},{160,128},{192,224},{224,1... | collective-permute-start | bytes 1228808 | tf_op jit(solution)/shard_map/ppermute | solution.py:452
  50.8 11.4 %copy-start.7 = (bf16[4,400,128]{2,1,0:T(8,128)(2,1)}, bf16[4,400,128]{2,1,0:T(8,128)(2,1)S(1)}, u32[]{:S(2)}) copy-start(bf16[4,400,128]{2,1,0:T(8,128)(2,1)S(1)} %get-tuple-element.35.refs_1_.refs_3_) | copy-start | bytes 1228804
  50.8 11.4 %copy-start.9 = (bf16[4,400,128]{2,1,0:T(8,128)(2,1)}, bf16[4,400,128]{2,1,0:T(8,128)(2,1)S(1)}, u32[]{:S(2)}) copy-start(bf16[4,400,128]{2,1,0:T(8,128)(2,1)S(1)} %get-tuple-element.36.refs_2_.refs_4_) | copy-start | bytes 1228804
  50.8 3.4 %collective-permute-start.16 = (bf16[4,400,128]{2,1,0:T(8,128)(2,1)S(1)}, bf16[4,400,128]{2,1,0:T(8,128)(2,1)S(1)}, u32[]{:S(2)}, u32[]{:S(2)}) collective-permute-start(bf16[4,400,128]{2,1,0:T(8,128)(2,1)S(1)} %get-tuple-element.35.refs_1_.refs_3_), channel_id=1, source_target_pairs={{0,32},{32,0},{64,96},{96,64},{128,160},{160,128},{192,224},{224,1... | collective-permute-start | bytes 1228808 | tf_op jit(solution)/shard_map/ppermute | solution.py:452
  51.5 2.8 %collective-permute-start.17 = (bf16[4,400,128]{2,1,0:T(8,128)(2,1)S(1)}, bf16[4,400,128]{2,1,0:T(8,128)(2,1)S(1)}, u32[]{:S(2)}, u32[]{:S(2)}) collective-permute-start(bf16[4,400,128]{2,1,0:T(8,128)(2,1)S(1)} %get-tuple-element.36.refs_2_.refs_4_), channel_id=1, source_target_pairs={{0,32},{32,0},{64,96},{96,64},{128,160},{160,128},{192,224},{224,1... | collective-permute-start | bytes 1228808 | tf_op jit(solution)/shard_map/ppermute | solution.py:452
  51.6 11.8 %collective-permute-start.13 = (bf16[4,400,128]{2,1,0:T(8,128)(2,1)S(1)}, bf16[4,400,128]{2,1,0:T(8,128)(2,1)S(1)}, u32[]{:S(2)}, u32[]{:S(2)}) collective-permute-start(bf16[4,400,128]{2,1,0:T(8,128)(2,1)S(1)} %get-tuple-element.35.refs_1_.refs_3_), channel_id=1, source_target_pairs={{0,1},{1,2},{2,3},{3,4},{4,5},{5,6},{6,7},{7,0},{8,9},{9,10},{10,1... | collective-permute-start | bytes 1228808 | tf_op jit(solution)/shard_map/ppermute | solution.py:449
  51.6 11.8 %collective-permute-start.14 = (bf16[4,400,128]{2,1,0:T(8,128)(2,1)S(1)}, bf16[4,400,128]{2,1,0:T(8,128)(2,1)S(1)}, u32[]{:S(2)}, u32[]{:S(2)}) collective-permute-start(bf16[4,400,128]{2,1,0:T(8,128)(2,1)S(1)} %get-tuple-element.36.refs_2_.refs_4_), channel_id=1, source_target_pairs={{0,7},{1,0},{2,1},{3,2},{4,3},{5,4},{6,5},{7,6},{8,15},{9,8},{10,9... | collective-permute-start | bytes 1228808 | tf_op jit(solution)/shard_map/ppermute | solution.py:449
  63.4 10.9 %copy-start = (bf16[4,400,128]{2,1,0:T(8,128)(2,1)}, bf16[4,400,128]{2,1,0:T(8,128)(2,1)S(1)}, u32[]{:S(2)}) copy-start(bf16[4,400,128]{2,1,0:T(8,128)(2,1)S(1)} %get-tuple-element.38.refs_0_.refs_5_) | copy-start | bytes 1228804
  63.4 10.9 %copy-start.2 = (bf16[4,400,128]{2,1,0:T(8,128)(2,1)}, bf16[4,400,128]{2,1,0:T(8,128)(2,1)S(1)}, u32[]{:S(2)}) copy-start(bf16[4,400,128]{2,1,0:T(8,128)(2,1)S(1)} %get-tuple-element.39.refs_1_.refs_6_) | copy-start | bytes 1228804
  63.4 4.2 %collective-permute-start.20 = (bf16[4,400,128]{2,1,0:T(8,128)(2,1)S(1)}, bf16[4,400,128]{2,1,0:T(8,128)(2,1)S(1)}, u32[]{:S(2)}, u32[]{:S(2)}) collective-permute-start(bf16[4,400,128]{2,1,0:T(8,128)(2,1)S(1)} %get-tuple-element.38.refs_0_.refs_5_), channel_id=1, source_target_pairs={{0,32},{32,0},{64,96},{96,64},{128,160},{160,128},{192,224},{224,1... | collective-permute-start | bytes 1228808 | tf_op jit(solution)/shard_map/ppermute | solution.py:452
  64.7 2.9 %collective-permute-start.21 = (bf16[4,400,128]{2,1,0:T(8,128)(2,1)S(1)}, bf16[4,400,128]{2,1,0:T(8,128)(2,1)S(1)}, u32[]{:S(2)}, u32[]{:S(2)}) collective-permute-start(bf16[4,400,128]{2,1,0:T(8,128)(2,1)S(1)} %get-tuple-element.39.refs_1_.refs_6_), channel_id=1, source_target_pairs={{0,32},{32,0},{64,96},{96,64},{128,160},{160,128},{192,224},{224,1... | collective-permute-start | bytes 1228808 | tf_op jit(solution)/shard_map/ppermute | solution.py:452
  64.9 9.4 %collective-permute-start.18 = (bf16[2,400,128]{2,1,0:T(8,128)(2,1)S(1)}, bf16[2,400,128]{2,1,0:T(8,128)(2,1)}, u32[]{:S(2)}, u32[]{:S(2)}) collective-permute-start(bf16[2,400,128]{2,1,0:T(8,128)(2,1)S(1)} %slice.32), channel_id=1, source_target_pairs={{0,1},{1,2},{2,3},{3,4},{4,5},{5,6},{6,7},{7,0},{8,9},{9,10},{10,1... | collective-permute-start | bytes 614408 | tf_op jit(solution)/shard_map/ppermute | solution.py:449
  67.2 7.1 %collective-permute-start.19 = (bf16[2,400,128]{2,1,0:T(8,128)(2,1)S(1)}, bf16[2,400,128]{2,1,0:T(8,128)(2,1)}, u32[]{:S(2)}, u32[]{:S(2)}) collective-permute-start(bf16[2,400,128]{2,1,0:T(8,128)(2,1)S(1)} %slice.33), channel_id=1, source_target_pairs={{0,7},{1,0},{2,1},{3,2},{4,3},{5,4},{6,5},{7,6},{8,15},{9,8},{10,9... | collective-permute-start | bytes 614408 | tf_op jit(solution)/shard_map/ppermute | solution.py:449
  74.3 2.5 %collective-permute-start.22 = (bf16[2,400,128]{2,1,0:T(8,128)(2,1)}, bf16[2,400,128]{2,1,0:T(8,128)(2,1)}, u32[]{:S(2)}, u32[]{:S(2)}) collective-permute-start(bf16[2,400,128]{2,1,0:T(8,128)(2,1)} %get-tuple-element.41.refs_0_.refs_7_), channel_id=1, source_target_pairs={{0,32},{32,0},{64,96},{96,64},{128,160},{160,128},{192,224},{224,1... | collective-permute-start | bytes 614408 | tf_op jit(solution)/shard_map/ppermute | solution.py:452
  75.4 1.8 %collective-permute-start.23 = (bf16[2,400,128]{2,1,0:T(8,128)(2,1)}, bf16[2,400,128]{2,1,0:T(8,128)(2,1)}, u32[]{:S(2)}, u32[]{:S(2)}) collective-permute-start(bf16[2,400,128]{2,1,0:T(8,128)(2,1)} %get-tuple-element.42.refs_1_.refs_8_), channel_id=1, source_target_pairs={{0,32},{32,0},{64,96},{96,64},{128,160},{160,128},{192,224},{224,1... | collective-permute-start | bytes 614408 | tf_op jit(solution)/shard_map/ppermute | solution.py:452
  83.6 27.2 %collective-permute-start.24 = (bf16[64,48,128]{2,1,0:T(8,128)(2,1)}, bf16[64,48,128]{2,1,0:T(8,128)(2,1)}, u32[]{:S(2)}, u32[]{:S(2)}) collective-permute-start(bf16[64,48,128]{2,1,0:T(8,128)(2,1)} %get-tuple-element.46), channel_id=1, source_target_pairs={{0,192},{32,224},{64,0},{96,32},{128,64},{160,96},{192,128},{224,1... | collective-permute-start | bytes 2359304 | tf_op jit(solution)/shard_map/ppermute | solution.py:452
  84.2 26.6 %collective-permute-start.25 = (bf16[64,48,128]{2,1,0:T(8,128)(2,1)}, bf16[64,48,128]{2,1,0:T(8,128)(2,1)}, u32[]{:S(2)}, u32[]{:S(2)}) collective-permute-start(bf16[64,48,128]{2,1,0:T(8,128)(2,1)} %get-tuple-element.47), channel_id=1, source_target_pairs={{0,128},{32,160},{64,192},{96,224},{128,0},{160,32},{192,64},{224,... | collective-permute-start | bytes 2359304 | tf_op jit(solution)/shard_map/ppermute | solution.py:452
  85.8 36.6 %collective-permute-start.26 = (bf16[64,48,128]{2,1,0:T(8,128)(2,1)}, bf16[64,48,128]{2,1,0:T(8,128)(2,1)}, u32[]{:S(2)}, u32[]{:S(2)}) collective-permute-start(bf16[64,48,128]{2,1,0:T(8,128)(2,1)} %get-tuple-element.48), channel_id=1, source_target_pairs={{0,64},{32,96},{64,128},{96,160},{128,192},{160,224},{192,0},{224,... | collective-permute-start | bytes 2359304 | tf_op jit(solution)/shard_map/ppermute | solution.py:452
  122.4 11.7 %collective-permute-start.27 = (f32[8,128]{1,0:T(8,128)S(1)}, f32[8,128]{1,0:T(8,128)S(1)}, u32[]{:S(2)}, u32[]{:S(2)}) collective-permute-start(f32[8,128]{1,0:T(8,128)S(1)} %hold.9), channel_id=1, source_target_pairs={{0,0},{64,32},{128,64},{192,96},{32,128},{96,160},{160,192},{224,2... | collective-permute-start | bytes 12296 | tf_op jit(solution)/shard_map/ppermute | solution.py:529
  (16 other events, 91.2 us)
